TPU v7x, 256 devices: a whole 4x4x8 slice. The times are simulated.
256 devices in a mesh: dp: 16 (over y_hi, x, core), mp: 16 (over y_lo, z).
Axes of the slice: x: 4, y: 4 (y_hi: 2, y_lo: 2; y = y_hi * 2 + y_lo), z: 8, core: 2. Of those that a mesh axis runs over, the one named last changes fastest.
Arguments:
- series: bfloat16 [16, 2048, 16, 256], P('dp', 'mp'), may hold values from -6 to 6
- upstream_grad: bfloat16 [16, 2048, 16, 256], P('dp', None, 'mp'), may hold values from -3 to 3
- time_weights: bfloat16 [4, 256, 256], replicated, may hold values from -0.375 to 0.375
- channel_weights: bfloat16 [4, 256, 256], replicated, may hold values from -0.375 to 0.375
- neighbors: int32 [16, 3], replicated, may hold values from 0 to 15, as said below
Outputs:
- mixed_series: bfloat16 [16, 2048, 16, 256], P('dp', None, 'mp')
- series_grad: bfloat16 [16, 2048, 16, 256], P('dp', 'mp')
- time_grads: float32 [4, 256, 256], P(None, 'mp')
- channel_grads: float32 [4, 256, 256], P(None, 'mp')
Inputs may be any that keep to these rules, and one draw needn't show every extreme that they name: `neighbors`: row b names 3 different blocks; its first entry is b.
All inputs are finite; a program needn't handle non-finite values.
Results may differ from a plain program's by a relative error of at most 0.025.
Values may be sent and summed in bfloat16 or wider, within the bound.
No kernel may reach another device: no remote copies, remote signals or barrier semaphores. Data moves between devices by JAX's collectives and lax.ppermute only.
A program may use at most 192 MiB of HBM per device.

v0:
```python
import jax
import jax.numpy as jnp
from jax import lax
from jax.sharding import PartitionSpec as P

HEADS = 4


EPS = 1e-06
LOGIT_SCALE = 0.25


def row_norm(inputs):
    return inputs * lax.rsqrt(jnp.mean(inputs * inputs, axis=-1, keepdims=True) + EPS)


def head_norm(inputs):
    shaped = inputs.reshape(inputs.shape[:-1] + (HEADS, inputs.shape[-1] // HEADS))
    return row_norm(shaped).reshape(inputs.shape)


def project(normed, weights):
    raw_query = jnp.dot(normed, weights[0], preferred_element_type=jnp.float32)
    raw_key = jnp.dot(normed, weights[1], preferred_element_type=jnp.float32)
    value_rows = jnp.dot(normed, weights[2], preferred_element_type=jnp.float32).astype(
        jnp.bfloat16
    )
    query_rows = head_norm(raw_query).astype(jnp.bfloat16)
    key_rows = head_norm(raw_key).astype(jnp.bfloat16)
    return (raw_query, raw_key, query_rows, key_rows, value_rows)


def project_back(normed, raw_query, raw_key, query_grad, key_grad, value_grad, weights):
    query_back = jax.vjp(head_norm, raw_query)[1](query_grad)[0].astype(jnp.bfloat16)
    key_back = jax.vjp(head_norm, raw_key)[1](key_grad)[0].astype(jnp.bfloat16)
    value_back = value_grad.astype(jnp.bfloat16)
    weight_grads = [
        jnp.dot(normed.T, back_rows, preferred_element_type=jnp.float32)
        for back_rows in (query_back, key_back, value_back)
    ]
    normed_grad = jnp.dot(query_back, weights[0].T, preferred_element_type=jnp.float32)
    normed_grad = normed_grad + jnp.dot(key_back, weights[1].T, preferred_element_type=jnp.float32)
    normed_grad = normed_grad + jnp.dot(
        value_back, weights[2].T, preferred_element_type=jnp.float32
    )
    return (normed_grad, weight_grads)


def attend_time(query_heads, key_heads, value_heads):
    attention_logits = LOGIT_SCALE * jnp.einsum(
        "clhe,cmhe->hlmc", query_heads, key_heads, preferred_element_type=jnp.float32
    )
    exponent = jnp.exp(attention_logits)
    attention_layer = exponent / jnp.sum(exponent, axis=2, keepdims=True)
    mixed_heads = jnp.einsum(
        "hlmc,cmhe->clhe",
        attention_layer.astype(jnp.bfloat16),
        value_heads,
        preferred_element_type=jnp.float32,
    )
    return (mixed_heads.astype(jnp.bfloat16), attention_layer)


def revert_time(query_heads, key_heads, value_heads, attention_layer, grad_heads):
    weights_brain_float = attention_layer.astype(jnp.bfloat16)
    attention_gradient = jnp.einsum(
        "clhe,cmhe->hlmc", grad_heads, value_heads, preferred_element_type=jnp.float32
    )
    row_delta = jnp.sum(attention_layer * attention_gradient, axis=2, keepdims=True)
    logit_gradient = (LOGIT_SCALE * attention_layer * (attention_gradient - row_delta)).astype(
        jnp.bfloat16
    )
    query_grad = jnp.einsum(
        "hlmc,cmhe->clhe", logit_gradient, key_heads, preferred_element_type=jnp.float32
    )
    key_grad = jnp.einsum(
        "hlmc,clhe->cmhe", logit_gradient, query_heads, preferred_element_type=jnp.float32
    )
    value_grad = jnp.einsum(
        "hlmc,clhe->cmhe", weights_brain_float, grad_heads, preferred_element_type=jnp.float32
    )
    return (query_grad, key_grad, value_grad)


def forward_time(series_rows, weights):
    channel_count, length, features = series_rows.shape
    total_rows = channel_count * length
    normed = (
        row_norm(series_rows.astype(jnp.float32)).astype(jnp.bfloat16).reshape(total_rows, features)
    )
    raw_query, raw_key, query_rows, key_rows, value_rows = project(normed, weights)
    shaped = (channel_count, length, HEADS, features // HEADS)
    mixed_heads, attention_layer = attend_time(
        query_rows.reshape(shaped), key_rows.reshape(shaped), value_rows.reshape(shaped)
    )
    mixed_flat = mixed_heads.reshape(total_rows, features)
    branch = jnp.dot(mixed_flat, weights[3], preferred_element_type=jnp.float32).reshape(
        series_rows.shape
    )
    stream = (series_rows.astype(jnp.float32) + branch).astype(jnp.bfloat16)
    return (
        stream,
        (normed, raw_query, raw_key, query_rows, key_rows, value_rows, mixed_flat, attention_layer),
    )


def backward_time(series_rows, stored, stream_grad, weights):
    normed, raw_query, raw_key, query_rows, key_rows, value_rows, mixed_flat, attention_layer = (
        stored
    )
    channel_count, length, features = series_rows.shape
    total_rows = channel_count * length
    shaped = (channel_count, length, HEADS, features // HEADS)
    grad_flat = stream_grad.reshape(total_rows, features)
    out_grad = jnp.dot(mixed_flat.T, grad_flat, preferred_element_type=jnp.float32)
    mixed_grad = jnp.dot(grad_flat, weights[3].T, preferred_element_type=jnp.float32).astype(
        jnp.bfloat16
    )
    query_grad, key_grad, value_grad = revert_time(
        query_rows.reshape(shaped),
        key_rows.reshape(shaped),
        value_rows.reshape(shaped),
        attention_layer,
        mixed_grad.reshape(shaped),
    )
    normed_grad, weight_grads = project_back(
        normed,
        raw_query,
        raw_key,
        query_grad.reshape(total_rows, features),
        key_grad.reshape(total_rows, features),
        value_grad.reshape(total_rows, features),
        weights,
    )
    norm_back = jax.vjp(row_norm, series_rows.astype(jnp.float32))[1]
    series_grad = (
        stream_grad.astype(jnp.float32) + norm_back(normed_grad.reshape(series_rows.shape))[0]
    ).astype(jnp.bfloat16)
    return (series_grad, jnp.stack(weight_grads + [out_grad]))


def near_blocks(source_rows, neighbors):
    block_list = neighbors.shape[0]
    features = source_rows.shape[1]
    shaped = source_rows.reshape(block_list, source_rows.shape[0] // block_list, features)
    return shaped[neighbors].reshape(block_list, -1, HEADS, features // HEADS)


def split_blocks(rows, block_list):
    features = rows.shape[1]
    return rows.reshape(block_list, -1, HEADS, features // HEADS)


def channel_logits(query_blocks, key_near):
    return LOGIT_SCALE * jnp.einsum(
        "bqhe,bkhe->bhqk", query_blocks, key_near, preferred_element_type=jnp.float32
    )


def attend_channels(query_rows, key_rows, value_rows, neighbors):
    block_list = neighbors.shape[0]
    query_blocks = split_blocks(query_rows, block_list)
    key_near = near_blocks(key_rows, neighbors)
    value_near = near_blocks(value_rows, neighbors)
    exponent = jnp.exp(channel_logits(query_blocks, key_near))
    totals = jnp.sum(exponent, axis=3, keepdims=True)
    weights_brain_float = (exponent / totals).astype(jnp.bfloat16)
    mixed = jnp.einsum(
        "bhqk,bkhe->bqhe", weights_brain_float, value_near, preferred_element_type=jnp.float32
    )
    return (mixed.reshape(query_rows.shape).astype(jnp.bfloat16), totals)


def revert_channels(query_rows, key_rows, value_rows, neighbors, mixed_grad, totals):
    block_list, neighbor_count = neighbors.shape
    features = query_rows.shape[1]
    block_length = query_rows.shape[0] // block_list
    onehot = (
        neighbors.reshape(-1)[:, None] == jnp.arange(block_list, dtype=jnp.int32)[None, :]
    ).astype(jnp.float32)
    query_blocks = split_blocks(query_rows, block_list)
    grad_blocks = split_blocks(mixed_grad, block_list)
    key_near = near_blocks(key_rows, neighbors)
    value_near = near_blocks(value_rows, neighbors)
    attention_layer = jnp.exp(channel_logits(query_blocks, key_near)) / totals
    attention_gradient = jnp.einsum(
        "bqhe,bkhe->bhqk", grad_blocks, value_near, preferred_element_type=jnp.float32
    )
    row_delta = jnp.sum(attention_layer * attention_gradient, axis=3, keepdims=True)
    logit_gradient = (LOGIT_SCALE * attention_layer * (attention_gradient - row_delta)).astype(
        jnp.bfloat16
    )
    weights_brain_float = attention_layer.astype(jnp.bfloat16)
    query_grad = jnp.einsum(
        "bhqk,bkhe->bqhe", logit_gradient, key_near, preferred_element_type=jnp.float32
    ).reshape(query_rows.shape)
    near_key_grad = jnp.einsum(
        "bhqk,bqhe->bkhe", logit_gradient, query_blocks, preferred_element_type=jnp.float32
    ).reshape(block_list * neighbor_count, block_length, features)
    near_value_grad = jnp.einsum(
        "bhqk,bqhe->bkhe", weights_brain_float, grad_blocks, preferred_element_type=jnp.float32
    ).reshape(block_list * neighbor_count, block_length, features)
    key_grad = jnp.einsum(
        "ob,otd->btd", onehot, near_key_grad, precision=lax.Precision.HIGHEST
    ).reshape(query_rows.shape)
    value_grad = jnp.einsum(
        "ob,otd->btd", onehot, near_value_grad, precision=lax.Precision.HIGHEST
    ).reshape(query_rows.shape)
    return (query_grad, key_grad, value_grad)


def forward_channels(stream_rows, weights, neighbors):
    stream_float = stream_rows.astype(jnp.float32)
    normed = row_norm(stream_float).astype(jnp.bfloat16)
    raw_query, raw_key, query_rows, key_rows, value_rows = project(normed, weights)
    mixed_rows, totals = attend_channels(query_rows, key_rows, value_rows, neighbors)
    output_rows = (
        stream_float + jnp.dot(mixed_rows, weights[3], preferred_element_type=jnp.float32)
    ).astype(jnp.bfloat16)
    return (output_rows, normed, raw_query, raw_key, value_rows, mixed_rows, totals)


def backward_channels(
    stream_rows,
    normed,
    raw_query,
    raw_key,
    value_rows,
    mixed_rows,
    totals,
    upstream_rows,
    weights,
    neighbors,
):
    out_grad = jnp.dot(mixed_rows.T, upstream_rows, preferred_element_type=jnp.float32)
    mixed_grad = jnp.dot(upstream_rows, weights[3].T, preferred_element_type=jnp.float32).astype(
        jnp.bfloat16
    )
    query_rows = head_norm(raw_query).astype(jnp.bfloat16)
    key_rows = head_norm(raw_key).astype(jnp.bfloat16)
    query_grad, key_grad, value_grad = revert_channels(
        query_rows, key_rows, value_rows, neighbors, mixed_grad, totals
    )
    normed_grad, weight_grads = project_back(
        normed, raw_query, raw_key, query_grad, key_grad, value_grad, weights
    )
    norm_back = jax.vjp(row_norm, stream_rows.astype(jnp.float32))[1]
    stream_grad = (upstream_rows.astype(jnp.float32) + norm_back(normed_grad)[0]).astype(
        jnp.bfloat16
    )
    return (stream_grad, jnp.stack(weight_grads + [out_grad]))


def reduce_grads(partial_sum):
    whole_sum = lax.psum(partial_sum.astype(jnp.bfloat16), "dp")
    return lax.psum_scatter(whole_sum, "mp", scatter_dimension=1, tiled=True).astype(jnp.float32)


def shards(series, upstream_grad, time_weights, channel_weights, neighbors):
    model_size = lax.axis_size("mp")
    data_size = lax.axis_size("dp")
    series_rows = series[0]
    channel_count, length, features = series_rows.shape
    seg_count = length // model_size
    stream, stored = forward_time(series_rows, time_weights)
    columns = lax.all_to_all(
        stream.reshape(channel_count, model_size, seg_count, features),
        "mp",
        split_axis=1,
        concat_axis=0,
        tiled=True,
    )[:, 0]

    def one_segment(stream_seg):
        return forward_channels(stream_seg, channel_weights, neighbors) + (stream_seg,)

    results = jax.vmap(one_segment, in_axes=1, out_axes=1)(columns)
    output_rows, seg_normed, seg_query, seg_key, seg_values, seg_mixed, seg_totals, seg_stream = (
        results
    )

    def one_back(
        stream_seg, normed, raw_query, raw_key, value_rows, mixed_rows, totals, upstream_seg
    ):
        return backward_channels(
            stream_seg,
            normed,
            raw_query,
            raw_key,
            value_rows,
            mixed_rows,
            totals,
            upstream_seg,
            channel_weights,
            neighbors,
        )

    stream_grad, channel_parts = jax.vmap(one_back, in_axes=1, out_axes=(1, 0))(
        seg_stream,
        seg_normed,
        seg_query,
        seg_key,
        seg_values,
        seg_mixed,
        seg_totals,
        upstream_grad[0],
    )
    returned = lax.all_to_all(
        stream_grad.reshape(model_size, channel_count, seg_count, features),
        "mp",
        split_axis=0,
        concat_axis=2,
        tiled=True,
    )
    channel_grads = reduce_grads(jnp.sum(channel_parts, axis=0)) / data_size
    series_grad, time_part = backward_time(
        series_rows, stored, returned.reshape(channel_count, length, features), time_weights
    )
    time_grads = reduce_grads(time_part) / data_size
    return (output_rows[None], series_grad[None], time_grads, channel_grads)


def solution(mesh):
    placed = (P("dp", "mp", None, None), P("dp", None, "mp", None), P(), P(), P())
    return jax.shard_map(
        shards,
        mesh=mesh,
        in_specs=placed,
        out_specs=(
            P("dp", None, "mp", None),
            P("dp", "mp", None, None),
            P(None, "mp", None),
            P(None, "mp", None),
        ),
        check_vma=False,
    )
```

profile of v0, /device:TPU:7, one launch (start us, length us, event | category | flops | bytes accessed | tf_op | source)
XLA Modules:
  0.0 580.1 jit_solution(12377547107588961812)
XLA Ops:
  21.9 2.9 copy.218
  24.7 4.8 fusion.120
  29.5 3.9 copy.221
  36.4 3.8 copy.271
  40.2 3.8 convert_bitcast_fusion.1
  44.0 3.2 copy.224
  47.2 2.7 fusion.48
  49.9 9.5 %all-to-all-start = ((bf16[128,16,1,256]{3,0,2,1:T(8,128)(2,1)}), bf16[128,16,1,256]{3,0,2,1:T(8,128)(2,1)S(1)}, u32[]{:S(2)}, u32[]{:S(2)}) async-start(bf16[128,16,1,256]{3,0,2,1:T(8,128)(2,1)} %fusion.48), calls=%async_computation | async-start | bytes 2097152 | tf_op jit(solution)/shard_map/all_to_all | solution.py:266
  59.4 4.1 copy.276
  67.4 3.9 copy.237
  71.7 2.5 copy.274
  74.2 4.3 reshape.704
  78.5 6.4 %all-to-all-done = bf16[128,16,1,256]{3,0,2,1:T(8,128)(2,1)S(1)} async-done(((bf16[128,16,1,256]{3,0,2,1:T(8,128)(2,1)}), bf16[128,16,1,256]{3,0,2,1:T(8,128)(2,1)S(1)}, u32[]{:S(2)}, u32[]{:S(2)}) %all-to-all-start) | async-done | bytes 1048608 | tf_op jit(solution)/shard_map/all_to_all | solution.py:266
  92.6 2.9 copy.229
  98.9 2.9 copy.230
  101.8 3.4 multiply_convert_fusion.1
  105.2 3.8 gather_fusion.1
  109.0 3.8 gather_fusion
  112.8 10.2 %reshape.745 = bf16[16,384,4,64]{3,2,1,0:T(4,128)(2,1)} reshape(bf16[48,128,256]{2,1,0:T(8,128)(2,1)} %gather_fusion) | data formatting | bytes 6291456 | tf_op jit(solution)/shard_map/reshape.16
  123.0 9.7 %copy.234 = bf16[16,384,4,64]{1,3,2,0:T(8,128)(2,1)} copy(bf16[16,384,4,64]{3,2,1,0:T(4,128)(2,1)} %reshape.745) | data formatting | bytes 6291456 | tf_op jit(solution)/shard_map/reshape.16
  132.7 10.4 %reshape.746 = bf16[16,384,4,64]{3,2,1,0:T(4,128)(2,1)} reshape(bf16[48,128,256]{2,1,0:T(8,128)(2,1)} %gather_fusion.1) | data formatting | bytes 6291456 | tf_op jit(solution)/shard_map/reshape.13
  143.1 9.6 %copy.233 = bf16[16,384,4,64]{1,3,2,0:T(8,128)(2,1)} copy(bf16[16,384,4,64]{3,2,1,0:T(4,128)(2,1)} %reshape.746) | data formatting | bytes 6291456 | tf_op jit(solution)/shard_map/reshape.13
  152.6 5.2 fusion.2
  157.9 5.1 fusion.7
  162.9 6.5 %multiply_reduce_fusion = (f32[16,4,128]{2,1,0:T(4,128)S(1)}, f32[16,4,128,384]{3,2,1,0:T(8,128)}) fusion(f32[16,4,128]{2,1,0:T(4,128)S(1)} %get-tuple-element.34, f32[16,4,128,384]{3,2,1,0:T(8,128)S(1)} %get-tuple-element.35, bf16[16,128,4,64]{1,3,2,0:T(8,128)(2,1)S(1)} %copy-done.54, bf16[16,384,4,64]{1,3,2,0:T(8,128)(2,1)S(1)} %copy-done.50), kind=kOutput, calls=%fused_computation.4 | convolution fusion | flops 415227904 | bytes 29425664 | tf_op jit(solution)/shard_map/vmap(bqhe,bkhe->bhqk)/dot_general | solution.py:186
  169.5 7.4 %multiply_convert_fusion = bf16[16,4,128,384]{3,2,1,0:T(8,128)(2,1)S(1)} fusion(f32[16,4,128,384]{3,2,1,0:T(8,128)} %get-tuple-element.37, f32[16,4,128]{2,1,0:T(4,128)S(1)} %get-tuple-element.36, f32[16,4,128]{2,1,0:T(4,128)S(1)} %get-tuple-element.34, f32[16,4,128,384]{3,2,1,0:T(8,128)S(1)} %get-tuple-element.35), kind=kLoop, calls=%fused_computation.3 | loop fusion | flops 18874368 | bytes 31522816 | tf_op jit(solution)/shard_map/vmap()/convert_element_type | solution.py:190
  176.9 4.3 convolution_bitcast_fusion.3
  182.4 6.3 %copy.245 = f32[1,16,384,4,64]{2,1,4,3,0:T(8,128)} copy(f32[1,16,384,4,64]{2,4,3,1,0:T(8,128)S(1)} %convolution_bitcast_fusion) | data formatting | bytes 12582912 | tf_op jit(solution)/shard_map/vmap(bhqk,bqhe->bkhe)/transpose | solution.py:197
  188.7 6.9 %reshape.700 = f32[48,128,256]{1,0,2:T(8,128)} reshape(f32[1,16,384,4,64]{2,1,4,3,0:T(8,128)} %copy.245) | data formatting | bytes 12582912 | tf_op jit(solution)/shard_map/reshape.40
  195.6 6.7 %copy.246 = f32[48,128,256]{2,0,1:T(8,128)} copy(f32[48,128,256]{1,0,2:T(8,128)} %reshape.700) | data formatting | bytes 12582912 | tf_op jit(solution)/shard_map/reshape.40
  202.3 6.3 %fusion.112 = f32[16,128,256]{2,0,1:T(8,128)} fusion(f32[48,128,256]{2,0,1:T(8,128)} %copy.246, s32[48]{0:T(128)S(1)} %eq.15), kind=kOutput, calls=%fused_computation.187 | convolution fusion | flops 301990656 | bytes 8388800 | tf_op jit(solution)/shard_map/vmap(ob,otd->btd)/dot_general | solution.py:203
  208.6 3.5 copy.249
  212.1 4.3 copy.247
  216.4 2.6 copy.241
  219.0 2.5 copy.240
  221.5 9.1 %copy.252 = f32[1,16,384,4,64]{2,1,4,3,0:T(8,128)} copy(f32[1,16,384,4,64]{2,4,3,1,0:T(8,128)} %fusion.7) | data formatting | bytes 12582912 | tf_op jit(solution)/shard_map/vmap(bhqk,bqhe->bkhe)/transpose | solution.py:200
  230.6 6.9 %reshape.701 = f32[48,128,256]{1,0,2:T(8,128)} reshape(f32[1,16,384,4,64]{2,1,4,3,0:T(8,128)} %copy.252) | data formatting | bytes 12582912 | tf_op jit(solution)/shard_map/reshape.52
  237.5 6.7 %copy.253 = f32[48,128,256]{2,0,1:T(8,128)} copy(f32[48,128,256]{1,0,2:T(8,128)} %reshape.701) | data formatting | bytes 12582912 | tf_op jit(solution)/shard_map/reshape.52
  244.2 5.0 convolution_convert_fusion.4
  250.5 2.8 transpose.115
  253.3 2.6 multiply_reduce_fusion.3
  257.5 3.1 copy.250
  260.6 5.2 fusion.37
  275.6 6.2 %all-to-all-start.1 = ((bf16[16,128,1,256]{3,1,2,0:T(8,128)(2,1)}), bf16[16,128,1,256]{3,1,2,0:T(8,128)(2,1)S(1)}, u32[]{:S(2)}, u32[]{:S(2)}) async-start(bf16[16,128,1,256]{3,1,2,0:T(8,128)(2,1)} %bitcast.329), calls=%async_computation.1 | async-start | bytes 2097152 | tf_op jit(solution)/shard_map/all_to_all | solution.py:308
  281.8 7.1 %fusion.45 = bf16[1,16,128,4,64]{2,4,3,1,0:T(8,128)(2,1)S(1)} fusion(bf16[16,384,4,64]{1,3,2,0:T(8,128)(2,1)} %copy.234, f32[16,4,128,384]{3,2,1,0:T(8,128)} %copy-done.2, f32[16,4,128]{2,1,0:T(4,128)S(1)} %get-tuple-element.34), kind=kOutput, calls=%fused_computation.90 | convolution fusion | flops 412614656 | bytes 16809984 | tf_op jit(solution)/shard_map/vmap(bhqk,bkhe->bqhe)/dot_general | solution.py:168
  294.1 2.7 fusion.11
  296.8 10.4 %all-to-all-done.1 = bf16[16,128,1,256]{3,1,2,0:T(8,128)(2,1)S(1)} async-done(((bf16[16,128,1,256]{3,1,2,0:T(8,128)(2,1)}), bf16[16,128,1,256]{3,1,2,0:T(8,128)(2,1)S(1)}, u32[]{:S(2)}, u32[]{:S(2)}) %all-to-all-start.1) | async-done | bytes 1048608 | tf_op jit(solution)/shard_map/all_to_all | solution.py:308
  308.9 2.3 convolution_convert_fusion
  311.2 4.6 reshape.702
  315.8 4.8 fusion.30
  320.6 3.2 copy.259
  324.1 3.8 copy.266
  327.9 4.5 convolution_bitcast_fusion.2
  333.6 2.4 copy.267
  336.1 3.8 copy.268
  339.9 4.6 copy.262
  344.5 4.1 copy.263
  348.6 2.1 multiply_reduce_fusion.2
  358.1 2.6 copy.272
  360.7 4.4 convert_element_type.360
  365.1 1.9 fusion.53
  375.2 52.5 %reduce-scatter.3.cloned.1.call-done = bf16[4,16,256]{2,1,0:T(8,128)(2,1)} async-done(((bf16[4,256,256]{2,1,0:T(8,128)(2,1)}), bf16[4,16,256]{2,1,0:T(8,128)(2,1)}) %reduce-scatter.3.cloned.1.call-update) | async-done | bytes 32784 | tf_op jit(solution)/shard_map/reduce_scatter | solution.py:256
  427.7 2.9 fusion.19
  432.2 139.7 %all-reduce.3.cloned.1.call-done = (bf16[4,16,256]{2,1,0:T(8,128)(2,1)}, bf16[4,16,256]{2,1,0:T(8,128)(2,1)}) async-done(((bf16[4,16,256]{2,1,0:T(8,128)(2,1)}, bf16[4,16,256]{2,1,0:T(8,128)(2,1)}), (bf16[4,16,256]{2,1,0:T(8,128)(2,1)}, bf16[4,16,256]{2,1,0:T(8,128)(2,1)})) %all-reduce.3.cloned.1.call-update) | async-done | bytes 65552 | tf_op jit(solution)/shard_map/psum | solution.py:255
  (227 shorter events, 73.2 us)
Async XLA Ops:
  7.2 3.5 copy-start.9
  11.7 7.2 %copy-start = (bf16[1,128,16,256]{3,2,1,0:T(8,128)(2,1)}, bf16[1,128,16,256]{3,2,1,0:T(8,128)(2,1)S(1)}, u32[]{:S(2)}) copy-start(bf16[1,128,16,256]{3,2,1,0:T(8,128)(2,1)S(1)} %copy.216) | copy-start | bytes 3145732
  15.5 1.3 copy-start.3
  19.3 1.3 copy-start.5
  19.4 1.3 copy-start.57
  19.4 1.3 copy-start.61
  21.8 2.9 copy-start.23
  33.3 6.9 %copy-start.13 = (bf16[128,16,4,64]{3,2,1,0:T(4,128)(2,1)S(1)}, bf16[128,16,4,64]{3,2,1,0:T(4,128)(2,1)}, u32[]{:S(2)}) copy-start(bf16[128,16,4,64]{3,2,1,0:T(4,128)(2,1)} %reshape.688) | copy-start | bytes 3145732
  49.9 35.0 %all-to-all-start = ((bf16[128,16,1,256]{3,0,2,1:T(8,128)(2,1)}), bf16[128,16,1,256]{3,0,2,1:T(8,128)(2,1)S(1)}, u32[]{:S(2)}, u32[]{:S(2)}) async-start(bf16[128,16,1,256]{3,0,2,1:T(8,128)(2,1)} %fusion.48), calls=%async_computation | async-start | bytes 2097152 | tf_op jit(solution)/shard_map/all_to_all | solution.py:266
  59.4 4.1 copy-start.69
  85.9 2.8 copy-start.17
  85.9 1.4 copy-start.52
  152.6 5.2 copy-start.54
  157.8 11.7 %copy-start.2 = (f32[16,4,128,384]{3,2,1,0:T(8,128)}, f32[16,4,128,384]{3,2,1,0:T(8,128)S(1)}, u32[]{:S(2)}) copy-start(f32[16,4,128,384]{3,2,1,0:T(8,128)S(1)} %get-tuple-element.35) | copy-start | bytes 37748740
  157.8 5.1 copy-start.50
  169.5 7.4 %copy-start.8 = (bf16[16,384,4,64]{1,3,2,0:T(8,128)(2,1)S(1)}, bf16[16,384,4,64]{1,3,2,0:T(8,128)(2,1)}, u32[]{:S(2)}) copy-start(bf16[16,384,4,64]{1,3,2,0:T(8,128)(2,1)} %copy.233) | copy-start | bytes 9437188
  176.9 4.3 copy-start.27
  212.1 4.3 copy-start.22
  260.6 5.3 copy-start.43
  260.6 7.6 %copy-start.53 = (bf16[4,256,256]{2,1,0:T(8,128)(2,1)S(1)}, bf16[4,256,256]{2,1,0:T(8,128)(2,1)}, u32[]{:S(2)}) copy-start(bf16[4,256,256]{2,1,0:T(8,128)(2,1)} %param.8) | copy-start | bytes 1572868
  265.9 2.8 copy-start.21
  265.9 2.8 copy-start.42
  266.0 3.2 copy-start.44
  268.3 1.7 copy-start.7
  270.7 1.6 copy-start.12
  270.7 1.9 copy-start.28
  272.6 1.2 copy-start.47
  275.6 31.7 %all-to-all-start.1 = ((bf16[16,128,1,256]{3,1,2,0:T(8,128)(2,1)}), bf16[16,128,1,256]{3,1,2,0:T(8,128)(2,1)S(1)}, u32[]{:S(2)}, u32[]{:S(2)}) async-start(bf16[16,128,1,256]{3,1,2,0:T(8,128)(2,1)} %bitcast.329), calls=%async_computation.1 | async-start | bytes 2097152 | tf_op jit(solution)/shard_map/all_to_all | solution.py:308
  281.8 93.4 %reduce-scatter.5.cloned.1.call-start = ((), (), s32[]{:S(2)}) async-start(), calls=%async_computation.5 | async-start | bytes 557056 | tf_op jit(solution)/shard_map/reduce_scatter | solution.py:256
  289.0 1.2 copy-start.34
  289.0 1.5 copy-start.39
  289.7 2.5 copy-start.49
  290.5 1.2 copy-start.36
  291.0 1.3 copy-start.48
  292.3 1.8 copy-start.18
  293.6 134.1 %reduce-scatter.3.cloned.1.call-start = ((), (), s32[]{:S(2)}) async-start(), calls=%async_computation.4 | async-start | bytes 557056 | tf_op jit(solution)/shard_map/reduce_scatter | solution.py:256
  311.2 4.6 copy-start.14
  320.6 3.2 copy-start.45
  320.6 3.3 copy-start.64
  324.1 3.8 copy-start.25
  327.9 4.5 copy-start.24
  327.9 4.5 copy-start.26
  344.5 4.1 copy-start.4
  348.6 2.2 copy-start.56
  348.6 2.2 copy-start.20
  348.6 2.2 copy-start.60
  350.9 2.0 copy-start.6
  350.9 2.6 copy-start.19
  354.3 1.9 copy-start.15
  354.3 2.6 copy-start.16
  360.7 4.4 copy-start.1
  365.1 1.9 copy-start.31
  365.1 2.4 copy-start.30
  365.1 2.4 copy-start.46
  367.0 1.3 copy-start.37
  368.3 1.4 copy-start.32
  369.7 1.6 copy-start.40
  369.7 202.2 %all-reduce.3.cloned.1.call-start = ((), (), s32[]{:S(2)}) async-start(), calls=%async_computation.6 | async-start | bytes 131072 | tf_op jit(solution)/shard_map/psum | solution.py:255
  369.7 1.5 copy-start.51
  371.3 1.2 copy-start.38
  371.3 1.9 copy-start.41
  373.2 2.0 copy-start.68
  373.2 54.5 %copy-start.10 = (bf16[1,128,16,256]{3,2,1,0:T(8,128)(2,1)S(1)}, bf16[1,128,16,256]{3,2,1,0:T(8,128)(2,1)}, u32[]{:S(2)}) copy-start(bf16[1,128,16,256]{3,2,1,0:T(8,128)(2,1)} %param.5) | copy-start | bytes 3145732
  373.2 54.5 %copy-start.66 = (f32[128,16]{0,1:T(8,128)S(1)}, f32[128,16]{0,1:T(8,128)}, u32[]{:S(2)}) copy-start(f32[128,16]{0,1:T(8,128)} %copy-done.65) | copy-start | bytes 24580
  (11 other events, 9.3 us)
Sparse Core Ops, SparseCore 0:
  293.8 59.6 reduce-scatter.4
  369.8 57.8 reduce-scatter.2
  430.4 141.4 all-reduce.2
where the time goes:
time: 591 us; the launch traced here: 580 us
  local copies, waits for them, and re-layouts  209 us (35%)
  waiting for transfers between devices  209 us (35%)
  matrix products  87.1 us (15%)
  other arithmetic  43.8 us (7%)
  starting transfers between devices  16.2 us (3%)
  between operations  14.9 us (3%)
    psum x1, waiting for transfers between devices, reduce_grads(): whole_sum = lax.psum(partial_sum.astype(jnp.bfloat16), 'dp')  140 us
    another operation x10, local copies, waits for them, and re-layouts  72.8 us
    reduce_scatter x2, waiting for transfers between devices, reduce_grads(): lax.psum_scatter(whole_sum, 'mp', scatter_dimension=1, tiled=True)  52.5 us
    unnamed x143, local copies, waits for them, and re-layouts  19 us
  transfers between devices with their start and end apart: 5, of which 4 were waited for; matrix products, arithmetic and copies ran while one was open for 17% of the time, Pallas kernels for 0%

commit v1 on v0

v1 whole, which is shorter than its diff:
```python
import jax
import jax.numpy as jnp
from jax import lax
from jax.experimental import pallas as pl
from jax.experimental.pallas import tpu as pltpu
from jax.sharding import PartitionSpec as P

HEADS = 4
D = 256
HD = D // HEADS
L = 16
CH = 128
BLK = 128
NBR = 3
ROWS = 2048
STEP = 256
STEPS = ROWS // STEP
EPS = 1e-06
LOG2E = 1.4426950408889634
LN2 = 0.6931471805599453
QSCALE = 0.25 * LOG2E
F32 = jnp.float32
BF16 = jnp.bfloat16


def dot(a, b):
    return lax.dot_general(a, b, (((1,), (0,)), ((), ())), preferred_element_type=F32)


def dot_rt(a, b):
    return lax.dot_general(a, b, (((1,), (1,)), ((), ())), preferred_element_type=F32)


def dot_lt(a, b):
    return lax.dot_general(a, b, (((0,), (0,)), ((), ())), preferred_element_type=F32)


def iota(shape, dim):
    return lax.broadcasted_iota(jnp.int32, shape, dim)


def div(a, n):
    return lax.shift_right_logical(a, jnp.int32(n.bit_length() - 1))


def head_mean_matrix():
    same = div(iota((D, D), 0), HD) == div(iota((D, D), 1), HD)
    return jnp.where(same, 1.0 / HD, 0.0).astype(BF16)


def swap_matrix():
    row, col = iota((D, D), 0), iota((D, D), 1)
    same = (div(row, L) == (col & (L - 1))) & ((row & (L - 1)) == div(col, L))
    return jnp.where(same, 1.0, 0.0).astype(BF16)


def rms_scale(x):
    return lax.rsqrt(jnp.mean(x * x, axis=-1, keepdims=True) + EPS)


def head_scale(raw, means):
    return lax.rsqrt(dot((raw * raw).astype(BF16), means) + EPS)


def project(xn, wqkv, means):
    qkv = dot(xn, wqkv)
    raw_q, raw_k = qkv[:, :D], qkv[:, D : 2 * D]
    rq, rk = head_scale(raw_q, means), head_scale(raw_k, means)
    qs = (raw_q * (rq * QSCALE)).astype(BF16)
    kn = (raw_k * rk).astype(BF16)
    return qs, kn, qkv[:, 2 * D :].astype(BF16), rq, rk


def head_masks(rows):
    lane = div(iota((rows, D), 1), HD)
    return [lane == h for h in range(HEADS)]


def stack_heads(x, masks):
    zero = jnp.zeros_like(x)
    return jnp.concatenate([jnp.where(m, x, zero) for m in masks], axis=0)


def time_consts():
    row, col = iota((BLK, HEADS * BLK), 0), iota((BLK, HEADS * BLK), 1)
    diag = jnp.where(div(row, L) == div(col & (BLK - 1), L), 1.0, 0.0).astype(F32)
    ones = jnp.where(
        div(iota((HEADS * BLK, D), 0), BLK) == div(iota((HEADS * BLK, D), 1), HD), 1.0, 0.0
    ).astype(BF16)
    return diag, ones


def time_attend(q, k, v, masks, diag, ones):
    kst, vst = stack_heads(k, masks), stack_heads(v, masks)
    e = jnp.exp2(dot_rt(q, kst)) * diag
    eb = e.astype(BF16)
    rden = 1.0 / dot(eb, ones)
    return e, eb, dot(eb, vst) * rden, rden, kst, vst


def load_wqkv(w_ref):
    return jnp.concatenate([w_ref[0], w_ref[1], w_ref[2]], axis=1)


def time_forward_kernel(x_ref, w_ref, out_ref):
    means, swap = head_mean_matrix(), swap_matrix()
    masks = head_masks(BLK)
    diag, ones = time_consts()
    wqkv = load_wqkv(w_ref)
    wo = w_ref[3]

    def step(i, _):
        x = x_ref[pl.ds(i * STEP, STEP), :].astype(F32)
        xn = (x * rms_scale(x)).astype(BF16)
        qs, kn, v, _, _ = project(xn, wqkv, means)
        mixed = []
        for g in range(STEP // BLK):
            rows = slice(g * BLK, (g + 1) * BLK)
            o = time_attend(qs[rows], kn[rows], v[rows], masks, diag, ones)[2]
            mixed.append(o.astype(BF16))
        stream = (x + dot(jnp.concatenate(mixed, axis=0), wo)).astype(BF16)
        out = dot(swap, stream).astype(BF16)
        out_ref[:, pl.ds(i * L, L), :] = out.reshape(L, STEP // L, D)
        return 0

    lax.fori_loop(0, STEPS, step, 0)


def head_norm_back(r, y, g, means):
    return r * (g - y * dot((y * g).astype(BF16), means))


def query_back(rq, qs, dq, means):
    qf = qs.astype(F32)
    m = dot((qf * dq).astype(BF16), means)
    return (rq * 0.25) * (dq - qf * (m * (1.0 / (QSCALE * QSCALE))))


def key_back(rk, kn, dk, means):
    kf = kn.astype(F32)
    m = dot((kf * dk).astype(BF16), means)
    return (rk * LN2) * (dk - kf * m)


def rms_back(x, r, ng):
    xh = x * r
    return r * (ng - xh * jnp.mean(xh * ng, axis=-1, keepdims=True))


def time_backward_kernel(x_ref, sg_ref, w_ref, out_ref, grads_ref, acc, acc_o):
    means, swap = head_mean_matrix(), swap_matrix()
    masks = head_masks(BLK)
    diag, ones = time_consts()
    spread = jnp.where(
        div(iota((D, HEADS * BLK), 0), HD) == div(iota((D, HEADS * BLK), 1), BLK), 1.0, 0.0
    ).astype(BF16)
    wqkv = load_wqkv(w_ref)
    wo = w_ref[3]
    acc[...] = jnp.zeros_like(acc)
    acc_o[...] = jnp.zeros_like(acc_o)

    def step(i, _):
        x = x_ref[pl.ds(i * STEP, STEP), :].astype(F32)
        r = rms_scale(x)
        xn = (x * r).astype(BF16)
        qs, kn, v, rq, rk = project(xn, wqkv, means)
        sg = sg_ref[:, pl.ds(i * L, L), :].reshape(STEP, D)
        sgf = dot(swap, sg)
        sg = sgf.astype(BF16)
        do = dot_rt(sg, wo)
        mixed, dqs, dks, dvs = [], [], [], []
        for g in range(STEP // BLK):
            rows = slice(g * BLK, (g + 1) * BLK)
            q = qs[rows]
            e, eb, o, rden, kst, vst = time_attend(q, kn[rows], v[rows], masks, diag, ones)
            mixed.append(o.astype(BF16))
            dof = do[rows] * rden
            dob = dof.astype(BF16)
            dp = dot_rt(dob, vst) - dot((dof * o).astype(BF16), spread)
            ds = (e * dp).astype(BF16)
            dqs.append(dot(ds, kst))
            cols = [slice(h * BLK, (h + 1) * BLK) for h in range(HEADS)]
            dsr = jnp.concatenate([ds[:, c] for c in cols], axis=0)
            ebr = jnp.concatenate([eb[:, c] for c in cols], axis=0)
            dks.append(dot_lt(dsr, stack_heads(q, masks)))
            dvs.append(dot_lt(ebr, stack_heads(dob, masks)))
        mixed = jnp.concatenate(mixed, axis=0)
        qb = query_back(rq, qs, jnp.concatenate(dqs, axis=0), means).astype(BF16)
        kb = key_back(rk, kn, jnp.concatenate(dks, axis=0), means).astype(BF16)
        vb = jnp.concatenate(dvs, axis=0).astype(BF16)
        back = jnp.concatenate([qb, kb, vb], axis=1)
        ng = dot_rt(back, wqkv)
        out_ref[pl.ds(i * STEP, STEP), :] = (sgf + rms_back(x, r, ng)).astype(BF16)
        acc[...] += dot_lt(xn, back)
        acc_o[...] += dot_lt(mixed, sg)
        return 0

    lax.fori_loop(0, STEPS, step, 0)
    for j in range(3):
        grads_ref[:, j] = acc[:, j * D : (j + 1) * D].astype(BF16).reshape(16, 16, D)
    grads_ref[:, 3] = acc_o[...].astype(BF16).reshape(16, 16, D)


def channel_kernel(
    nb_ref, x_ref, up_ref, w_ref, sg_ref, back_ref, mixed_ref,
    qs_s, kn_s, v_s, do_s, rq_s, rk_s, dq_s, dk_s, dv_s,
):
    means = head_mean_matrix()
    masks = head_masks(BLK)
    wqkv = load_wqkv(w_ref)
    wo = w_ref[3]

    def first(i, _):
        at = pl.ds(i * STEP, STEP)
        x = x_ref[at, :].astype(F32)
        xn = (x * rms_scale(x)).astype(BF16)
        qs_s[at, :], kn_s[at, :], v_s[at, :], rq_s[at, :], rk_s[at, :] = project(xn, wqkv, means)
        do_s[at, :] = dot_rt(up_ref[at, :], wo).astype(BF16)
        dk_s[at, :] = jnp.zeros((STEP, D), F32)
        dv_s[at, :] = jnp.zeros((STEP, D), F32)
        return 0

    lax.fori_loop(0, STEPS, first, 0)

    def pick(parts):
        out = parts[0]
        for h in range(1, HEADS):
            out = jnp.where(masks[h], parts[h], out)
        return out

    def heads_of(x):
        return [x[h * BLK : (h + 1) * BLK] for h in range(HEADS)]

    def attend(b, _):
        at = pl.ds(b * BLK, BLK)
        near = [pl.ds(pl.multiple_of(nb_ref[b, j] * BLK, BLK), BLK) for j in range(NBR)]
        k = jnp.concatenate([kn_s[n, :] for n in near], axis=0)
        v = jnp.concatenate([v_s[n, :] for n in near], axis=0)
        qst = stack_heads(qs_s[at, :], masks)
        e = jnp.exp2(dot_rt(qst, k))
        rden = 1.0 / jnp.sum(e, axis=-1, keepdims=True)
        eb = e.astype(BF16)
        rdens = heads_of(rden)
        scale = pick([jnp.broadcast_to(d, (BLK, D)) for d in rdens])
        o = pick(heads_of(dot(eb, v))) * scale
        mixed_ref[at, :] = o.astype(BF16)
        dof = do_s[at, :].astype(F32) * scale
        prod = dof * o
        zero = jnp.zeros_like(prod)
        delta = jnp.concatenate(
            [jnp.sum(jnp.where(m, prod, zero), axis=-1, keepdims=True) for m in masks], axis=0
        )
        dost = stack_heads(dof.astype(BF16), masks)
        ds = (e * (dot_rt(dost, v) - delta)).astype(BF16)
        dq_s[at, :] = pick(heads_of(dot(ds, k)))
        dk = dot_lt(ds, qst)
        dv = dot_lt(eb, dost)
        for j, n in enumerate(near):
            rows = slice(j * BLK, (j + 1) * BLK)
            dk_s[n, :] += dk[rows]
            dv_s[n, :] += dv[rows]
        return 0

    lax.fori_loop(0, ROWS // BLK, attend, 0)

    def last(i, _):
        at = pl.ds(i * STEP, STEP)
        x = x_ref[at, :].astype(F32)
        r = rms_scale(x)
        qb = query_back(rq_s[at, :], qs_s[at, :], dq_s[at, :], means).astype(BF16)
        kb = key_back(rk_s[at, :], kn_s[at, :], dk_s[at, :], means).astype(BF16)
        back = jnp.concatenate([qb, kb, dv_s[at, :].astype(BF16)], axis=1)
        back_ref[at, :] = back
        dx = rms_back(x, r, dot_rt(back, wqkv))
        sg_ref[at, :] = (up_ref[at, :].astype(F32) + dx).astype(BF16)
        return 0

    lax.fori_loop(0, STEPS, last, 0)


def channel_grads_kernel(x_ref, up_ref, back_ref, mixed_ref, w_ref, out_ref, grads_ref, acc, acc_o):
    wo = w_ref[3]
    acc[...] = jnp.zeros_like(acc)
    acc_o[...] = jnp.zeros_like(acc_o)

    def step(i, _):
        at = pl.ds(i * STEP, STEP)
        x = x_ref[at, :].astype(F32)
        xn = (x * rms_scale(x)).astype(BF16)
        mixed = mixed_ref[at, :]
        out_ref[at, :] = (x + dot(mixed, wo)).astype(BF16)
        acc[...] += dot_lt(xn, back_ref[at, :])
        acc_o[...] += dot_lt(mixed, up_ref[at, :])
        return 0

    lax.fori_loop(0, STEPS, step, 0)
    for j in range(3):
        grads_ref[:, j] = acc[:, j * D : (j + 1) * D].astype(BF16).reshape(16, 16, D)
    grads_ref[:, 3] = acc_o[...].astype(BF16).reshape(16, 16, D)


def vmem(n=None):
    return pl.BlockSpec(memory_space=pltpu.VMEM)


def shape(dims, dtype=BF16):
    return jax.ShapeDtypeStruct(dims, dtype)


def params(mib):
    return pltpu.CompilerParams(vmem_limit_bytes=mib << 20)


def time_forward(x, w):
    return pl.pallas_call(
        time_forward_kernel,
        out_shape=shape((L, CH, D)),
        in_specs=[vmem(), vmem()],
        out_specs=vmem(),
        compiler_params=params(24),
        name="time_forward",
    )(x, w)


def time_backward(x, sg, w):
    return pl.pallas_call(
        time_backward_kernel,
        out_shape=(shape((ROWS, D)), shape((16, 4, 16, D))),
        in_specs=[vmem()] * 3,
        out_specs=(vmem(), vmem()),
        scratch_shapes=[pltpu.VMEM((D, 3 * D), F32), pltpu.VMEM((D, D), F32)],
        compiler_params=params(24),
        name="time_backward",
    )(x, sg, w)


def channel(nb, x, up, w):
    return pl.pallas_call(
        channel_kernel,
        out_shape=(shape((ROWS, D)), shape((ROWS, 3 * D)), shape((ROWS, D))),
        in_specs=[pl.BlockSpec(memory_space=pltpu.SMEM)] + [vmem()] * 3,
        out_specs=(vmem(),) * 3,
        scratch_shapes=[pltpu.VMEM((ROWS, D), BF16)] * 4 + [pltpu.VMEM((ROWS, D), F32)] * 5,
        compiler_params=params(40),
        name="channel",
    )(nb, x, up, w)


def channel_grads(x, up, back, mixed, w):
    return pl.pallas_call(
        channel_grads_kernel,
        out_shape=(shape((ROWS, D)), shape((16, 4, 16, D))),
        in_specs=[vmem()] * 5,
        out_specs=(vmem(), vmem()),
        scratch_shapes=[pltpu.VMEM((D, 3 * D), F32), pltpu.VMEM((D, D), F32)],
        compiler_params=params(24),
        name="channel_grads",
    )(x, up, back, mixed, w)


def exchange(x, axis):
    return lax.all_to_all(x, axis, split_axis=0, concat_axis=0, tiled=True)


def reduce_grads(parts):
    rows = exchange(parts, "mp")
    mine = jnp.sum(rows.astype(F32), axis=0).astype(BF16)
    every = exchange(jnp.broadcast_to(mine[None], parts.shape), "dp")
    return jnp.sum(every.astype(F32), axis=0) * (1.0 / 16)


def shards(series, upstream_grad, time_weights, channel_weights, neighbors):
    x = series.reshape(ROWS, D)
    up = upstream_grad.reshape(ROWS, D)
    stream = exchange(time_forward(x, time_weights), "mp").reshape(ROWS, D)
    sg, back, mixed = channel(neighbors, stream, up, channel_weights)
    returned = exchange(sg.reshape(16, CH, D), "mp")
    out, cparts = channel_grads(stream, up, back, mixed, channel_weights)
    cgrads = reduce_grads(cparts)
    sgrad, tparts = time_backward(x, returned, time_weights)
    tgrads = reduce_grads(tparts)
    return (
        out.reshape(1, ROWS, 1, D),
        sgrad.reshape(1, CH, L, D),
        tgrads,
        cgrads,
    )


def solution(mesh):
    placed = (P("dp", "mp", None, None), P("dp", None, "mp", None), P(), P(), P())
    return jax.shard_map(
        shards,
        mesh=mesh,
        in_specs=placed,
        out_specs=(
            P("dp", None, "mp", None),
            P("dp", "mp", None, None),
            P(None, "mp", None),
            P(None, "mp", None),
        ),
        check_vma=False,
    )
```

time: 591 us -> 206 us (0.35)
  the two profiles are of different devices: /device:TPU:7 before, /device:TPU:1 now
where the time goes in v1:
time: 206 us; the launch traced here: 205 us
  waiting for transfers between devices  75.4 us (37%)
  Pallas kernels  68.4 us (33%)
  starting transfers between devices  44.1 us (21%)
  local copies, waits for them, and re-layouts  14.9 us (7%)
    all_to_all x6, waiting for transfers between devices, exchange(): return lax.all_to_all(x, axis, split_axis=0, concat_axis=0, tiled=True)  75.4 us
    all_to_all x6, starting transfers between devices, exchange(): return lax.all_to_all(x, axis, split_axis=0, concat_axis=0, tiled=True)  44.1 us
    pallas_call x1, Pallas kernels, channel(): pl.pallas_call(channel_kernel, out_shape=(shape((ROWS, D)), shape((ROWS,...  32.3 us
    pallas_call x1, Pallas kernels, time_backward(): pl.pallas_call(time_backward_kernel, out_shape=(shape((ROWS, D)), shape((...  19.7 us
    unnamed x31, local copies, waits for them, and re-layouts  13.2 us
    pallas_call x1, Pallas kernels, time_forward(): pl.pallas_call(time_forward_kernel, out_shape=shape((L, CH, D)), in_specs...  11.9 us
    pallas_call x1, Pallas kernels, channel_grads(): pl.pallas_call(channel_grads_kernel, out_shape=(shape((ROWS, D)), shape((...  4.48 us
  transfers between devices with their start and end apart: 6, of which 5 were waited for; matrix products, arithmetic and copies ran while one was open for 0% of the time, Pallas kernels for 12%

profile of v1, /device:TPU:1, one launch (start us, length us, event | category | flops | bytes accessed | tf_op | source)
XLA Modules:
  0.0 205.1 jit_solution(14334567007402018965)
XLA Ops:
  0.6 0.0 copy-start
  0.6 1.2 copy-done
  1.9 0.0 copy-start.6
  1.9 1.0 copy-done.6
  2.9 0.0 copy-start.14
  2.9 0.0 copy-start.2
  2.9 0.0 copy-start.8
  2.9 11.9 %time_forward.1 = bf16[16,128,256]{2,1,0:T(8,128)(2,1)} custom-call(bf16[2048,256]{1,0:T(8,128)(2,1)S(1)} %bitcast.8, bf16[4,256,256]{2,1,0:T(8,128)(2,1)S(1)} %copy-done.6), custom_call_target="tpu_custom_call" | custom-call | tf_op jit(solution)/shard_map/time_forward/pallas_call | solution.py:315
  14.8 10.1 %all-to-all-start = ((bf16[16,128,256]{2,1,0:T(8,128)(2,1)}), bf16[16,128,256]{2,1,0:T(8,128)(2,1)S(1)}, u32[]{:S(2)}, u32[]{:S(2)}) async-start(bf16[16,128,256]{2,1,0:T(8,128)(2,1)} %time_forward.1), calls=%async_computation | async-start | bytes 2097152 | tf_op jit(solution)/shard_map/all_to_all | solution.py:362
  25.0 0.0 copy-done.14
  25.0 0.1 copy.10.nb_ref
  25.0 25.6 %all-to-all-done = bf16[16,128,256]{2,1,0:T(8,128)(2,1)S(1)} async-done(((bf16[16,128,256]{2,1,0:T(8,128)(2,1)}), bf16[16,128,256]{2,1,0:T(8,128)(2,1)S(1)}, u32[]{:S(2)}, u32[]{:S(2)}) %all-to-all-start) | async-done | bytes 1048608 | tf_op jit(solution)/shard_map/all_to_all | solution.py:362
  50.7 0.0 copy-done.2
  50.7 0.0 copy-done.8
  50.7 32.3 %channel.1 = (bf16[2048,256]{1,0:T(8,128)(2,1)S(1)}, bf16[2048,768]{1,0:T(8,128)(2,1)S(1)}, bf16[2048,256]{1,0:T(8,128)(2,1)S(1)}) custom-call(s32[16,3]{1,0:T(8,128)S(1)} %copy.10.nb_ref, bf16[2048,256]{1,0:T(8,128)(2,1)S(1)} %bitcast.6, bf16[2048,256]{1,0:T(8,128)(2,1)S(1)} %bitcast.10, bf16[4,256,256]{2,1,0:T(8,128)(2,1)S(1)} %copy-done.8), custom_call_target="tpu_custom_call" | custom-call | tf_op jit(solution)/shard_map/channel/pallas_call | solution.py:338
  83.0 0.0 copy-start.4
  83.0 1.6 copy-done.4
  84.6 0.0 copy-start.10
  84.6 1.0 copy-done.10
  85.6 0.0 copy-start.11
  85.6 1.0 copy-done.11
  86.6 6.0 %all-to-all-start.1 = ((bf16[16,128,256]{2,1,0:T(8,128)(2,1)}), bf16[16,128,256]{2,1,0:T(8,128)(2,1)S(1)}, u32[]{:S(2)}, u32[]{:S(2)}) async-start(bf16[16,128,256]{2,1,0:T(8,128)(2,1)} %bitcast.12), calls=%async_computation.1 | async-start | bytes 2097152 | tf_op jit(solution)/shard_map/all_to_all | solution.py:362
  92.6 0.0 copy-start.3
  92.6 1.2 copy-done.3
  93.8 0.0 copy-start.5
  93.8 1.9 copy-done.5
  95.7 0.0 copy-start.9
  95.7 1.0 copy-done.9
  96.7 0.0 copy-start.12
  96.7 1.2 copy-done.12
  97.9 0.0 copy-start.1
  97.9 4.5 %channel_grads.1 = (bf16[2048,256]{1,0:T(8,128)(2,1)}, bf16[16,4,16,256]{3,2,1,0:T(8,128)(2,1)S(1)}) custom-call(bf16[2048,256]{1,0:T(8,128)(2,1)S(1)} %bitcast.7, bf16[2048,256]{1,0:T(8,128)(2,1)S(1)} %bitcast.11, bf16[2048,768]{1,0:T(8,128)(2,1)S(1)} %copy-done.5, bf16[2048,256]{1,0:T(8,128)(2,1)S(1)} %copy-done.12, bf16[4,256,256]{2,1,0:T(8,128)(2,1)S(1)} %copy-done.9), custom_call_target="tpu_custom_call" | custom-call | tf_op jit(solution)/shard_map/channel_grads/pallas_call | solution.py:350
  102.4 0.0 copy-start.13
  102.4 0.8 copy-done.13
  103.2 14.8 %all-to-all-done.1.sg_ref = bf16[16,128,256]{2,1,0:T(8,128)(2,1)S(1)} async-done(((bf16[16,128,256]{2,1,0:T(8,128)(2,1)}), bf16[16,128,256]{2,1,0:T(8,128)(2,1)S(1)}, u32[]{:S(2)}, u32[]{:S(2)}) %all-to-all-start.1) | async-done | bytes 1048608 | tf_op jit(solution)/shard_map/all_to_all | solution.py:362
  118.0 6.2 %all-to-all-start.4 = ((bf16[16,4,16,256]{3,2,1,0:T(8,128)(2,1)}), bf16[16,4,16,256]{3,2,1,0:T(8,128)(2,1)S(1)}, u32[]{:S(2)}, u32[]{:S(2)}) async-start(bf16[16,4,16,256]{3,2,1,0:T(8,128)(2,1)} %copy-done.13), calls=%async_computation.4 | async-start | bytes 1048576 | tf_op jit(solution)/shard_map/all_to_all | solution.py:362
  124.2 0.0 copy-done.1
  124.2 0.0 copy-start.7
  124.2 1.0 copy-done.7
  125.3 19.7 %time_backward.1 = (bf16[2048,256]{1,0:T(8,128)(2,1)}, bf16[16,4,16,256]{3,2,1,0:T(8,128)(2,1)}) custom-call(bf16[2048,256]{1,0:T(8,128)(2,1)S(1)} %bitcast.9, bf16[16,128,256]{2,1,0:T(8,128)(2,1)S(1)} %all-to-all-done.1.sg_ref, bf16[4,256,256]{2,1,0:T(8,128)(2,1)S(1)} %copy-done.7), custom_call_target="tpu_custom_call" | custom-call | tf_op jit(solution)/shard_map/time_backward/pallas_call | solution.py:326
  145.0 0.0 all-to-all-done.4
  145.0 7.5 %all-to-all-start.2 = ((bf16[16,4,16,256]{3,2,1,0:T(8,128)(2,1)}), bf16[16,4,16,256]{3,2,1,0:T(8,128)(2,1)S(1)}, u32[]{:S(2)}, u32[]{:S(2)}) async-start(bf16[16,4,16,256]{3,2,1,0:T(8,128)(2,1)} %get-tuple-element.16), calls=%async_computation.2 | async-start | bytes 1048576 | tf_op jit(solution)/shard_map/all_to_all | solution.py:362
  152.5 0.1 reduce_sum.44
  152.6 12.9 %all-to-all-done.2 = bf16[16,4,16,256]{3,2,1,0:T(8,128)(2,1)S(1)} async-done(((bf16[16,4,16,256]{3,2,1,0:T(8,128)(2,1)}), bf16[16,4,16,256]{3,2,1,0:T(8,128)(2,1)S(1)}, u32[]{:S(2)}, u32[]{:S(2)}) %all-to-all-start.2) | async-done | bytes 524320 | tf_op jit(solution)/shard_map/all_to_all | solution.py:362
  165.5 0.9 broadcast_in_dim.5
  166.4 9.8 %all-to-all-start.5 = ((bf16[16,4,16,256]{3,2,1,0:T(8,128)(2,1)}), bf16[16,4,16,256]{3,2,1,0:T(8,128)(2,1)S(1)}, u32[]{:S(2)}, u32[]{:S(2)}) async-start(bf16[16,4,16,256]{3,2,1,0:T(8,128)(2,1)} %broadcast_in_dim.5), calls=%async_computation.5 | async-start | bytes 1048576 | tf_op jit(solution)/shard_map/all_to_all | solution.py:362
  176.2 0.1 reduce_sum.42
  176.3 11.3 %all-to-all-done.5 = bf16[16,4,16,256]{3,2,1,0:T(8,128)(2,1)S(1)} async-done(((bf16[16,4,16,256]{3,2,1,0:T(8,128)(2,1)}), bf16[16,4,16,256]{3,2,1,0:T(8,128)(2,1)S(1)}, u32[]{:S(2)}, u32[]{:S(2)}) %all-to-all-start.5) | async-done | bytes 524320 | tf_op jit(solution)/shard_map/all_to_all | solution.py:362
  187.6 0.9 broadcast_in_dim.4
  188.4 4.4 %all-to-all-start.3 = ((bf16[16,4,16,256]{3,2,1,0:T(8,128)(2,1)}), bf16[16,4,16,256]{3,2,1,0:T(8,128)(2,1)S(1)}, u32[]{:S(2)}, u32[]{:S(2)}) async-start(bf16[16,4,16,256]{3,2,1,0:T(8,128)(2,1)} %broadcast_in_dim.4), calls=%async_computation.3 | async-start | bytes 1048576 | tf_op jit(solution)/shard_map/all_to_all | solution.py:362
  192.9 0.1 convert_reduce_fusion
  192.9 0.6 broadcast_multiply_fusion
  193.6 10.8 %all-to-all-done.3 = bf16[16,4,16,256]{3,2,1,0:T(8,128)(2,1)S(1)} async-done(((bf16[16,4,16,256]{3,2,1,0:T(8,128)(2,1)}), bf16[16,4,16,256]{3,2,1,0:T(8,128)(2,1)S(1)}, u32[]{:S(2)}, u32[]{:S(2)}) %all-to-all-start.3) | async-done | bytes 524320 | tf_op jit(solution)/shard_map/all_to_all | solution.py:362
  204.4 0.1 convert_reduce_fusion.1
  204.4 0.6 broadcast_multiply_fusion.1
Async XLA Ops:
  0.6 1.2 copy-start
  1.9 1.0 copy-start.6
  2.9 22.1 %copy-start.14 = (s32[16,3]{0,1:T(4,128)S(1)}, s32[16,3]{0,1:T(4,128)}, u32[]{:S(2)}) copy-start(s32[16,3]{0,1:T(4,128)} %param.9) | copy-start | bytes 580
  2.9 47.8 %copy-start.2 = (bf16[1,2048,1,256]{3,1,2,0:T(8,128)(2,1)S(1)}, bf16[1,2048,1,256]{3,1,2,0:T(8,128)(2,1)}, u32[]{:S(2)}) copy-start(bf16[1,2048,1,256]{3,1,2,0:T(8,128)(2,1)} %param.6) | copy-start | bytes 3145732
  2.9 47.8 %copy-start.8 = (bf16[4,256,256]{2,1,0:T(8,128)(2,1)S(1)}, bf16[4,256,256]{2,1,0:T(8,128)(2,1)}, u32[]{:S(2)}) copy-start(bf16[4,256,256]{2,1,0:T(8,128)(2,1)} %w_ref.6) | copy-start | bytes 1572868
  14.8 35.8 %all-to-all-start = ((bf16[16,128,256]{2,1,0:T(8,128)(2,1)}), bf16[16,128,256]{2,1,0:T(8,128)(2,1)S(1)}, u32[]{:S(2)}, u32[]{:S(2)}) async-start(bf16[16,128,256]{2,1,0:T(8,128)(2,1)} %time_forward.1), calls=%async_computation | async-start | bytes 2097152 | tf_op jit(solution)/shard_map/all_to_all | solution.py:362
  83.0 1.6 copy-start.4
  84.6 1.0 copy-start.10
  85.6 1.0 copy-start.11
  86.6 31.4 %all-to-all-start.1 = ((bf16[16,128,256]{2,1,0:T(8,128)(2,1)}), bf16[16,128,256]{2,1,0:T(8,128)(2,1)S(1)}, u32[]{:S(2)}, u32[]{:S(2)}) async-start(bf16[16,128,256]{2,1,0:T(8,128)(2,1)} %bitcast.12), calls=%async_computation.1 | async-start | bytes 2097152 | tf_op jit(solution)/shard_map/all_to_all | solution.py:362
  92.6 1.2 copy-start.3
  93.8 1.9 copy-start.5
  95.7 1.0 copy-start.9
  96.7 1.2 copy-start.12
  97.9 26.3 %copy-start.1 = (bf16[1,128,16,256]{3,2,1,0:T(8,128)(2,1)S(1)}, bf16[1,128,16,256]{3,2,1,0:T(8,128)(2,1)}, u32[]{:S(2)}) copy-start(bf16[1,128,16,256]{3,2,1,0:T(8,128)(2,1)} %param.5) | copy-start | bytes 3145732
  102.4 0.8 copy-start.13
  118.0 27.0 %all-to-all-start.4 = ((bf16[16,4,16,256]{3,2,1,0:T(8,128)(2,1)}), bf16[16,4,16,256]{3,2,1,0:T(8,128)(2,1)S(1)}, u32[]{:S(2)}, u32[]{:S(2)}) async-start(bf16[16,4,16,256]{3,2,1,0:T(8,128)(2,1)} %copy-done.13), calls=%async_computation.4 | async-start | bytes 1048576 | tf_op jit(solution)/shard_map/all_to_all | solution.py:362
  124.2 1.0 copy-start.7
  145.0 20.5 %all-to-all-start.2 = ((bf16[16,4,16,256]{3,2,1,0:T(8,128)(2,1)}), bf16[16,4,16,256]{3,2,1,0:T(8,128)(2,1)S(1)}, u32[]{:S(2)}, u32[]{:S(2)}) async-start(bf16[16,4,16,256]{3,2,1,0:T(8,128)(2,1)} %get-tuple-element.16), calls=%async_computation.2 | async-start | bytes 1048576 | tf_op jit(solution)/shard_map/all_to_all | solution.py:362
  166.4 21.2 %all-to-all-start.5 = ((bf16[16,4,16,256]{3,2,1,0:T(8,128)(2,1)}), bf16[16,4,16,256]{3,2,1,0:T(8,128)(2,1)S(1)}, u32[]{:S(2)}, u32[]{:S(2)}) async-start(bf16[16,4,16,256]{3,2,1,0:T(8,128)(2,1)} %broadcast_in_dim.5), calls=%async_computation.5 | async-start | bytes 1048576 | tf_op jit(solution)/shard_map/all_to_all | solution.py:362
  188.4 15.9 %all-to-all-start.3 = ((bf16[16,4,16,256]{3,2,1,0:T(8,128)(2,1)}), bf16[16,4,16,256]{3,2,1,0:T(8,128)(2,1)S(1)}, u32[]{:S(2)}, u32[]{:S(2)}) async-start(bf16[16,4,16,256]{3,2,1,0:T(8,128)(2,1)} %broadcast_in_dim.4), calls=%async_computation.3 | async-start | bytes 1048576 | tf_op jit(solution)/shard_map/all_to_all | solution.py:362

commit v2 on v1

v2 whole, which is shorter than its diff:
```python
import jax
import jax.numpy as jnp
from jax import lax
from jax.experimental import pallas as pl
from jax.experimental.pallas import tpu as pltpu
from jax.sharding import PartitionSpec as P

HEADS = 4
D = 256
HD = D // HEADS
L = 16
CH = 128
BLK = 128
NBR = 3
ROWS = 2048
SQ = 256
GROUPS = 2
EPS = 1e-06
LOG2E = 1.4426950408889634
LN2 = 0.6931471805599453
QSCALE = 0.25 * LOG2E
F32 = jnp.float32
BF16 = jnp.bfloat16


def dot(a, b):
    return lax.dot_general(a, b, (((1,), (0,)), ((), ())), preferred_element_type=F32)


def dot_rt(a, b):
    return lax.dot_general(a, b, (((1,), (1,)), ((), ())), preferred_element_type=F32)


def dot_lt(a, b):
    return lax.dot_general(a, b, (((0,), (0,)), ((), ())), preferred_element_type=F32)


def iota(shape, dim):
    return lax.broadcasted_iota(jnp.int32, shape, dim)


def div(a, n):
    return lax.shift_right_logical(a, jnp.int32(n.bit_length() - 1))


def head_mean_matrix():
    same = div(iota((D, D), 0), HD) == div(iota((D, D), 1), HD)
    return jnp.where(same, 1.0 / HD, 0.0).astype(BF16)


def swap_matrix():
    row, col = iota((D, D), 0), iota((D, D), 1)
    same = (div(row, L) == (col & (L - 1))) & ((row & (L - 1)) == div(col, L))
    return jnp.where(same, 1.0, 0.0).astype(BF16)


def rms_scale(x):
    return lax.rsqrt(jnp.mean(x * x, axis=-1, keepdims=True) + EPS)


def head_scale(raw, means):
    return lax.rsqrt(dot((raw * raw).astype(BF16), means) + EPS)


def project(xn, wqkv, means):
    qkv = dot(xn, wqkv)
    raw_q, raw_k = qkv[:, :D], qkv[:, D : 2 * D]
    rq, rk = head_scale(raw_q, means), head_scale(raw_k, means)
    qs = (raw_q * (rq * QSCALE)).astype(BF16)
    kn = (raw_k * rk).astype(BF16)
    return qs, kn, qkv[:, 2 * D :].astype(BF16), rq, rk


def head_masks(rows):
    lane = div(iota((rows, D), 1), HD)
    return [lane == h for h in range(HEADS)]


def stack_heads(x, masks):
    zero = jnp.zeros_like(x)
    return jnp.concatenate([jnp.where(m, x, zero) for m in masks], axis=0)


def time_diag():
    row, col = iota((BLK, HEADS * BLK), 0), iota((BLK, HEADS * BLK), 1)
    return jnp.where(div(row, L) == div(col & (BLK - 1), L), 1.0, 0.0).astype(F32)


def head_columns():
    return [slice(h * BLK, (h + 1) * BLK) for h in range(HEADS)]


def stack_product(xts, parts):
    out = []
    for xt, p in zip(xts, parts):
        heads = [dot(xt[h * HD : (h + 1) * HD], p[:, c]) for h, c in enumerate(head_columns())]
        out.append(jnp.concatenate(heads, axis=0).T)
    return out


def softmax_columns(es):
    return [e * (1.0 / jnp.sum(e, axis=0, keepdims=True)) for e in es]


def score_grads(ps, dps):
    ts = [p * dp for p, dp in zip(ps, dps)]
    return [
        (t - p * jnp.sum(t, axis=0, keepdims=True)).astype(BF16) for t, p in zip(ts, ps)
    ]


def split(x, size=BLK):
    return [x[i : i + size] for i in range(0, x.shape[0], size)]


def join(parts):
    return jnp.concatenate(parts, axis=0)


def load_wqkv(w_ref):
    return jnp.concatenate([w_ref[0], w_ref[1], w_ref[2]], axis=1)


def loop(size, body):
    def step(i, carry):
        body(i, pl.ds(pl.multiple_of(i * size, size), size))
        return carry

    lax.fori_loop(0, ROWS // size, step, 0)


def copies(src, dst, sems, size):
    return [
        pltpu.make_async_copy(
            src.at[pl.ds(i * size, size)], dst.at[pl.ds(i * size, size)], sems.at[i]
        )
        for i in range(ROWS // size)
    ]


def kept_copies(srcs, dsts, sems, size):
    out = []
    for i in range(ROWS // size):
        step = []
        for n, (src, dst) in enumerate(zip(srcs, dsts)):
            rows = size // BLK if len(src.shape) == 3 else size
            at = pl.ds(i * rows, rows)
            step.append(pltpu.make_async_copy(src.at[at], dst.at[at], sems.at[n, i]))
        out.append(step)
    return out


A_STEP = 1024


def time_forward_kernel(x_hbm, w_hbm, out_hbm, x_ref, w_ref, out_ref, w_sem, in_sem, out_sem):
    w_in = pltpu.make_async_copy(w_hbm, w_ref, w_sem)
    x_in = copies(x_hbm, x_ref, in_sem, A_STEP)
    x_in[0].start()
    w_in.start()
    for c in x_in[1:]:
        c.start()
    means, swap = head_mean_matrix(), swap_matrix()
    masks = head_masks(BLK)
    diag = time_diag()
    ones = jnp.where(
        div(iota((HEADS * BLK, D), 0), BLK) == div(iota((HEADS * BLK, D), 1), HD), 1.0, 0.0
    ).astype(BF16)
    chans = A_STEP // L
    outs = []
    for i in range(ROWS // A_STEP):
        x_in[i].wait()
        if i == 0:
            w_in.wait()
            wqkv = load_wqkv(w_ref)
            wo = w_ref[3]
        x = x_ref[i * A_STEP : (i + 1) * A_STEP, :].astype(F32)
        xn = (x * rms_scale(x)).astype(BF16)
        qs, kn, v, _, _ = project(xn, wqkv, means)
        es = [
            (jnp.exp2(dot_rt(q, stack_heads(k, masks))) * diag).astype(BF16)
            for q, k in zip(split(qs), split(kn))
        ]
        dens = [dot(e, ones) for e in es]
        os = [dot(e, stack_heads(u, masks)) for e, u in zip(es, split(v))]
        mixed = join([(o * (1.0 / den)).astype(BF16) for o, den in zip(os, dens)])
        stream = (x + dot(mixed, wo)).astype(BF16)
        for j, part in enumerate(split(stream, SQ)):
            at = i * chans + j * L
            out_ref[:, at : at + L, :] = dot(swap, part).astype(BF16).reshape(L, L, D)
        at = pl.ds(i * chans, chans)
        c = pltpu.make_async_copy(out_ref.at[:, at], out_hbm.at[:, at], out_sem.at[i])
        c.start()
        outs.append(c)
    for c in outs:
        c.wait()


PREP_STEP = 512


def prepare_kernel(x_ref, w_ref, *refs):
    outs, (xn_ref, qs_ref, kn_ref, v_ref, rq_ref, rk_ref, p_ref, mixed_ref), sems = (
        refs[:8], refs[8:16], refs[16],
    )
    means = head_mean_matrix()
    masks = head_masks(BLK)
    diag = time_diag()
    wqkv = load_wqkv(w_ref)
    groups = PREP_STEP // BLK
    moves = kept_copies(refs[8:16], outs, sems, PREP_STEP)
    for i in range(ROWS // PREP_STEP):
        at = slice(i * PREP_STEP, (i + 1) * PREP_STEP)
        x = x_ref[at, :].astype(F32)
        xn = (x * rms_scale(x)).astype(BF16)
        qs, kn, v, rq, rk = project(xn, wqkv, means)
        xn_ref[at, :] = xn
        qs_ref[at, :] = qs
        kn_ref[at, :] = kn
        v_ref[at, :] = v
        rq_ref[at, :] = rq.astype(BF16)
        rk_ref[at, :] = rk.astype(BF16)
        es = [
            jnp.exp2(dot_rt(k, stack_heads(q, masks))) * diag
            for q, k in zip(split(qs), split(kn))
        ]
        pbs = [p.astype(BF16) for p in softmax_columns(es)]
        p_ref[i * groups : (i + 1) * groups] = jnp.stack(pbs)
        os = stack_product([u.T for u in split(v)], pbs)
        mixed_ref[at, :] = join(os).astype(BF16)
        for c in moves[i]:
            c.start()
    for step in moves:
        for c in step:
            c.wait()


def head_back(r, y, g, means, scale):
    yf = y.astype(F32)
    m = dot((yf * g).astype(BF16), means)
    return r * (g - yf * (m * scale))


def query_back(rq, qs, dq, means):
    return head_back(rq, qs, dq, means, 1.0 / (QSCALE * QSCALE)).astype(BF16)


def key_back(rk, kn, dk, means):
    return head_back(rk * LN2, kn, dk, means, 1.0).astype(BF16)


def rms_back(x, r, ng):
    xh = x * r
    return r * (ng - xh * jnp.mean(xh * ng, axis=-1, keepdims=True))


def write_grads(grads_ref, acc, acc_o):
    for j in range(4):
        whole = (acc[:, j * D : (j + 1) * D] if j < 3 else acc_o[...]).reshape(16, 2, 8, D)
        for half in range(2):
            grads_ref[half, :, j] = whole[:, half].astype(BF16)


T_STEP = 512


def time_backward_kernel(sg_ref, w_hbm, *refs):
    kept_hbm, back_hbm, grads_ref = refs[:8], refs[8], refs[9]
    w_ref, kept, back_ref, acc, acc_o = refs[10], refs[11:19], refs[19], refs[20], refs[21]
    w_sem, in_sem, out_sem = refs[22:]
    xn_ref, qs_ref, kn_ref, v_ref, rq_ref, rk_ref, p_ref, mixed_ref = kept
    w_in = pltpu.make_async_copy(w_hbm, w_ref, w_sem)
    w_in.start()
    moves = kept_copies(kept_hbm, kept, in_sem, T_STEP)
    for step in moves:
        for c in step:
            c.start()
    back_out = copies(back_ref, back_hbm, out_sem, T_STEP)
    means, swap = head_mean_matrix(), swap_matrix()
    masks = head_masks(BLK)
    groups, chans = T_STEP // BLK, T_STEP // L
    w_in.wait()
    wo = w_ref[...]
    for i in range(ROWS // T_STEP):
        at = slice(i * T_STEP, (i + 1) * T_STEP)
        sg = []
        for j in range(T_STEP // SQ):
            part = sg_ref[:, i * chans + j * L : i * chans + (j + 1) * L, :]
            sg.append(dot(swap, part.reshape(SQ, D)).astype(BF16))
        sg = join(sg)
        do = dot_rt(sg, wo).astype(BF16)
        for c in moves[i]:
            c.wait()
        qs, kn = qs_ref[at, :], kn_ref[at, :]
        pbs = [p_ref[i * groups + g] for g in range(groups)]
        dosts = [stack_heads(d, masks) for d in split(do)]
        dps = [dot_rt(v, d) for v, d in zip(split(v_ref[at, :]), dosts)]
        dss = score_grads([p.astype(F32) for p in pbs], dps)
        vb = join([dot(p, d).astype(BF16) for p, d in zip(pbs, dosts)])
        dk = join([dot(ds, stack_heads(q, masks)) for ds, q in zip(dss, split(qs))])
        dq = join(stack_product([k.T for k in split(kn)], dss))
        qb = query_back(rq_ref[at, :].astype(F32) * 0.25, qs, dq, means)
        kb = key_back(rk_ref[at, :].astype(F32), kn, dk, means)
        back = jnp.concatenate([qb, kb, vb], axis=1)
        back_ref[at, :] = back
        back_out[i].start()
        part, part_o = dot_lt(xn_ref[at, :], back), dot_lt(mixed_ref[at, :], sg)
        acc[...] = part if i == 0 else acc[...] + part
        acc_o[...] = part_o if i == 0 else acc_o[...] + part_o
    write_grads(grads_ref, acc, acc_o)
    for c in back_out:
        c.wait()


S_STEP = 512


def series_grad_kernel(x_ref, sg_ref, back_ref, w_ref, out_ref):
    swap = swap_matrix()
    wqkv = load_wqkv(w_ref)
    chans = S_STEP // L

    def body(i, at):
        x = x_ref[at, :].astype(F32)
        sg = []
        for j in range(S_STEP // SQ):
            part = sg_ref[:, pl.ds(pl.multiple_of(i * chans + j * L, L), L), :]
            sg.append(dot(swap, part.reshape(SQ, D)))
        ng = dot_rt(back_ref[at, :], wqkv)
        out_ref[at, :] = (join(sg) + rms_back(x, rms_scale(x), ng)).astype(BF16)

    loop(S_STEP, body)


C_STEP = 512


def channel_kernel(
    nb_ref, x_ref, up_hbm, w_hbm, sg_hbm, back_hbm, mixed_hbm,
    up_ref, w_ref, do_ref, up_sem, w_sem, sg_s, back_s, mixed_s, qs_s, kn_s, v_s, kt_s, vt_s, rq_s, rk_s, dq_s, dk_s, dv_s,
    sg_sem, back_sem, mixed_sem,
):
    w_in = pltpu.make_async_copy(w_hbm, w_ref, w_sem)
    w_in.start()
    up_in = pltpu.make_async_copy(up_hbm, up_ref, up_sem)
    up_in.start()
    means = head_mean_matrix()
    masks = head_masks(BLK)
    w_in.wait()
    wqkv = load_wqkv(w_ref)
    wo = w_ref[3]
    up_in.wait()

    def first(i, at):
        do_ref[at, :] = dot_rt(up_ref[at, :], wo).astype(BF16)
        x = x_ref[at, :].astype(F32)
        xn = (x * rms_scale(x)).astype(BF16)
        qs, kn, v, rq_s[at, :], rk_s[at, :] = project(xn, wqkv, means)
        qs_s[at, :] = qs
        kn_s[at, :] = kn
        v_s[at, :] = v
        kt_s[:, at] = kn.T
        vt_s[:, at] = v.T
        dk_s[at, :] = jnp.zeros((C_STEP, D), F32)
        dv_s[at, :] = jnp.zeros((C_STEP, D), F32)

    loop(C_STEP, first)

    def attend(i, carry):
        bs = [i * GROUPS + g for g in range(GROUPS)]
        ats = [pl.ds(pl.multiple_of(b * BLK, BLK), BLK) for b in bs]
        nears = [
            [pl.ds(pl.multiple_of(nb_ref[b, j] * BLK, BLK), BLK) for j in range(NBR)] for b in bs
        ]
        qsts = [stack_heads(qs_s[at, :], masks) for at in ats]
        es = [
            jnp.exp2(dot_rt(join([kn_s[n, :] for n in near]), q))
            for near, q in zip(nears, qsts)
        ]
        dosts = [stack_heads(do_ref[at, :], masks) for at in ats]
        dps = [dot_rt(join([v_s[n, :] for n in near]), d) for near, d in zip(nears, dosts)]
        ps = softmax_columns(es)
        pbs = [p.astype(BF16) for p in ps]
        dss = score_grads(ps, dps)
        dvs = [dot(p, d) for p, d in zip(pbs, dosts)]
        os = stack_product(
            [jnp.concatenate([vt_s[:, n] for n in near], axis=1) for near in nears], pbs
        )
        dks = [dot(ds, q) for ds, q in zip(dss, qsts)]
        dqs = stack_product(
            [jnp.concatenate([kt_s[:, n] for n in near], axis=1) for near in nears], dss
        )
        for at, o, dq in zip(ats, os, dqs):
            mixed_s[at, :] = o.astype(BF16)
            dq_s[at, :] = dq
        for near, dk, dv in zip(nears, dks, dvs):
            for n, k_part, v_part in zip(near, split(dk), split(dv)):
                dk_s[n, :] += k_part
                dv_s[n, :] += v_part
        return carry

    lax.fori_loop(0, ROWS // BLK // GROUPS, attend, 0)

    mixed_out = pltpu.make_async_copy(mixed_s, mixed_hbm, mixed_sem)
    mixed_out.start()
    sg_out = copies(sg_s, sg_hbm, sg_sem, C_STEP)
    back_out = copies(back_s, back_hbm, back_sem, C_STEP)
    for i in range(ROWS // C_STEP):
        at = slice(i * C_STEP, (i + 1) * C_STEP)
        x = x_ref[at, :].astype(F32)
        r = rms_scale(x)
        qb = query_back(rq_s[at, :] * 0.25, qs_s[at, :], dq_s[at, :], means)
        kb = key_back(rk_s[at, :], kn_s[at, :], dk_s[at, :], means)
        back = jnp.concatenate([qb, kb, dv_s[at, :].astype(BF16)], axis=1)
        back_s[at, :] = back
        back_out[i].start()
        dx = rms_back(x, r, dot_rt(back, wqkv))
        sg_s[at, :] = (up_ref[at, :].astype(F32) + dx).astype(BF16)
        sg_out[i].start()
    mixed_out.wait()
    for c in back_out + sg_out:
        c.wait()


G_STEP = 512


def channel_grads_kernel(x_ref, up_ref, back_ref, mixed_ref, w_ref, out_ref, grads_ref, acc, acc_o):
    wo = w_ref[3]
    acc[...] = jnp.zeros_like(acc)
    acc_o[...] = jnp.zeros_like(acc_o)

    def body(i, at):
        x = x_ref[at, :].astype(F32)
        xn = (x * rms_scale(x)).astype(BF16)
        mixed = mixed_ref[at, :]
        out_ref[at, :] = (x + dot(mixed, wo)).astype(BF16)
        acc[...] += dot_lt(xn, back_ref[at, :])
        acc_o[...] += dot_lt(mixed, up_ref[at, :])

    loop(G_STEP, body)
    write_grads(grads_ref, acc, acc_o)


VM = pl.BlockSpec(memory_space=pltpu.VMEM)
HB = pl.BlockSpec(memory_space=pltpu.HBM)
SM = pl.BlockSpec(memory_space=pltpu.SMEM)
DMA = pltpu.SemaphoreType.DMA


def shape(dims, dtype=BF16):
    return jax.ShapeDtypeStruct(dims, dtype)


def vm(dims, dtype=BF16):
    return pltpu.VMEM(dims, dtype)


ROW = (ROWS, D)
GRADS = (2, 16, 4, 8, D)


def call(kernel, name, mib, outs, ins, out_specs, args, scratch=(), flops=0):
    args = [
        pltpu.with_memory_space_constraint(a, pltpu.HBM) if spec is HB else a
        for a, spec in zip(args, ins)
    ]
    return pl.pallas_call(
        kernel,
        out_shape=[
            pltpu.HBM(o.shape, o.dtype) if spec is HB else o for o, spec in zip(outs, out_specs)
        ],
        in_specs=ins,
        out_specs=out_specs,
        scratch_shapes=scratch,
        compiler_params=pltpu.CompilerParams(vmem_limit_bytes=mib << 20),
        cost_estimate=pl.CostEstimate(
            flops=flops, bytes_accessed=8 << 20, transcendentals=1 << 20
        ),
        name=name,
    )(*args)


def time_forward(x, w):
    return call(
        time_forward_kernel, "time_forward", 24, [shape((L, CH, D))], [HB, HB], [HB], (x, w),
        [vm(ROW), vm((4, D, D)), vm((L, CH, D)), DMA, DMA((2,)), DMA((2,))],
        flops=2 * 10**9,
    )[0]


def prepare(x, w):
    names = [shape(ROW)] * 6 + [shape((ROWS // BLK, BLK, HEADS * BLK)), shape(ROW)]
    return call(
        prepare_kernel, "prepare", 28, names, [VM] * 2, [HB] * 8, (x, w),
        [vm(o.shape) for o in names] + [DMA((8, ROWS // PREP_STEP))],
        flops=3 * 10**9,
    )


def channel(nb, x, up, w):
    return call(
        channel_kernel, "channel", 36,
        [shape(ROW), shape((ROWS, 3 * D)), shape(ROW)],
        [SM, VM, HB, HB], [HB] * 3, (nb, x, up, w),
        [vm(ROW), vm((4, D, D)), vm(ROW), DMA, DMA]
        + [vm(ROW), vm((ROWS, 3 * D)), vm(ROW), vm(ROW), vm(ROW), vm(ROW)]
        + [vm((D, ROWS))] * 2 + [vm(ROW, F32)] * 5 + [DMA((4,)), DMA((4,)), DMA],
        flops=8 * 10**9,
    )


def channel_grads(x, up, back, mixed, w):
    return call(
        channel_grads_kernel, "channel_grads", 20, [shape(ROW), shape(GRADS)],
        [VM] * 5, [VM] * 2, (x, up, back, mixed, w),
        [vm((D, 3 * D), F32), vm((D, D), F32)], flops=2 * 10**9,
    )


def time_backward(sg, kept, w):
    return call(
        time_backward_kernel, "time_backward", 30, [shape((ROWS, 3 * D)), shape(GRADS)],
        [VM] + [HB] * 9, [HB, VM], (sg, w[3]) + tuple(kept),
        [vm((D, D))] + [vm(k.shape) for k in kept]
        + [vm((ROWS, 3 * D)), vm((D, 3 * D), F32), vm((D, D), F32)]
        + [DMA, DMA((8, ROWS // T_STEP)), DMA((ROWS // T_STEP,))],
        flops=4 * 10**9,
    )


def series_gradient(x, sg, back, w):
    return call(
        series_grad_kernel, "series_grad", 20, [shape(ROW)], [VM] * 4, [VM], (x, sg, back, w),
        flops=10**9,
    )[0]


def exchange(x, axis, groups=None):
    return lax.all_to_all(
        x, axis, split_axis=0, concat_axis=0, tiled=True, axis_index_groups=groups
    )


def other_core(x):
    return lax.ppermute(x, "dp", [(i, i ^ 1) for i in range(16)])


def add_cores(parts, core):
    mine = lax.dynamic_index_in_dim(parts, core, 0, keepdims=False)
    theirs = lax.dynamic_index_in_dim(other_core(parts), core, 0, keepdims=False)
    return (mine.astype(F32) + theirs.astype(F32)).astype(BF16)


CHIPS = [[i for i in range(16) if i % 2 == c] for c in range(2)]


def reduce_grads(halves, core, beside):
    rows = exchange(halves, "mp")
    halves_first = lambda a: lax.optimization_barrier((a, halves))[0]
    other = beside(halves_first)
    rows, other = lax.optimization_barrier((rows, other))
    mine = jnp.sum(rows.astype(F32), axis=0).astype(BF16)
    every = exchange(jnp.broadcast_to(mine[None], (8,) + mine.shape), "dp", CHIPS)
    total = jnp.sum(every.astype(F32), axis=0).astype(BF16)
    theirs = other_core(total)
    low = jnp.where(core == 0, total, theirs)
    high = jnp.where(core == 0, theirs, total)
    return jnp.concatenate([low, high], axis=1).astype(F32) * (1.0 / 16), other


def shards(series, upstream_grad, time_weights, channel_weights, neighbors):
    core = lax.axis_index("dp") & 1
    x = series.reshape(ROWS, D)
    up = upstream_grad.reshape(ROWS, D)
    stream = exchange(time_forward(x, time_weights), "mp").reshape(ROWS, D)
    sg, back, mixed = channel(neighbors, stream, up, channel_weights)
    x, sg = lax.optimization_barrier((x, sg))
    returned = exchange(sg.reshape(16, CH, D), "mp")
    out, channel_parts = channel_grads(stream, up, back, mixed, channel_weights)
    channel_half = add_cores(channel_parts, core)
    kept = prepare(x, time_weights)
    returned, channel_half, kept = lax.optimization_barrier((returned, channel_half, kept))
    time_back, time_parts = time_backward(returned, kept, time_weights)
    halves = jnp.concatenate([channel_half, add_cores(time_parts, core)], axis=1)
    sums, series_grad = reduce_grads(
        halves, core, lambda gate: series_gradient(x, returned, gate(time_back), time_weights)
    )
    return (
        out.reshape(1, ROWS, 1, D),
        series_grad.reshape(1, CH, L, D),
        sums[4:],
        sums[:4],
    )


def solution(mesh):
    placed = (P("dp", "mp", None, None), P("dp", None, "mp", None), P(), P(), P())
    return jax.shard_map(
        shards,
        mesh=mesh,
        in_specs=placed,
        out_specs=(
            P("dp", None, "mp", None),
            P("dp", "mp", None, None),
            P(None, "mp", None),
            P(None, "mp", None),
        ),
        check_vma=False,
    )
```

time: 206 us -> 152 us (0.74)
  waiting for transfers between devices: 75.4 us -> 42.6 us
  starting transfers between devices: 44.1 us -> 28.1 us
  Pallas kernels: 68.4 us -> 53.7 us
  blocking collectives: 0 us -> 13.8 us
  local copies, waits for them, and re-layouts: 14.9 us -> 10.6 us
    all_to_all x6 -> x3, waiting for transfers between devices: 75.4 us -> 40.2 us  [exchange(): lax.all_to_all(x, axis, split_axis=0, concat_axis=0, tiled=True, axis_ind...]
    all_to_all x6 -> x3, starting transfers between devices: 44.1 us -> 20.3 us  [exchange(): lax.all_to_all(x, axis, split_axis=0, concat_axis=0, tiled=True, axis_ind...]
    pallas_call x4 -> x6, Pallas kernels: 68.4 us -> 53.7 us  [call(): pl.pallas_call(kernel, out_shape=[pltpu.HBM(o.shape, o.dtype) if spec is...]
    all_to_all x0 -> x1, blocking collectives: none -> 13.8 us  [exchange(): lax.all_to_all(x, axis, split_axis=0, concat_axis=0, tiled=True, axis_ind...]
    ppermute x0 -> x3, starting transfers between devices: none -> 7.78 us  [other_core(): return lax.ppermute(x, 'dp', [(i, i ^ 1) for i in range(16)])]
    unnamed x31 -> x19, local copies, waits for them, and re-layouts: 13.2 us -> 8.4 us
    ppermute x0 -> x3, waiting for transfers between devices: none -> 2.4 us  [other_core(): return lax.ppermute(x, 'dp', [(i, i ^ 1) for i in range(16)])]
  transfers between devices with their start and end apart: 6 -> 6, of which waited for: 5 -> 5; matrix products, arithmetic and copies ran while one was open for 0% -> 2% of each run, Pallas kernels for 12% -> 8%
where the time goes in v2:
time: 152 us
  Pallas kernels  53.7 us (35%)
  waiting for transfers between devices  42.6 us (28%)
  starting transfers between devices  28.1 us (18%)
  blocking collectives  13.8 us (9%)
  local copies, waits for them, and re-layouts  10.6 us (7%)
  other arithmetic  2.1 us (1%)
    pallas_call x6, Pallas kernels, call(): pl.pallas_call(kernel, out_shape=[pltpu.HBM(o.shape, o.dtype) if spec is...  53.7 us
    all_to_all x3, waiting for transfers between devices, exchange(): lax.all_to_all(x, axis, split_axis=0, concat_axis=0, tiled=True, axis_ind...  40.2 us
    all_to_all x3, starting transfers between devices, exchange(): lax.all_to_all(x, axis, split_axis=0, concat_axis=0, tiled=True, axis_ind...  20.3 us
    all_to_all x1, blocking collectives, exchange(): lax.all_to_all(x, axis, split_axis=0, concat_axis=0, tiled=True, axis_ind...  13.8 us
    unnamed x19, local copies, waits for them, and re-layouts  8.4 us
    ppermute x3, starting transfers between devices, other_core(): return lax.ppermute(x, 'dp', [(i, i ^ 1) for i in range(16)])  7.78 us
  transfers between devices with their start and end apart: 6, of which 5 were waited for; matrix products, arithmetic and copies ran while one was open for 2% of the time, Pallas kernels for 8%

profile of v2, /device:TPU:1, one launch (start us, length us, event | category | flops | bytes accessed | tf_op | source)
XLA Modules:
  0.0 151.7 jit_solution(4913263310119254897)
XLA Ops:
  0.6 0.0 copy-start.8
  0.6 7.2 %time_forward.1 = bf16[16,128,256]{2,1,0:T(8,128)(2,1)} custom-call(bf16[2048,256]{1,0:T(8,128)(2,1)} %bitcast.14, bf16[4,256,256]{2,1,0:T(8,128)(2,1)} %w_ref.5), custom_call_target="tpu_custom_call" | custom-call | flops 2000000000 | bytes 8388608 | tf_op jit(solution)/shard_map/time_forward/pallas_call | solution.py:468
  7.8 10.1 %all-to-all-start = ((bf16[16,128,256]{2,1,0:T(8,128)(2,1)}), bf16[16,128,256]{2,1,0:T(8,128)(2,1)S(1)}, u32[]{:S(2)}, u32[]{:S(2)}) async-start(bf16[16,128,256]{2,1,0:T(8,128)(2,1)} %time_forward.1), calls=%async_computation | async-start | bytes 2097152 | tf_op jit(solution)/shard_map/all_to_all | solution.py:540
  18.0 0.0 copy-done.8
  18.0 0.1 copy.10.nb_ref
  18.1 25.6 %all-to-all-done = bf16[16,128,256]{2,1,0:T(8,128)(2,1)S(1)} async-done(((bf16[16,128,256]{2,1,0:T(8,128)(2,1)}), bf16[16,128,256]{2,1,0:T(8,128)(2,1)S(1)}, u32[]{:S(2)}, u32[]{:S(2)}) %all-to-all-start) | async-done | bytes 1048608 | tf_op jit(solution)/shard_map/all_to_all | solution.py:540
  43.7 21.8 %channel.1 = (bf16[2048,256]{1,0:T(8,128)(2,1)}, bf16[2048,768]{1,0:T(8,128)(2,1)}, bf16[2048,256]{1,0:T(8,128)(2,1)}) custom-call(s32[16,3]{1,0:T(8,128)S(1)} %copy.10.nb_ref, bf16[2048,256]{1,0:T(8,128)(2,1)S(1)} %bitcast.12, bf16[2048,256]{1,0:T(8,128)(2,1)} %bitcast.17, bf16[4,256,256]{2,1,0:T(8,128)(2,1)} %w_ref.3), custom_call_target="tpu_custom_call" | custom-call | flops 8000000000 | bytes 8388608 | tf_op jit(solution)/shard_map/channel/pallas_call | solution.py:468
  65.5 6.0 %all-to-all-start.1 = ((bf16[16,128,256]{2,1,0:T(8,128)(2,1)}), bf16[16,128,256]{2,1,0:T(8,128)(2,1)S(1)}, u32[]{:S(2)}, u32[]{:S(2)}) async-start(bf16[16,128,256]{2,1,0:T(8,128)(2,1)} %bitcast.19), calls=%async_computation.1 | async-start | bytes 2097152 | tf_op jit(solution)/shard_map/all_to_all | solution.py:540
  71.4 0.0 copy-start.4
  71.4 1.2 copy-done.4
  72.7 0.0 copy-start.5
  72.7 1.0 copy-done.5
  73.7 0.0 copy-start.6
  73.7 1.9 %copy-done.6 = bf16[2048,768]{1,0:T(8,128)(2,1)S(1)} copy-done((bf16[2048,768]{1,0:T(8,128)(2,1)S(1)}, bf16[2048,768]{1,0:T(8,128)(2,1)}, u32[]{:S(2)}) %copy-start.6) | copy-done | bytes 3145752
  75.6 0.0 copy-start.7
  75.6 1.2 copy-done.7
  76.8 0.0 copy-start.1
  76.8 3.6 %channel_grads.1 = (bf16[2048,256]{1,0:T(8,128)(2,1)}, bf16[2,16,4,8,256]{4,3,2,1,0:T(8,128)(2,1)}) custom-call(bf16[2048,256]{1,0:T(8,128)(2,1)S(1)} %bitcast.13, bf16[2048,256]{1,0:T(8,128)(2,1)S(1)} %bitcast.18, bf16[2048,768]{1,0:T(8,128)(2,1)S(1)} %copy-done.6, bf16[2048,256]{1,0:T(8,128)(2,1)S(1)} %copy-done.7, bf16[4,256,256]{2,1,0:T(8,128)(2,1)S(1)} %copy-done.5), custom_call_target="tpu_custom_call" | custom-call | flops 2000000000 | bytes 8388608 | tf_op jit(solution)/shard_map/channel_grads/pallas_call | solution.py:468
  80.4 0.8 collective-permute-start
  81.2 1.6 %slice_bitcast_fusion.w_hbm = bf16[256,256]{1,0:T(8,128)(2,1)} fusion(bf16[4,256,256]{2,1,0:T(8,128)(2,1)} %w_ref.5), kind=kLoop, calls=%fused_computation.6 | loop fusion | bytes 262144 | tf_op jit(solution)/shard_map/squeeze | solution.py:524
  82.8 0.0 copy-done.1
  82.8 0.0 copy-start.2
  82.8 1.0 copy-done.2
  83.8 5.9 %prepare.1 = (bf16[2048,256]{1,0:T(8,128)(2,1)}, bf16[2048,256]{1,0:T(8,128)(2,1)}, bf16[2048,256]{1,0:T(8,128)(2,1)}, bf16[2048,256]{1,0:T(8,128)(2,1)}, bf16[2...) custom-call(bf16[2048,256]{1,0:T(8,128)(2,1)S(1)} %bitcast.15, ...), custom_call_target="tpu_custom_call" | custom-call | flops 3000000000 | bytes 8388608 | tf_op jit(solution)/shard_map/prepare/pallas_call | solution.py:468
  89.7 0.0 collective-permute-done
  89.7 1.0 fusion
  90.8 6.1 %all-to-all-done.1.sg_ref = bf16[16,128,256]{2,1,0:T(8,128)(2,1)S(1)} async-done(((bf16[16,128,256]{2,1,0:T(8,128)(2,1)}), bf16[16,128,256]{2,1,0:T(8,128)(2,1)S(1)}, u32[]{:S(2)}, u32[]{:S(2)}) %all-to-all-start.1) | async-done | bytes 1048608 | tf_op jit(solution)/shard_map/all_to_all | solution.py:540
  96.9 12.1 %time_backward.1 = (bf16[2048,768]{1,0:T(8,128)(2,1)}, bf16[2,16,4,8,256]{4,3,2,1,0:T(8,128)(2,1)S(1)}) custom-call(bf16[16,128,256]{2,1,0:T(8,128)(2,1)S(1)} %all-to-all-done.1.sg_ref, bf16[256,256]{1,0:T(8,128)(2,1)} %slice_bitcast_fusion.w_hbm, bf16[2048,256]{1,0:T(8,128)(2,1)} %get-tuple-element.51.refs_0_, bf16[2048,256]{1,0:T(8,128)(2,1)} %get-tuple-element.52.refs_1_, ...), custom_call_target="tpu_custom_call" | custom-call | flops 4000000000 | bytes 8388608 | tf_op jit(solution)/shard_map/time_backward/pallas_call | solution.py:468
  109.0 0.0 copy-start.3
  109.0 2.7 %collective-permute-start.1 = (bf16[2,16,4,8,256]{4,3,2,1,0:T(8,128)(2,1)S(1)}, bf16[2,16,4,8,256]{4,3,2,1,0:T(8,128)(2,1)S(1)}, u32[]{:S(2)}, u32[]{:S(2)}) collective-permute-start(bf16[2,16,4,8,256]{4,3,2,1,0:T(8,128)(2,1)S(1)} %get-tuple-element.59), channel_id=1, source_target_pairs={{0,16},{16,0},{32,48},{48,32},{64,80},{80,64},{96,112},{112,96},{1... | collective-permute-start | bytes 1572872 | tf_op jit(solution)/shard_map/ppermute | solution.py:546
  111.7 1.5 %collective-permute-done.1 = bf16[2,16,4,8,256]{4,3,2,1,0:T(8,128)(2,1)S(1)} collective-permute-done((bf16[2,16,4,8,256]{4,3,2,1,0:T(8,128)(2,1)S(1)}, bf16[2,16,4,8,256]{4,3,2,1,0:T(8,128)(2,1)S(1)}, u32[]{:S(2)}, u32[]{:S(2)}) %collective-permute-start.1) | collective-permute-done | bytes 524320 | tf_op jit(solution)/shard_map/ppermute | solution.py:546
  113.2 0.1 fusion.1
  113.3 0.8 pad_maximum_fusion
  114.1 4.2 %all-to-all-start.2 = ((bf16[16,8,8,256]{3,2,1,0:T(8,128)(2,1)}), bf16[16,8,8,256]{3,2,1,0:T(8,128)(2,1)S(1)}, u32[]{:S(2)}, u32[]{:S(2)}) async-start(bf16[16,8,8,256]{3,2,1,0:T(8,128)(2,1)} %pad_maximum_fusion), calls=%async_computation.2 | async-start | bytes 1048576 | tf_op jit(solution)/shard_map/all_to_all | solution.py:540
  118.3 0.0 copy-done.3
  118.3 0.0 copy-start
  118.3 1.9 %copy-done = bf16[2048,768]{1,0:T(8,128)(2,1)S(1)} copy-done((bf16[2048,768]{1,0:T(8,128)(2,1)S(1)}, bf16[2048,768]{1,0:T(8,128)(2,1)}, u32[]{:S(2)}) %copy-start) | copy-done | bytes 3145752
  120.2 3.2 %series_grad.1 = bf16[2048,256]{1,0:T(8,128)(2,1)} custom-call(bf16[2048,256]{1,0:T(8,128)(2,1)S(1)} %bitcast.16, bf16[16,128,256]{2,1,0:T(8,128)(2,1)S(1)} %all-to-all-done.1.sg_ref, bf16[2048,768]{1,0:T(8,128)(2,1)S(1)} %copy-done, bf16[4,256,256]{2,1,0:T(8,128)(2,1)S(1)} %copy-done.3), custom_call_target="tpu_custom_call" | custom-call | flops 1000000000 | bytes 8388608 | tf_op jit(solution)/shard_map/series_grad/pallas_call | solution.py:468
  123.4 8.5 %all-to-all-done.2 = bf16[16,8,8,256]{3,2,1,0:T(8,128)(2,1)S(1)} async-done(((bf16[16,8,8,256]{3,2,1,0:T(8,128)(2,1)}), bf16[16,8,8,256]{3,2,1,0:T(8,128)(2,1)S(1)}, u32[]{:S(2)}, u32[]{:S(2)}) %all-to-all-start.2) | async-done | bytes 524320 | tf_op jit(solution)/shard_map/all_to_all | solution.py:540
  131.9 0.1 reduce_sum.24
  132.0 13.8 %all_to_all.20 = bf16[8,8,8,256]{3,2,1,0:T(8,128)(2,1)S(1)} all-to-all(bf16[8,8,8,256]{3,2,1,0:T(8,128)(2,1)S(1)} %broadcast_in_dim.2), channel_id=1, replica_groups={{0,32,64,96,128,160,192,224},{16,48,80,112,144,176,208,240},{1,33,65,97..., dimensions={0} | all-to-all | bytes 524288 | tf_op jit(solution)/shard_map/all_to_all | solution.py:540
  145.8 4.3 %collective-permute-start.2 = (bf16[8,8,256]{2,1,0:T(8,128)(2,1)S(1)}, bf16[8,8,256]{2,1,0:T(8,128)(2,1)S(1)}, u32[]{:S(2)}, u32[]{:S(2)}) collective-permute-start(bf16[8,8,256]{2,1,0:T(8,128)(2,1)S(1)} %reduce_sum.25), channel_id=1, source_target_pairs={{0,16},{16,0},{32,48},{48,32},{64,80},{80,64},{96,112},{112,96},{1... | collective-permute-start | bytes 98312 | tf_op jit(solution)/shard_map/ppermute | solution.py:546
  150.2 0.9 collective-permute-done.2
  151.1 0.7 fusion.2
  (4 shorter events, 0.1 us)
Async XLA Ops:
  0.6 17.4 %copy-start.8 = (s32[16,3]{0,1:T(4,128)S(1)}, s32[16,3]{0,1:T(4,128)}, u32[]{:S(2)}) copy-start(s32[16,3]{0,1:T(4,128)} %param.9) | copy-start | bytes 580
  7.8 35.8 %all-to-all-start = ((bf16[16,128,256]{2,1,0:T(8,128)(2,1)}), bf16[16,128,256]{2,1,0:T(8,128)(2,1)S(1)}, u32[]{:S(2)}, u32[]{:S(2)}) async-start(bf16[16,128,256]{2,1,0:T(8,128)(2,1)} %time_forward.1), calls=%async_computation | async-start | bytes 2097152 | tf_op jit(solution)/shard_map/all_to_all | solution.py:540
  65.5 31.5 %all-to-all-start.1 = ((bf16[16,128,256]{2,1,0:T(8,128)(2,1)}), bf16[16,128,256]{2,1,0:T(8,128)(2,1)S(1)}, u32[]{:S(2)}, u32[]{:S(2)}) async-start(bf16[16,128,256]{2,1,0:T(8,128)(2,1)} %bitcast.19), calls=%async_computation.1 | async-start | bytes 2097152 | tf_op jit(solution)/shard_map/all_to_all | solution.py:540
  71.4 1.2 copy-start.4
  72.7 1.0 copy-start.5
  73.7 1.9 %copy-start.6 = (bf16[2048,768]{1,0:T(8,128)(2,1)S(1)}, bf16[2048,768]{1,0:T(8,128)(2,1)}, u32[]{:S(2)}) copy-start(bf16[2048,768]{1,0:T(8,128)(2,1)} %get-tuple-element.34.back_ref) | copy-start | bytes 9437188
  75.6 1.2 copy-start.7
  76.8 5.9 %copy-start.1 = (bf16[1,128,16,256]{3,2,1,0:T(8,128)(2,1)S(1)}, bf16[1,128,16,256]{3,2,1,0:T(8,128)(2,1)}, u32[]{:S(2)}) copy-start(bf16[1,128,16,256]{3,2,1,0:T(8,128)(2,1)} %param.5) | copy-start | bytes 3145732
  80.4 9.3 %collective-permute-start = (bf16[2,16,4,8,256]{4,3,2,1,0:T(8,128)(2,1)}, bf16[2,16,4,8,256]{4,3,2,1,0:T(8,128)(2,1)S(1)}, u32[]{:S(2)}, u32[]{:S(2)}) collective-permute-start(bf16[2,16,4,8,256]{4,3,2,1,0:T(8,128)(2,1)} %get-tuple-element.39), channel_id=1, source_target_pairs={{0,16},{16,0},{32,48},{48,32},{64,80},{80,64},{96,112},{112,96},{1... | collective-permute-start | bytes 1572872 | tf_op jit(solution)/shard_map/ppermute | solution.py:546
  82.8 1.0 copy-start.2
  109.0 9.3 %copy-start.3 = (bf16[4,256,256]{2,1,0:T(8,128)(2,1)S(1)}, bf16[4,256,256]{2,1,0:T(8,128)(2,1)}, u32[]{:S(2)}) copy-start(bf16[4,256,256]{2,1,0:T(8,128)(2,1)} %w_ref.5) | copy-start | bytes 1572868
  109.0 4.2 %collective-permute-start.1 = (bf16[2,16,4,8,256]{4,3,2,1,0:T(8,128)(2,1)S(1)}, bf16[2,16,4,8,256]{4,3,2,1,0:T(8,128)(2,1)S(1)}, u32[]{:S(2)}, u32[]{:S(2)}) collective-permute-start(bf16[2,16,4,8,256]{4,3,2,1,0:T(8,128)(2,1)S(1)} %get-tuple-element.59), channel_id=1, source_target_pairs={{0,16},{16,0},{32,48},{48,32},{64,80},{80,64},{96,112},{112,96},{1... | collective-permute-start | bytes 1572872 | tf_op jit(solution)/shard_map/ppermute | solution.py:546
  114.1 17.8 %all-to-all-start.2 = ((bf16[16,8,8,256]{3,2,1,0:T(8,128)(2,1)}), bf16[16,8,8,256]{3,2,1,0:T(8,128)(2,1)S(1)}, u32[]{:S(2)}, u32[]{:S(2)}) async-start(bf16[16,8,8,256]{3,2,1,0:T(8,128)(2,1)} %pad_maximum_fusion), calls=%async_computation.2 | async-start | bytes 1048576 | tf_op jit(solution)/shard_map/all_to_all | solution.py:540
  118.3 1.9 %copy-start = (bf16[2048,768]{1,0:T(8,128)(2,1)S(1)}, bf16[2048,768]{1,0:T(8,128)(2,1)}, u32[]{:S(2)}) copy-start(bf16[2048,768]{1,0:T(8,128)(2,1)} %get-tuple-element.61.back_ref) | copy-start | bytes 9437188
  145.8 5.2 %collective-permute-start.2 = (bf16[8,8,256]{2,1,0:T(8,128)(2,1)S(1)}, bf16[8,8,256]{2,1,0:T(8,128)(2,1)S(1)}, u32[]{:S(2)}, u32[]{:S(2)}) collective-permute-start(bf16[8,8,256]{2,1,0:T(8,128)(2,1)S(1)} %reduce_sum.25), channel_id=1, source_target_pairs={{0,16},{16,0},{32,48},{48,32},{64,80},{80,64},{96,112},{112,96},{1... | collective-permute-start | bytes 98312 | tf_op jit(solution)/shard_map/ppermute | solution.py:546

commit v3 on v2

--- a/solution.py
+++ b/solution.py
@@ -14,7 +14,7 @@
 NBR = 3
 ROWS = 2048
 SQ = 256
-GROUPS = 2
+GROUPS = 4
 EPS = 1e-06
 LOG2E = 1.4426950408889634
 LN2 = 0.6931471805599453
@@ -144,7 +144,7 @@
         step = []
         for n, (src, dst) in enumerate(zip(srcs, dsts)):
             rows = size // BLK if len(src.shape) == 3 else size
-            at = pl.ds(i * rows, rows)
+            at = (slice(None), pl.ds(i * rows, rows)) if src.shape[0] == D else pl.ds(i * rows, rows)
             step.append(pltpu.make_async_copy(src.at[at], dst.at[at], sems.at[n, i]))
         out.append(step)
     return out
@@ -163,9 +163,6 @@
     means, swap = head_mean_matrix(), swap_matrix()
     masks = head_masks(BLK)
     diag = time_diag()
-    ones = jnp.where(
-        div(iota((HEADS * BLK, D), 0), BLK) == div(iota((HEADS * BLK, D), 1), HD), 1.0, 0.0
-    ).astype(BF16)
     chans = A_STEP // L
     outs = []
     for i in range(ROWS // A_STEP):
@@ -178,12 +175,11 @@
         xn = (x * rms_scale(x)).astype(BF16)
         qs, kn, v, _, _ = project(xn, wqkv, means)
         es = [
-            (jnp.exp2(dot_rt(q, stack_heads(k, masks))) * diag).astype(BF16)
+            jnp.exp2(dot_rt(k, stack_heads(q, masks))) * diag
             for q, k in zip(split(qs), split(kn))
         ]
-        dens = [dot(e, ones) for e in es]
-        os = [dot(e, stack_heads(u, masks)) for e, u in zip(es, split(v))]
-        mixed = join([(o * (1.0 / den)).astype(BF16) for o, den in zip(os, dens)])
+        pbs = [p.astype(BF16) for p in softmax_columns(es)]
+        mixed = join(stack_product([u.T for u in split(v)], pbs)).astype(BF16)
         stream = (x + dot(mixed, wo)).astype(BF16)
         for j, part in enumerate(split(stream, SQ)):
             at = i * chans + j * L
@@ -199,22 +195,22 @@
 PREP_STEP = 512
 
 
-def prepare_kernel(x_ref, w_ref, *refs):
-    outs, (xn_ref, qs_ref, kn_ref, v_ref, rq_ref, rk_ref, p_ref, mixed_ref), sems = (
-        refs[:8], refs[8:16], refs[16],
+def prepare_kernel(x_ref, w_ref, v_ref, *refs):
+    outs, (xt_ref, p_ref, qs_ref, kn_ref, rq_ref, rk_ref, mt_ref), sems = (
+        refs[:7], refs[7:14], refs[14],
     )
     means = head_mean_matrix()
     masks = head_masks(BLK)
     diag = time_diag()
     wqkv = load_wqkv(w_ref)
     groups = PREP_STEP // BLK
-    moves = kept_copies(refs[8:16], outs, sems, PREP_STEP)
+    moves = kept_copies(refs[7:14], outs, sems, PREP_STEP)
     for i in range(ROWS // PREP_STEP):
         at = slice(i * PREP_STEP, (i + 1) * PREP_STEP)
         x = x_ref[at, :].astype(F32)
         xn = (x * rms_scale(x)).astype(BF16)
         qs, kn, v, rq, rk = project(xn, wqkv, means)
-        xn_ref[at, :] = xn
+        xt_ref[:, at] = xn.T
         qs_ref[at, :] = qs
         kn_ref[at, :] = kn
         v_ref[at, :] = v
@@ -227,7 +223,7 @@
         pbs = [p.astype(BF16) for p in softmax_columns(es)]
         p_ref[i * groups : (i + 1) * groups] = jnp.stack(pbs)
         os = stack_product([u.T for u in split(v)], pbs)
-        mixed_ref[at, :] = join(os).astype(BF16)
+        mt_ref[:, at] = join(os).astype(BF16).T
         for c in moves[i]:
             c.start()
     for step in moves:
@@ -261,20 +257,19 @@
             grads_ref[half, :, j] = whole[:, half].astype(BF16)
 
 
-T_STEP = 512
-
-
-def time_backward_kernel(sg_ref, w_hbm, *refs):
-    kept_hbm, back_hbm, grads_ref = refs[:8], refs[8], refs[9]
-    w_ref, kept, back_ref, acc, acc_o = refs[10], refs[11:19], refs[19], refs[20], refs[21]
-    w_sem, in_sem, out_sem = refs[22:]
-    xn_ref, qs_ref, kn_ref, v_ref, rq_ref, rk_ref, p_ref, mixed_ref = kept
+T_STEP = 1024
+
+
+def time_backward_kernel(sg_ref, w_hbm, v_ref, *refs):
+    kept_hbm, back_hbm, grads_ref = refs[:7], refs[7], refs[8]
+    w_ref, kept, back_ref, acc, acc_o = refs[9], refs[10:17], refs[17], refs[18], refs[19]
+    w_sem, in_sem, out_sem = refs[20:]
+    xt_ref, p_ref, qs_ref, kn_ref, rq_ref, rk_ref, mt_ref = kept
     w_in = pltpu.make_async_copy(w_hbm, w_ref, w_sem)
     w_in.start()
     moves = kept_copies(kept_hbm, kept, in_sem, T_STEP)
-    for step in moves:
-        for c in step:
-            c.start()
+    for c in moves[0]:
+        c.start()
     back_out = copies(back_ref, back_hbm, out_sem, T_STEP)
     means, swap = head_mean_matrix(), swap_matrix()
     masks = head_masks(BLK)
@@ -291,6 +286,8 @@
         do = dot_rt(sg, wo).astype(BF16)
         for c in moves[i]:
             c.wait()
+        for c in moves[i + 1] if i + 1 < len(moves) else []:
+            c.start()
         qs, kn = qs_ref[at, :], kn_ref[at, :]
         pbs = [p_ref[i * groups + g] for g in range(groups)]
         dosts = [stack_heads(d, masks) for d in split(do)]
@@ -304,7 +301,7 @@
         back = jnp.concatenate([qb, kb, vb], axis=1)
         back_ref[at, :] = back
         back_out[i].start()
-        part, part_o = dot_lt(xn_ref[at, :], back), dot_lt(mixed_ref[at, :], sg)
+        part, part_o = dot(xt_ref[:, at], back), dot(mt_ref[:, at], sg)
         acc[...] = part if i == 0 else acc[...] + part
         acc_o[...] = part_o if i == 0 else acc_o[...] + part_o
     write_grads(grads_ref, acc, acc_o)
@@ -332,12 +329,12 @@
     loop(S_STEP, body)
 
 
-C_STEP = 512
+C_STEP = 1024
 
 
 def channel_kernel(
     nb_ref, x_ref, up_hbm, w_hbm, sg_hbm, back_hbm, mixed_hbm,
-    up_ref, w_ref, do_ref, up_sem, w_sem, sg_s, back_s, mixed_s, qs_s, kn_s, v_s, kt_s, vt_s, rq_s, rk_s, dq_s, dk_s, dv_s,
+    up_ref, w_ref, up_sem, w_sem, sg_s, back_s, mixed_s, qs_s, kn_s, v_s, kt_s, vt_s, rq_s, rk_s, dq_s, dk_s, dv_s,
     sg_sem, back_sem, mixed_sem,
 ):
     w_in = pltpu.make_async_copy(w_hbm, w_ref, w_sem)
@@ -349,13 +346,13 @@
     w_in.wait()
     wqkv = load_wqkv(w_ref)
     wo = w_ref[3]
-    up_in.wait()
 
     def first(i, at):
-        do_ref[at, :] = dot_rt(up_ref[at, :], wo).astype(BF16)
         x = x_ref[at, :].astype(F32)
         xn = (x * rms_scale(x)).astype(BF16)
-        qs, kn, v, rq_s[at, :], rk_s[at, :] = project(xn, wqkv, means)
+        qs, kn, v, rq, rk = project(xn, wqkv, means)
+        rq_s[at, :] = rq.astype(BF16)
+        rk_s[at, :] = rk.astype(BF16)
         qs_s[at, :] = qs
         kn_s[at, :] = kn
         v_s[at, :] = v
@@ -365,6 +362,9 @@
         dv_s[at, :] = jnp.zeros((C_STEP, D), F32)
 
     loop(C_STEP, first)
+    up_in.wait()
+
+    span = GROUPS * BLK
 
     def attend(i, carry):
         bs = [i * GROUPS + g for g in range(GROUPS)]
@@ -377,7 +377,8 @@
             jnp.exp2(dot_rt(join([kn_s[n, :] for n in near]), q))
             for near, q in zip(nears, qsts)
         ]
-        dosts = [stack_heads(do_ref[at, :], masks) for at in ats]
+        do = dot_rt(up_ref[pl.ds(pl.multiple_of(i * span, span), span), :], wo).astype(BF16)
+        dosts = [stack_heads(d, masks) for d in split(do)]
         dps = [dot_rt(join([v_s[n, :] for n in near]), d) for near, d in zip(nears, dosts)]
         ps = softmax_columns(es)
         pbs = [p.astype(BF16) for p in ps]
@@ -409,8 +410,8 @@
         at = slice(i * C_STEP, (i + 1) * C_STEP)
         x = x_ref[at, :].astype(F32)
         r = rms_scale(x)
-        qb = query_back(rq_s[at, :] * 0.25, qs_s[at, :], dq_s[at, :], means)
-        kb = key_back(rk_s[at, :], kn_s[at, :], dk_s[at, :], means)
+        qb = query_back(rq_s[at, :].astype(F32) * 0.25, qs_s[at, :], dq_s[at, :], means)
+        kb = key_back(rk_s[at, :].astype(F32), kn_s[at, :], dk_s[at, :], means)
         back = jnp.concatenate([qb, kb, dv_s[at, :].astype(BF16)], axis=1)
         back_s[at, :] = back
         back_out[i].start()
@@ -458,6 +459,7 @@
 
 ROW = (ROWS, D)
 GRADS = (2, 16, 4, 8, D)
+SCORES = (ROWS // BLK, BLK, HEADS * BLK)
 
 
 def call(kernel, name, mib, outs, ins, out_specs, args, scratch=(), flops=0):
@@ -490,22 +492,22 @@
 
 
 def prepare(x, w):
-    names = [shape(ROW)] * 6 + [shape((ROWS // BLK, BLK, HEADS * BLK)), shape(ROW)]
+    names = [shape(ROW), shape((D, ROWS)), shape(SCORES)] + [shape(ROW)] * 4 + [shape((D, ROWS))]
     return call(
-        prepare_kernel, "prepare", 28, names, [VM] * 2, [HB] * 8, (x, w),
-        [vm(o.shape) for o in names] + [DMA((8, ROWS // PREP_STEP))],
+        prepare_kernel, "prepare", 28, names, [VM] * 2, [VM] + [HB] * 7, (x, w),
+        [vm(o.shape) for o in names[1:]] + [DMA((7, ROWS // PREP_STEP))],
         flops=3 * 10**9,
     )
 
 
 def channel(nb, x, up, w):
     return call(
-        channel_kernel, "channel", 36,
+        channel_kernel, "channel", 48,
         [shape(ROW), shape((ROWS, 3 * D)), shape(ROW)],
         [SM, VM, HB, HB], [HB] * 3, (nb, x, up, w),
-        [vm(ROW), vm((4, D, D)), vm(ROW), DMA, DMA]
+        [vm(ROW), vm((4, D, D)), DMA, DMA]
         + [vm(ROW), vm((ROWS, 3 * D)), vm(ROW), vm(ROW), vm(ROW), vm(ROW)]
-        + [vm((D, ROWS))] * 2 + [vm(ROW, F32)] * 5 + [DMA((4,)), DMA((4,)), DMA],
+        + [vm((D, ROWS))] * 2 + [vm(ROW)] * 2 + [vm(ROW, F32)] * 3 + [DMA((2,)), DMA((2,)), DMA],
         flops=8 * 10**9,
     )
 
@@ -521,10 +523,10 @@
 def time_backward(sg, kept, w):
     return call(
         time_backward_kernel, "time_backward", 30, [shape((ROWS, 3 * D)), shape(GRADS)],
-        [VM] + [HB] * 9, [HB, VM], (sg, w[3]) + tuple(kept),
-        [vm((D, D))] + [vm(k.shape) for k in kept]
+        [VM, HB, VM] + [HB] * 7, [HB, VM], (sg, w[3]) + tuple(kept),
+        [vm((D, D))] + [vm(k.shape) for k in kept[1:]]
         + [vm((ROWS, 3 * D)), vm((D, 3 * D), F32), vm((D, D), F32)]
-        + [DMA, DMA((8, ROWS // T_STEP)), DMA((ROWS // T_STEP,))],
+        + [DMA, DMA((7, ROWS // T_STEP)), DMA((ROWS // T_STEP,))],
         flops=4 * 10**9,
     )
 

time: 152 us -> 148 us (0.974)
  Pallas kernels: 53.7 us -> 49.2 us
    pallas_call x6, Pallas kernels: 53.7 us -> 49.2 us  [call(): pl.pallas_call(kernel, out_shape=[pltpu.HBM(o.shape, o.dtype) if spec is...]
  transfers between devices with their start and end apart: 6 -> 6, of which waited for: 5 -> 5; matrix products, arithmetic and copies ran while one was open for 2% -> 2% of each run, Pallas kernels for 8% -> 9%
where the time goes in v3:
time: 148 us; the launch traced here: 147 us
  Pallas kernels  49.2 us (33%)
  waiting for transfers between devices  42.5 us (29%)
  starting transfers between devices  28.2 us (19%)
  blocking collectives  13.8 us (9%)
  local copies, waits for them, and re-layouts  10.6 us (7%)
  other arithmetic  2.18 us (1%)
    pallas_call x6, Pallas kernels, call(): pl.pallas_call(kernel, out_shape=[pltpu.HBM(o.shape, o.dtype) if spec is...  49.2 us
    all_to_all x3, waiting for transfers between devices, exchange(): lax.all_to_all(x, axis, split_axis=0, concat_axis=0, tiled=True, axis_ind...  40.1 us
    all_to_all x3, starting transfers between devices, exchange(): lax.all_to_all(x, axis, split_axis=0, concat_axis=0, tiled=True, axis_ind...  20.5 us
    all_to_all x1, blocking collectives, exchange(): lax.all_to_all(x, axis, split_axis=0, concat_axis=0, tiled=True, axis_ind...  13.8 us
    unnamed x19, local copies, waits for them, and re-layouts  8.4 us
    ppermute x3, starting transfers between devices, other_core(): return lax.ppermute(x, 'dp', [(i, i ^ 1) for i in range(16)])  7.78 us
  transfers between devices with their start and end apart: 6, of which 5 were waited for; matrix products, arithmetic and copies ran while one was open for 2% of the time, Pallas kernels for 9%

profile of v3, /device:TPU:1, one launch (start us, length us, event | category | flops | bytes accessed | tf_op | source)
XLA Modules:
  0.0 147.4 jit_solution(16255932662799058945)
XLA Ops:
  0.6 0.0 copy-start.8
  0.6 6.6 %time_forward.1 = bf16[16,128,256]{2,1,0:T(8,128)(2,1)} custom-call(bf16[2048,256]{1,0:T(8,128)(2,1)} %bitcast.14, bf16[4,256,256]{2,1,0:T(8,128)(2,1)} %w_ref.5), custom_call_target="tpu_custom_call" | custom-call | flops 2000000000 | bytes 8388608 | tf_op jit(solution)/shard_map/time_forward/pallas_call | solution.py:470
  7.3 10.1 %all-to-all-start = ((bf16[16,128,256]{2,1,0:T(8,128)(2,1)}), bf16[16,128,256]{2,1,0:T(8,128)(2,1)S(1)}, u32[]{:S(2)}, u32[]{:S(2)}) async-start(bf16[16,128,256]{2,1,0:T(8,128)(2,1)} %time_forward.1), calls=%async_computation | async-start | bytes 2097152 | tf_op jit(solution)/shard_map/all_to_all | solution.py:542
  17.4 0.0 copy-done.8
  17.4 0.1 copy.10.nb_ref
  17.5 25.6 %all-to-all-done = bf16[16,128,256]{2,1,0:T(8,128)(2,1)S(1)} async-done(((bf16[16,128,256]{2,1,0:T(8,128)(2,1)}), bf16[16,128,256]{2,1,0:T(8,128)(2,1)S(1)}, u32[]{:S(2)}, u32[]{:S(2)}) %all-to-all-start) | async-done | bytes 1048608 | tf_op jit(solution)/shard_map/all_to_all | solution.py:542
  43.1 20.5 %channel.1 = (bf16[2048,256]{1,0:T(8,128)(2,1)}, bf16[2048,768]{1,0:T(8,128)(2,1)}, bf16[2048,256]{1,0:T(8,128)(2,1)}) custom-call(s32[16,3]{1,0:T(8,128)S(1)} %copy.10.nb_ref, bf16[2048,256]{1,0:T(8,128)(2,1)S(1)} %bitcast.12, bf16[2048,256]{1,0:T(8,128)(2,1)} %bitcast.17, bf16[4,256,256]{2,1,0:T(8,128)(2,1)} %w_ref.3), custom_call_target="tpu_custom_call" | custom-call | flops 8000000000 | bytes 8388608 | tf_op jit(solution)/shard_map/channel/pallas_call | solution.py:470
  63.6 6.2 %all-to-all-start.1 = ((bf16[16,128,256]{2,1,0:T(8,128)(2,1)}), bf16[16,128,256]{2,1,0:T(8,128)(2,1)S(1)}, u32[]{:S(2)}, u32[]{:S(2)}) async-start(bf16[16,128,256]{2,1,0:T(8,128)(2,1)} %bitcast.19), calls=%async_computation.1 | async-start | bytes 2097152 | tf_op jit(solution)/shard_map/all_to_all | solution.py:542
  69.8 0.0 copy-start.4
  69.8 1.2 copy-done.4
  71.0 0.0 copy-start.5
  71.0 1.0 copy-done.5
  72.1 0.0 copy-start.6
  72.1 1.9 %copy-done.6 = bf16[2048,768]{1,0:T(8,128)(2,1)S(1)} copy-done((bf16[2048,768]{1,0:T(8,128)(2,1)S(1)}, bf16[2048,768]{1,0:T(8,128)(2,1)}, u32[]{:S(2)}) %copy-start.6) | copy-done | bytes 3145752
  74.0 0.0 copy-start.7
  74.0 1.2 copy-done.7
  75.2 0.0 copy-start.1
  75.2 3.6 %channel_grads.1 = (bf16[2048,256]{1,0:T(8,128)(2,1)}, bf16[2,16,4,8,256]{4,3,2,1,0:T(8,128)(2,1)}) custom-call(bf16[2048,256]{1,0:T(8,128)(2,1)S(1)} %bitcast.13, bf16[2048,256]{1,0:T(8,128)(2,1)S(1)} %bitcast.18, bf16[2048,768]{1,0:T(8,128)(2,1)S(1)} %copy-done.6, bf16[2048,256]{1,0:T(8,128)(2,1)S(1)} %copy-done.7, bf16[4,256,256]{2,1,0:T(8,128)(2,1)S(1)} %copy-done.5), custom_call_target="tpu_custom_call" | custom-call | flops 2000000000 | bytes 8388608 | tf_op jit(solution)/shard_map/channel_grads/pallas_call | solution.py:470
  78.8 0.8 collective-permute-start
  79.6 1.6 %slice_bitcast_fusion.w_hbm = bf16[256,256]{1,0:T(8,128)(2,1)} fusion(bf16[4,256,256]{2,1,0:T(8,128)(2,1)} %w_ref.5), kind=kLoop, calls=%fused_computation.6 | loop fusion | bytes 262144 | tf_op jit(solution)/shard_map/squeeze | solution.py:526
  81.1 0.0 copy-done.1
  81.1 0.0 copy-start.2
  81.1 1.0 copy-done.2
  82.2 6.0 %prepare.1 = (bf16[2048,256]{1,0:T(8,128)(2,1)S(1)}, bf16[256,2048]{1,0:T(8,128)(2,1)}, bf16[16,128,512]{2,1,0:T(8,128)(2,1)}, bf16[2048,256]{1,0:T(8,128)(2,1)}...) custom-call(bf16[2048,256]{1,0:T(8,128)(2,1)S(1)} %bitcast.15, ...), custom_call_target="tpu_custom_call" | custom-call | flops 3000000000 | bytes 8388608 | tf_op jit(solution)/shard_map/prepare/pallas_call | solution.py:470
  88.1 0.0 collective-permute-done
  88.1 1.1 fusion
  89.3 6.0 %all-to-all-done.1.sg_ref = bf16[16,128,256]{2,1,0:T(8,128)(2,1)S(1)} async-done(((bf16[16,128,256]{2,1,0:T(8,128)(2,1)}), bf16[16,128,256]{2,1,0:T(8,128)(2,1)S(1)}, u32[]{:S(2)}, u32[]{:S(2)}) %all-to-all-start.1) | async-done | bytes 1048608 | tf_op jit(solution)/shard_map/all_to_all | solution.py:542
  95.3 9.4 %time_backward.1 = (bf16[2048,768]{1,0:T(8,128)(2,1)}, bf16[2,16,4,8,256]{4,3,2,1,0:T(8,128)(2,1)S(1)}) custom-call(bf16[16,128,256]{2,1,0:T(8,128)(2,1)S(1)} %all-to-all-done.1.sg_ref, bf16[256,256]{1,0:T(8,128)(2,1)} %slice_bitcast_fusion.w_hbm, bf16[2048,256]{1,0:T(8,128)(2,1)S(1)} %get-tuple-element.51.v_ref, ...), custom_call_target="tpu_custom_call" | custom-call | flops 4000000000 | bytes 8388608 | tf_op jit(solution)/shard_map/time_backward/pallas_call | solution.py:470
  104.7 0.0 copy-start.3
  104.7 2.7 %collective-permute-start.1 = (bf16[2,16,4,8,256]{4,3,2,1,0:T(8,128)(2,1)S(1)}, bf16[2,16,4,8,256]{4,3,2,1,0:T(8,128)(2,1)S(1)}, u32[]{:S(2)}, u32[]{:S(2)}) collective-permute-start(bf16[2,16,4,8,256]{4,3,2,1,0:T(8,128)(2,1)S(1)} %get-tuple-element.59), channel_id=1, source_target_pairs={{0,16},{16,0},{32,48},{48,32},{64,80},{80,64},{96,112},{112,96},{1... | collective-permute-start | bytes 1572872 | tf_op jit(solution)/shard_map/ppermute | solution.py:548
  107.3 1.5 %collective-permute-done.1 = bf16[2,16,4,8,256]{4,3,2,1,0:T(8,128)(2,1)S(1)} collective-permute-done((bf16[2,16,4,8,256]{4,3,2,1,0:T(8,128)(2,1)S(1)}, bf16[2,16,4,8,256]{4,3,2,1,0:T(8,128)(2,1)S(1)}, u32[]{:S(2)}, u32[]{:S(2)}) %collective-permute-start.1) | collective-permute-done | bytes 524320 | tf_op jit(solution)/shard_map/ppermute | solution.py:548
  108.9 0.1 fusion.1
  109.0 0.8 pad_maximum_fusion
  109.8 4.2 %all-to-all-start.2 = ((bf16[16,8,8,256]{3,2,1,0:T(8,128)(2,1)}), bf16[16,8,8,256]{3,2,1,0:T(8,128)(2,1)S(1)}, u32[]{:S(2)}, u32[]{:S(2)}) async-start(bf16[16,8,8,256]{3,2,1,0:T(8,128)(2,1)} %pad_maximum_fusion), calls=%async_computation.2 | async-start | bytes 1048576 | tf_op jit(solution)/shard_map/all_to_all | solution.py:542
  114.0 0.0 copy-done.3
  114.0 0.0 copy-start
  114.0 1.9 %copy-done = bf16[2048,768]{1,0:T(8,128)(2,1)S(1)} copy-done((bf16[2048,768]{1,0:T(8,128)(2,1)S(1)}, bf16[2048,768]{1,0:T(8,128)(2,1)}, u32[]{:S(2)}) %copy-start) | copy-done | bytes 3145752
  115.9 3.2 %series_grad.1 = bf16[2048,256]{1,0:T(8,128)(2,1)} custom-call(bf16[2048,256]{1,0:T(8,128)(2,1)S(1)} %bitcast.16, bf16[16,128,256]{2,1,0:T(8,128)(2,1)S(1)} %all-to-all-done.1.sg_ref, bf16[2048,768]{1,0:T(8,128)(2,1)S(1)} %copy-done, bf16[4,256,256]{2,1,0:T(8,128)(2,1)S(1)} %copy-done.3), custom_call_target="tpu_custom_call" | custom-call | flops 1000000000 | bytes 8388608 | tf_op jit(solution)/shard_map/series_grad/pallas_call | solution.py:470
  119.1 8.5 %all-to-all-done.2 = bf16[16,8,8,256]{3,2,1,0:T(8,128)(2,1)S(1)} async-done(((bf16[16,8,8,256]{3,2,1,0:T(8,128)(2,1)}), bf16[16,8,8,256]{3,2,1,0:T(8,128)(2,1)S(1)}, u32[]{:S(2)}, u32[]{:S(2)}) %all-to-all-start.2) | async-done | bytes 524320 | tf_op jit(solution)/shard_map/all_to_all | solution.py:542
  127.6 0.1 reduce_sum.24
  127.7 13.8 %all_to_all.20 = bf16[8,8,8,256]{3,2,1,0:T(8,128)(2,1)S(1)} all-to-all(bf16[8,8,8,256]{3,2,1,0:T(8,128)(2,1)S(1)} %broadcast_in_dim.2), channel_id=1, replica_groups={{0,32,64,96,128,160,192,224},{16,48,80,112,144,176,208,240},{1,33,65,97..., dimensions={0} | all-to-all | bytes 524288 | tf_op jit(solution)/shard_map/all_to_all | solution.py:542
  141.5 4.3 %collective-permute-start.2 = (bf16[8,8,256]{2,1,0:T(8,128)(2,1)S(1)}, bf16[8,8,256]{2,1,0:T(8,128)(2,1)S(1)}, u32[]{:S(2)}, u32[]{:S(2)}) collective-permute-start(bf16[8,8,256]{2,1,0:T(8,128)(2,1)S(1)} %reduce_sum.25), channel_id=1, source_target_pairs={{0,16},{16,0},{32,48},{48,32},{64,80},{80,64},{96,112},{112,96},{1... | collective-permute-start | bytes 98312 | tf_op jit(solution)/shard_map/ppermute | solution.py:548
  145.8 0.9 collective-permute-done.2
  146.7 0.7 fusion.2
  (4 shorter events, 0.1 us)
Async XLA Ops:
  0.6 16.8 %copy-start.8 = (s32[16,3]{0,1:T(4,128)S(1)}, s32[16,3]{0,1:T(4,128)}, u32[]{:S(2)}) copy-start(s32[16,3]{0,1:T(4,128)} %param.9) | copy-start | bytes 580
  7.3 35.8 %all-to-all-start = ((bf16[16,128,256]{2,1,0:T(8,128)(2,1)}), bf16[16,128,256]{2,1,0:T(8,128)(2,1)S(1)}, u32[]{:S(2)}, u32[]{:S(2)}) async-start(bf16[16,128,256]{2,1,0:T(8,128)(2,1)} %time_forward.1), calls=%async_computation | async-start | bytes 2097152 | tf_op jit(solution)/shard_map/all_to_all | solution.py:542
  63.6 31.6 %all-to-all-start.1 = ((bf16[16,128,256]{2,1,0:T(8,128)(2,1)}), bf16[16,128,256]{2,1,0:T(8,128)(2,1)S(1)}, u32[]{:S(2)}, u32[]{:S(2)}) async-start(bf16[16,128,256]{2,1,0:T(8,128)(2,1)} %bitcast.19), calls=%async_computation.1 | async-start | bytes 2097152 | tf_op jit(solution)/shard_map/all_to_all | solution.py:542
  69.8 1.2 copy-start.4
  71.0 1.0 copy-start.5
  72.1 1.9 %copy-start.6 = (bf16[2048,768]{1,0:T(8,128)(2,1)S(1)}, bf16[2048,768]{1,0:T(8,128)(2,1)}, u32[]{:S(2)}) copy-start(bf16[2048,768]{1,0:T(8,128)(2,1)} %get-tuple-element.34.back_ref) | copy-start | bytes 9437188
  74.0 1.2 copy-start.7
  75.2 5.9 %copy-start.1 = (bf16[1,128,16,256]{3,2,1,0:T(8,128)(2,1)S(1)}, bf16[1,128,16,256]{3,2,1,0:T(8,128)(2,1)}, u32[]{:S(2)}) copy-start(bf16[1,128,16,256]{3,2,1,0:T(8,128)(2,1)} %param.5) | copy-start | bytes 3145732
  78.8 9.4 %collective-permute-start = (bf16[2,16,4,8,256]{4,3,2,1,0:T(8,128)(2,1)}, bf16[2,16,4,8,256]{4,3,2,1,0:T(8,128)(2,1)}, u32[]{:S(2)}, u32[]{:S(2)}) collective-permute-start(bf16[2,16,4,8,256]{4,3,2,1,0:T(8,128)(2,1)} %get-tuple-element.39), channel_id=1, source_target_pairs={{0,16},{16,0},{32,48},{48,32},{64,80},{80,64},{96,112},{112,96},{1... | collective-permute-start | bytes 1572872 | tf_op jit(solution)/shard_map/ppermute | solution.py:548
  81.1 1.0 copy-start.2
  104.7 9.3 %copy-start.3 = (bf16[4,256,256]{2,1,0:T(8,128)(2,1)S(1)}, bf16[4,256,256]{2,1,0:T(8,128)(2,1)}, u32[]{:S(2)}) copy-start(bf16[4,256,256]{2,1,0:T(8,128)(2,1)} %w_ref.5) | copy-start | bytes 1572868
  104.7 4.2 %collective-permute-start.1 = (bf16[2,16,4,8,256]{4,3,2,1,0:T(8,128)(2,1)S(1)}, bf16[2,16,4,8,256]{4,3,2,1,0:T(8,128)(2,1)S(1)}, u32[]{:S(2)}, u32[]{:S(2)}) collective-permute-start(bf16[2,16,4,8,256]{4,3,2,1,0:T(8,128)(2,1)S(1)} %get-tuple-element.59), channel_id=1, source_target_pairs={{0,16},{16,0},{32,48},{48,32},{64,80},{80,64},{96,112},{112,96},{1... | collective-permute-start | bytes 1572872 | tf_op jit(solution)/shard_map/ppermute | solution.py:548
  109.8 17.8 %all-to-all-start.2 = ((bf16[16,8,8,256]{3,2,1,0:T(8,128)(2,1)}), bf16[16,8,8,256]{3,2,1,0:T(8,128)(2,1)S(1)}, u32[]{:S(2)}, u32[]{:S(2)}) async-start(bf16[16,8,8,256]{3,2,1,0:T(8,128)(2,1)} %pad_maximum_fusion), calls=%async_computation.2 | async-start | bytes 1048576 | tf_op jit(solution)/shard_map/all_to_all | solution.py:542
  114.0 1.9 %copy-start = (bf16[2048,768]{1,0:T(8,128)(2,1)S(1)}, bf16[2048,768]{1,0:T(8,128)(2,1)}, u32[]{:S(2)}) copy-start(bf16[2048,768]{1,0:T(8,128)(2,1)} %get-tuple-element.61.back_ref) | copy-start | bytes 9437188
  141.5 5.2 %collective-permute-start.2 = (bf16[8,8,256]{2,1,0:T(8,128)(2,1)S(1)}, bf16[8,8,256]{2,1,0:T(8,128)(2,1)S(1)}, u32[]{:S(2)}, u32[]{:S(2)}) collective-permute-start(bf16[8,8,256]{2,1,0:T(8,128)(2,1)S(1)} %reduce_sum.25), channel_id=1, source_target_pairs={{0,16},{16,0},{32,48},{48,32},{64,80},{80,64},{96,112},{112,96},{1... | collective-permute-start | bytes 98312 | tf_op jit(solution)/shard_map/ppermute | solution.py:548

commit v4 on v3

--- a/solution.py
+++ b/solution.py
@@ -150,12 +150,19 @@
     return out
 
 
-A_STEP = 1024
+A_PARTS = (1024, 1024)
 
 
 def time_forward_kernel(x_hbm, w_hbm, out_hbm, x_ref, w_ref, out_ref, w_sem, in_sem, out_sem):
     w_in = pltpu.make_async_copy(w_hbm, w_ref, w_sem)
-    x_in = copies(x_hbm, x_ref, in_sem, A_STEP)
+    spans, at = [], 0
+    for size in A_PARTS:
+        spans.append((at, size))
+        at += size
+    x_in = [
+        pltpu.make_async_copy(x_hbm.at[pl.ds(at, n)], x_ref.at[pl.ds(at, n)], in_sem.at[i])
+        for i, (at, n) in enumerate(spans)
+    ]
     x_in[0].start()
     w_in.start()
     for c in x_in[1:]:
@@ -163,15 +170,14 @@
     means, swap = head_mean_matrix(), swap_matrix()
     masks = head_masks(BLK)
     diag = time_diag()
-    chans = A_STEP // L
     outs = []
-    for i in range(ROWS // A_STEP):
+    for i, (start, size) in enumerate(spans):
         x_in[i].wait()
         if i == 0:
             w_in.wait()
             wqkv = load_wqkv(w_ref)
             wo = w_ref[3]
-        x = x_ref[i * A_STEP : (i + 1) * A_STEP, :].astype(F32)
+        x = x_ref[start : start + size, :].astype(F32)
         xn = (x * rms_scale(x)).astype(BF16)
         qs, kn, v, _, _ = project(xn, wqkv, means)
         es = [
@@ -182,9 +188,9 @@
         mixed = join(stack_product([u.T for u in split(v)], pbs)).astype(BF16)
         stream = (x + dot(mixed, wo)).astype(BF16)
         for j, part in enumerate(split(stream, SQ)):
-            at = i * chans + j * L
+            at = start // L + j * L
             out_ref[:, at : at + L, :] = dot(swap, part).astype(BF16).reshape(L, L, D)
-        at = pl.ds(i * chans, chans)
+        at = pl.ds(start // L, size // L)
         c = pltpu.make_async_copy(out_ref.at[:, at], out_hbm.at[:, at], out_sem.at[i])
         c.start()
         outs.append(c)
@@ -195,10 +201,13 @@
 PREP_STEP = 512
 
 
-def prepare_kernel(x_ref, w_ref, v_ref, *refs):
-    outs, (xt_ref, p_ref, qs_ref, kn_ref, rq_ref, rk_ref, mt_ref), sems = (
+def prepare_kernel(x_ref, w_ref, *refs):
+    outs, (v_ref, r_ref, xt_ref, p_ref, qs_ref, kn_ref, mt_ref), sems = (
         refs[:7], refs[7:14], refs[14],
     )
+    row, col = iota((D, BLK), 0), iota((D, BLK), 1)
+    pick_q = jnp.where(row == col * HD, 1.0, 0.0).astype(BF16)
+    pick_k = jnp.where(row == (col - HEADS) * HD, 1.0, 0.0).astype(BF16)
     means = head_mean_matrix()
     masks = head_masks(BLK)
     diag = time_diag()
@@ -214,8 +223,7 @@
         qs_ref[at, :] = qs
         kn_ref[at, :] = kn
         v_ref[at, :] = v
-        rq_ref[at, :] = rq.astype(BF16)
-        rk_ref[at, :] = rk.astype(BF16)
+        r_ref[at, :] = (dot(rq.astype(BF16), pick_q) + dot(rk.astype(BF16), pick_k)).astype(BF16)
         es = [
             jnp.exp2(dot_rt(k, stack_heads(q, masks))) * diag
             for q, k in zip(split(qs), split(kn))
@@ -250,21 +258,26 @@
     return r * (ng - xh * jnp.mean(xh * ng, axis=-1, keepdims=True))
 
 
-def write_grads(grads_ref, acc, acc_o):
+def write_grads(core_ref, mine_ref, theirs_ref, acc, acc_o):
+    first = core_ref[0] == 0
     for j in range(4):
         whole = (acc[:, j * D : (j + 1) * D] if j < 3 else acc_o[...]).reshape(16, 2, 8, D)
-        for half in range(2):
-            grads_ref[half, :, j] = whole[:, half].astype(BF16)
+        low, high = whole[:, 0], whole[:, 1]
+        mine_ref[:, j] = jnp.where(first, low, high).astype(BF16)
+        theirs_ref[:, j] = jnp.where(first, high, low).astype(BF16)
 
 
 T_STEP = 1024
 
 
-def time_backward_kernel(sg_ref, w_hbm, v_ref, *refs):
-    kept_hbm, back_hbm, grads_ref = refs[:7], refs[7], refs[8]
-    w_ref, kept, back_ref, acc, acc_o = refs[9], refs[10:17], refs[17], refs[18], refs[19]
-    w_sem, in_sem, out_sem = refs[20:]
-    xt_ref, p_ref, qs_ref, kn_ref, rq_ref, rk_ref, mt_ref = kept
+def time_backward_kernel(core_ref, sg_ref, w_hbm, *refs):
+    kept_hbm, back_hbm, mine_ref, theirs_ref = refs[:7], refs[7], refs[8], refs[9]
+    w_ref, kept, back_ref, acc, acc_o = refs[10], refs[11:18], refs[18], refs[19], refs[20]
+    w_sem, in_sem, out_sem = refs[21:]
+    v_ref, r_ref, xt_ref, p_ref, qs_ref, kn_ref, mt_ref = kept
+    spread = jnp.where(
+        iota((BLK, 2 * D), 0) == div(iota((BLK, 2 * D), 1), HD), 1.0, 0.0
+    ).astype(BF16)
     w_in = pltpu.make_async_copy(w_hbm, w_ref, w_sem)
     w_in.start()
     moves = kept_copies(kept_hbm, kept, in_sem, T_STEP)
@@ -296,15 +309,16 @@
         vb = join([dot(p, d).astype(BF16) for p, d in zip(pbs, dosts)])
         dk = join([dot(ds, stack_heads(q, masks)) for ds, q in zip(dss, split(qs))])
         dq = join(stack_product([k.T for k in split(kn)], dss))
-        qb = query_back(rq_ref[at, :].astype(F32) * 0.25, qs, dq, means)
-        kb = key_back(rk_ref[at, :].astype(F32), kn, dk, means)
+        r = dot(r_ref[at, :], spread)
+        qb = query_back(r[:, :D] * 0.25, qs, dq, means)
+        kb = key_back(r[:, D:], kn, dk, means)
         back = jnp.concatenate([qb, kb, vb], axis=1)
         back_ref[at, :] = back
         back_out[i].start()
         part, part_o = dot(xt_ref[:, at], back), dot(mt_ref[:, at], sg)
         acc[...] = part if i == 0 else acc[...] + part
         acc_o[...] = part_o if i == 0 else acc_o[...] + part_o
-    write_grads(grads_ref, acc, acc_o)
+    write_grads(core_ref, mine_ref, theirs_ref, acc, acc_o)
     for c in back_out:
         c.wait()
 
@@ -333,19 +347,20 @@
 
 
 def channel_kernel(
-    nb_ref, x_ref, up_hbm, w_hbm, sg_hbm, back_hbm, mixed_hbm,
-    up_ref, w_ref, up_sem, w_sem, sg_s, back_s, mixed_s, qs_s, kn_s, v_s, kt_s, vt_s, rq_s, rk_s, dq_s, dk_s, dv_s,
+    nb_ref, x_ref, up_hbm, do_hbm, w_hbm, sg_hbm, back_hbm, mixed_hbm,
+    up_ref, do_ref, w_ref, up_sem, do_sem, w_sem, sg_s, back_s, mixed_s, qs_s, kn_s, v_s, kt_s, vt_s, rq_s, rk_s, dq_s, dk_s, dv_s,
     sg_sem, back_sem, mixed_sem,
 ):
-    w_in = pltpu.make_async_copy(w_hbm, w_ref, w_sem)
+    w_in = pltpu.make_async_copy(w_hbm.at[pl.ds(0, 3)], w_ref, w_sem)
     w_in.start()
     up_in = pltpu.make_async_copy(up_hbm, up_ref, up_sem)
+    do_in = pltpu.make_async_copy(do_hbm, do_ref, do_sem)
+    do_in.start()
     up_in.start()
     means = head_mean_matrix()
     masks = head_masks(BLK)
     w_in.wait()
     wqkv = load_wqkv(w_ref)
-    wo = w_ref[3]
 
     def first(i, at):
         x = x_ref[at, :].astype(F32)
@@ -362,9 +377,8 @@
         dv_s[at, :] = jnp.zeros((C_STEP, D), F32)
 
     loop(C_STEP, first)
+    do_in.wait()
     up_in.wait()
-
-    span = GROUPS * BLK
 
     def attend(i, carry):
         bs = [i * GROUPS + g for g in range(GROUPS)]
@@ -377,8 +391,7 @@
             jnp.exp2(dot_rt(join([kn_s[n, :] for n in near]), q))
             for near, q in zip(nears, qsts)
         ]
-        do = dot_rt(up_ref[pl.ds(pl.multiple_of(i * span, span), span), :], wo).astype(BF16)
-        dosts = [stack_heads(d, masks) for d in split(do)]
+        dosts = [stack_heads(do_ref[at, :], masks) for at in ats]
         dps = [dot_rt(join([v_s[n, :] for n in near]), d) for near, d in zip(nears, dosts)]
         ps = softmax_columns(es)
         pbs = [p.astype(BF16) for p in ps]
@@ -426,7 +439,9 @@
 G_STEP = 512
 
 
-def channel_grads_kernel(x_ref, up_ref, back_ref, mixed_ref, w_ref, out_ref, grads_ref, acc, acc_o):
+def channel_grads_kernel(
+    core_ref, x_ref, up_ref, back_ref, mixed_ref, w_ref, out_ref, mine_ref, theirs_ref, acc, acc_o
+):
     wo = w_ref[3]
     acc[...] = jnp.zeros_like(acc)
     acc_o[...] = jnp.zeros_like(acc_o)
@@ -440,7 +455,7 @@
         acc_o[...] += dot_lt(mixed, up_ref[at, :])
 
     loop(G_STEP, body)
-    write_grads(grads_ref, acc, acc_o)
+    write_grads(core_ref, mine_ref, theirs_ref, acc, acc_o)
 
 
 VM = pl.BlockSpec(memory_space=pltpu.VMEM)
@@ -458,7 +473,7 @@
 
 
 ROW = (ROWS, D)
-GRADS = (2, 16, 4, 8, D)
+GRADS = (16, 4, 8, D)
 SCORES = (ROWS // BLK, BLK, HEADS * BLK)
 
 
@@ -486,45 +501,62 @@
 def time_forward(x, w):
     return call(
         time_forward_kernel, "time_forward", 24, [shape((L, CH, D))], [HB, HB], [HB], (x, w),
-        [vm(ROW), vm((4, D, D)), vm((L, CH, D)), DMA, DMA((2,)), DMA((2,))],
+        [vm(ROW), vm((4, D, D)), vm((L, CH, D)), DMA, DMA((len(A_PARTS),)), DMA((len(A_PARTS),))],
         flops=2 * 10**9,
     )[0]
 
 
 def prepare(x, w):
-    names = [shape(ROW), shape((D, ROWS)), shape(SCORES)] + [shape(ROW)] * 4 + [shape((D, ROWS))]
+    cols = shape((D, ROWS))
+    names = [shape(ROW), shape((ROWS, BLK)), cols, shape(SCORES), shape(ROW), shape(ROW), cols]
     return call(
-        prepare_kernel, "prepare", 28, names, [VM] * 2, [VM] + [HB] * 7, (x, w),
-        [vm(o.shape) for o in names[1:]] + [DMA((7, ROWS // PREP_STEP))],
+        prepare_kernel, "prepare", 28, names, [VM] * 2, [HB] * 7, (x, w),
+        [vm(o.shape) for o in names] + [DMA((7, ROWS // PREP_STEP))],
         flops=3 * 10**9,
     )
 
 
-def channel(nb, x, up, w):
+def output_back_kernel(up_ref, w_ref, do_ref):
+    wo = w_ref[3]
+
+    def body(i, at):
+        do_ref[at, :] = dot_rt(up_ref[at, :], wo).astype(BF16)
+
+    loop(512, body)
+
+
+def output_back(up, w):
+    return call(
+        output_back_kernel, "output_back", 16, [shape(ROW)], [VM] * 2, [VM], (up, w),
+        flops=10**9,
+    )[0]
+
+
+def channel(nb, x, up, do, w):
     return call(
         channel_kernel, "channel", 48,
         [shape(ROW), shape((ROWS, 3 * D)), shape(ROW)],
-        [SM, VM, HB, HB], [HB] * 3, (nb, x, up, w),
-        [vm(ROW), vm((4, D, D)), DMA, DMA]
+        [SM, VM, HB, HB, HB], [HB] * 3, (nb, x, up, do, w),
+        [vm(ROW), vm(ROW), vm((3, D, D)), DMA, DMA, DMA]
         + [vm(ROW), vm((ROWS, 3 * D)), vm(ROW), vm(ROW), vm(ROW), vm(ROW)]
         + [vm((D, ROWS))] * 2 + [vm(ROW)] * 2 + [vm(ROW, F32)] * 3 + [DMA((2,)), DMA((2,)), DMA],
         flops=8 * 10**9,
     )
 
 
-def channel_grads(x, up, back, mixed, w):
+def channel_grads(core, x, up, back, mixed, w):
     return call(
-        channel_grads_kernel, "channel_grads", 20, [shape(ROW), shape(GRADS)],
-        [VM] * 5, [VM] * 2, (x, up, back, mixed, w),
+        channel_grads_kernel, "channel_grads", 20, [shape(ROW), shape(GRADS), shape(GRADS)],
+        [SM] + [VM] * 5, [VM] * 3, (core, x, up, back, mixed, w),
         [vm((D, 3 * D), F32), vm((D, D), F32)], flops=2 * 10**9,
     )
 
 
-def time_backward(sg, kept, w):
+def time_backward(core, sg, kept, w):
     return call(
-        time_backward_kernel, "time_backward", 30, [shape((ROWS, 3 * D)), shape(GRADS)],
-        [VM, HB, VM] + [HB] * 7, [HB, VM], (sg, w[3]) + tuple(kept),
-        [vm((D, D))] + [vm(k.shape) for k in kept[1:]]
+        time_backward_kernel, "time_backward", 30, [shape((ROWS, 3 * D)), shape(GRADS), shape(GRADS)],
+        [SM, VM, HB] + [HB] * 7, [HB, VM, VM], (core, sg, w[3]) + tuple(kept),
+        [vm((D, D))] + [vm(k.shape) for k in kept]
         + [vm((ROWS, 3 * D)), vm((D, 3 * D), F32), vm((D, D), F32)]
         + [DMA, DMA((7, ROWS // T_STEP)), DMA((ROWS // T_STEP,))],
         flops=4 * 10**9,
@@ -548,10 +580,8 @@
     return lax.ppermute(x, "dp", [(i, i ^ 1) for i in range(16)])
 
 
-def add_cores(parts, core):
-    mine = lax.dynamic_index_in_dim(parts, core, 0, keepdims=False)
-    theirs = lax.dynamic_index_in_dim(other_core(parts), core, 0, keepdims=False)
-    return (mine.astype(F32) + theirs.astype(F32)).astype(BF16)
+def add_cores(mine, theirs):
+    return (mine.astype(F32) + other_core(theirs).astype(F32)).astype(BF16)
 
 
 CHIPS = [[i for i in range(16) if i % 2 == c] for c in range(2)]
@@ -576,15 +606,17 @@
     x = series.reshape(ROWS, D)
     up = upstream_grad.reshape(ROWS, D)
     stream = exchange(time_forward(x, time_weights), "mp").reshape(ROWS, D)
-    sg, back, mixed = channel(neighbors, stream, up, channel_weights)
+    do = output_back(up, channel_weights)
+    sg, back, mixed = channel(neighbors, stream, up, do, channel_weights)
     x, sg = lax.optimization_barrier((x, sg))
     returned = exchange(sg.reshape(16, CH, D), "mp")
-    out, channel_parts = channel_grads(stream, up, back, mixed, channel_weights)
-    channel_half = add_cores(channel_parts, core)
+    place = core.reshape(1)
+    out, *channel_parts = channel_grads(place, stream, up, back, mixed, channel_weights)
+    channel_half = add_cores(*channel_parts)
     kept = prepare(x, time_weights)
     returned, channel_half, kept = lax.optimization_barrier((returned, channel_half, kept))
-    time_back, time_parts = time_backward(returned, kept, time_weights)
-    halves = jnp.concatenate([channel_half, add_cores(time_parts, core)], axis=1)
+    time_back, *time_parts = time_backward(place, returned, kept, time_weights)
+    halves = jnp.concatenate([channel_half, add_cores(*time_parts)], axis=1)
     sums, series_grad = reduce_grads(
         halves, core, lambda gate: series_gradient(x, returned, gate(time_back), time_weights)
     )

time: 148 us -> 147 us (level)
    pallas_call x6 -> x7, Pallas kernels: 49.2 us -> 50.2 us  [call(): pl.pallas_call(kernel, out_shape=[pltpu.HBM(o.shape, o.dtype) if spec is...]
    unnamed x19 -> x25, local copies, waits for them, and re-layouts: 8.4 us -> 8.34 us
  transfers between devices with their start and end apart: 6 -> 6, of which waited for: 5 -> 5; matrix products, arithmetic and copies ran while one was open for 2% -> 1% of each run, Pallas kernels for 9% -> 9%
where the time goes in v4:
time: 147 us
  Pallas kernels  50.2 us (34%)
  waiting for transfers between devices  42.1 us (29%)
  starting transfers between devices  28.1 us (19%)
  blocking collectives  13.8 us (9%)
  local copies, waits for them, and re-layouts  10.6 us (7%)
    pallas_call x7, Pallas kernels, call(): pl.pallas_call(kernel, out_shape=[pltpu.HBM(o.shape, o.dtype) if spec is...  50.2 us
    all_to_all x3, waiting for transfers between devices, exchange(): lax.all_to_all(x, axis, split_axis=0, concat_axis=0, tiled=True, axis_ind...  40.1 us
    all_to_all x3, starting transfers between devices, exchange(): lax.all_to_all(x, axis, split_axis=0, concat_axis=0, tiled=True, axis_ind...  20.3 us
    all_to_all x1, blocking collectives, exchange(): lax.all_to_all(x, axis, split_axis=0, concat_axis=0, tiled=True, axis_ind...  13.8 us
    unnamed x25, local copies, waits for them, and re-layouts  8.34 us
    ppermute x3, starting transfers between devices, other_core(): return lax.ppermute(x, 'dp', [(i, i ^ 1) for i in range(16)])  7.79 us
  transfers between devices with their start and end apart: 6, of which 5 were waited for; matrix products, arithmetic and copies ran while one was open for 1% of the time, Pallas kernels for 9%

profile of v4, /device:TPU:1, one launch (start us, length us, event | category | flops | bytes accessed | tf_op | source)
XLA Modules:
  0.0 146.7 jit_solution(17154905625645976991)
XLA Ops:
  0.6 0.0 copy-start.11
  0.6 0.0 copy-start.4
  0.7 0.0 copy-start.6
  0.7 6.7 %time_forward.1 = bf16[16,128,256]{2,1,0:T(8,128)(2,1)} custom-call(bf16[2048,256]{1,0:T(8,128)(2,1)} %bitcast.11, bf16[4,256,256]{2,1,0:T(8,128)(2,1)} %w_ref.7), custom_call_target="tpu_custom_call" | custom-call | flops 2000000000 | bytes 8388608 | tf_op jit(solution)/shard_map/time_forward/pallas_call | solution.py:485
  7.4 10.1 %all-to-all-start = ((bf16[16,128,256]{2,1,0:T(8,128)(2,1)}), bf16[16,128,256]{2,1,0:T(8,128)(2,1)S(1)}, u32[]{:S(2)}, u32[]{:S(2)}) async-start(bf16[16,128,256]{2,1,0:T(8,128)(2,1)} %time_forward.1), calls=%async_computation | async-start | bytes 2097152 | tf_op jit(solution)/shard_map/all_to_all | solution.py:574
  17.6 0.0 copy-done.11
  17.6 0.1 copy.10.nb_ref
  17.7 0.0 copy-done.4
  17.7 0.0 copy-done.6
  17.7 1.1 output_back.1.do_hbm
  18.7 0.0 copy-start.10
  18.7 1.0 copy-done.10
  19.7 23.6 %all-to-all-done = bf16[16,128,256]{2,1,0:T(8,128)(2,1)S(1)} async-done(((bf16[16,128,256]{2,1,0:T(8,128)(2,1)}), bf16[16,128,256]{2,1,0:T(8,128)(2,1)S(1)}, u32[]{:S(2)}, u32[]{:S(2)}) %all-to-all-start) | async-done | bytes 1048608 | tf_op jit(solution)/shard_map/all_to_all | solution.py:574
  43.3 20.1 %channel.1 = (bf16[2048,256]{1,0:T(8,128)(2,1)}, bf16[2048,768]{1,0:T(8,128)(2,1)}, bf16[2048,256]{1,0:T(8,128)(2,1)}) custom-call(s32[16,3]{1,0:T(8,128)S(1)} %copy.10.nb_ref, bf16[2048,256]{1,0:T(8,128)(2,1)S(1)} %bitcast.9, bf16[2048,256]{1,0:T(8,128)(2,1)} %bitcast.14, bf16[2048,256]{1,0:T(8,128)(2,1)} %copy-done.10, bf16[4,256,256]{2,1,0:T(8,128)(2,1)} %w_ref.5), custom_call_target="tpu_custom_call" | custom-call | flops 8000000000 | bytes 8388608 | tf_op jit(solution)/shard_map/channel/pallas_call | solution.py:485
  63.4 6.0 %all-to-all-start.1 = ((bf16[16,128,256]{2,1,0:T(8,128)(2,1)}), bf16[16,128,256]{2,1,0:T(8,128)(2,1)S(1)}, u32[]{:S(2)}, u32[]{:S(2)}) async-start(bf16[16,128,256]{2,1,0:T(8,128)(2,1)} %bitcast.17), calls=%async_computation.1 | async-start | bytes 2097152 | tf_op jit(solution)/shard_map/all_to_all | solution.py:574
  69.4 1.6 %slice_bitcast_fusion.w_hbm = bf16[256,256]{1,0:T(8,128)(2,1)} fusion(bf16[4,256,256]{2,1,0:T(8,128)(2,1)} %w_ref.7), kind=kLoop, calls=%fused_computation.4 | loop fusion | bytes 262144 | tf_op jit(solution)/shard_map/squeeze | solution.py:558
  70.9 0.0 copy-start.5
  71.0 1.2 copy-done.5
  72.2 0.0 copy-start.7
  72.2 1.0 copy-done.7
  73.2 0.0 copy-start.8
  73.2 1.9 %copy-done.8 = bf16[2048,768]{1,0:T(8,128)(2,1)S(1)} copy-done((bf16[2048,768]{1,0:T(8,128)(2,1)S(1)}, bf16[2048,768]{1,0:T(8,128)(2,1)}, u32[]{:S(2)}) %copy-start.8) | copy-done | bytes 3145752
  75.1 0.0 copy-start.9
  75.1 1.2 copy-done.9
  76.3 0.0 copy-start.1
  76.3 0.0 copy-start.2
  76.3 3.3 %channel_grads.1 = (bf16[2048,256]{1,0:T(8,128)(2,1)}, bf16[16,4,8,256]{3,2,1,0:T(8,128)(2,1)S(1)}, bf16[16,4,8,256]{3,2,1,0:T(8,128)(2,1)S(1)}) custom-call(s32[1]{0:T(128)} %bitcast.core_ref, bf16[2048,256]{1,0:T(8,128)(2,1)S(1)} %bitcast.10, bf16[2048,256]{1,0:T(8,128)(2,1)S(1)} %bitcast.16, bf16[2048,768]{1,0:T(8,128)(2,1)S(1)} %copy-done.8, ...), custom_call_target="tpu_custom_call" | custom-call | flops 2000000000 | bytes 8388608 | tf_op jit(solution)/shard_map/channel_grads/pallas_call | solution.py:485
  79.7 0.8 collective-permute-start
  80.5 0.0 copy-done.1
  80.5 0.0 copy-done.2
  80.5 6.3 %prepare.1 = (bf16[2048,256]{1,0:T(8,128)(2,1)}, bf16[2048,128]{1,0:T(8,128)(2,1)}, bf16[256,2048]{1,0:T(8,128)(2,1)}, bf16[16,128,512]{2,1,0:T(8,128)(2,1)}, bf...) custom-call(bf16[2048,256]{1,0:T(8,128)(2,1)S(1)} %bitcast.12, ...), custom_call_target="tpu_custom_call" | custom-call | flops 3000000000 | bytes 8388608 | tf_op jit(solution)/shard_map/prepare/pallas_call | solution.py:485
  86.8 0.0 collective-permute-done
  86.8 0.1 add_convert_fusion.1
  86.9 8.0 %all-to-all-done.1.sg_ref = bf16[16,128,256]{2,1,0:T(8,128)(2,1)S(1)} async-done(((bf16[16,128,256]{2,1,0:T(8,128)(2,1)}), bf16[16,128,256]{2,1,0:T(8,128)(2,1)S(1)}, u32[]{:S(2)}, u32[]{:S(2)}) %all-to-all-start.1) | async-done | bytes 1048608 | tf_op jit(solution)/shard_map/all_to_all | solution.py:574
  94.8 9.4 %time_backward.1 = (bf16[2048,768]{1,0:T(8,128)(2,1)}, bf16[16,4,8,256]{3,2,1,0:T(8,128)(2,1)S(1)}, bf16[16,4,8,256]{3,2,1,0:T(8,128)(2,1)S(1)}) custom-call(s32[1]{0:T(128)} %bitcast.core_ref, bf16[16,128,256]{2,1,0:T(8,128)(2,1)S(1)} %all-to-all-done.1.sg_ref, bf16[256,256]{1,0:T(8,128)(2,1)} %slice_bitcast_fusion.w_hbm, ...), custom_call_target="tpu_custom_call" | custom-call | flops 4000000000 | bytes 8388608 | tf_op jit(solution)/shard_map/time_backward/pallas_call | solution.py:485
  104.3 0.0 copy-start.3
  104.3 2.7 %collective-permute-start.1 = (bf16[16,4,8,256]{3,2,1,0:T(8,128)(2,1)S(1)}, bf16[16,4,8,256]{3,2,1,0:T(8,128)(2,1)S(1)}, u32[]{:S(2)}, u32[]{:S(2)}) collective-permute-start(bf16[16,4,8,256]{3,2,1,0:T(8,128)(2,1)S(1)} %get-tuple-element.59), channel_id=1, source_target_pairs={{0,16},{16,0},{32,48},{48,32},{64,80},{80,64},{96,112},{112,96},{1... | collective-permute-start | bytes 786440 | tf_op jit(solution)/shard_map/ppermute | solution.py:580
  107.0 1.2 collective-permute-done.1
  108.1 0.1 add_convert_fusion
  108.2 0.8 pad_maximum_fusion
  109.1 4.2 %all-to-all-start.2 = ((bf16[16,8,8,256]{3,2,1,0:T(8,128)(2,1)}), bf16[16,8,8,256]{3,2,1,0:T(8,128)(2,1)S(1)}, u32[]{:S(2)}, u32[]{:S(2)}) async-start(bf16[16,8,8,256]{3,2,1,0:T(8,128)(2,1)} %pad_maximum_fusion), calls=%async_computation.2 | async-start | bytes 1048576 | tf_op jit(solution)/shard_map/all_to_all | solution.py:574
  113.2 0.0 copy-done.3
  113.2 0.0 copy-start
  113.3 1.9 %copy-done = bf16[2048,768]{1,0:T(8,128)(2,1)S(1)} copy-done((bf16[2048,768]{1,0:T(8,128)(2,1)S(1)}, bf16[2048,768]{1,0:T(8,128)(2,1)}, u32[]{:S(2)}) %copy-start) | copy-done | bytes 3145752
  115.1 3.2 %series_grad.1 = bf16[2048,256]{1,0:T(8,128)(2,1)} custom-call(bf16[2048,256]{1,0:T(8,128)(2,1)S(1)} %bitcast.13, bf16[16,128,256]{2,1,0:T(8,128)(2,1)S(1)} %all-to-all-done.1.sg_ref, bf16[2048,768]{1,0:T(8,128)(2,1)S(1)} %copy-done, bf16[4,256,256]{2,1,0:T(8,128)(2,1)S(1)} %copy-done.3), custom_call_target="tpu_custom_call" | custom-call | flops 1000000000 | bytes 8388608 | tf_op jit(solution)/shard_map/series_grad/pallas_call | solution.py:485
  118.3 8.5 %all-to-all-done.2 = bf16[16,8,8,256]{3,2,1,0:T(8,128)(2,1)S(1)} async-done(((bf16[16,8,8,256]{3,2,1,0:T(8,128)(2,1)}), bf16[16,8,8,256]{3,2,1,0:T(8,128)(2,1)S(1)}, u32[]{:S(2)}, u32[]{:S(2)}) %all-to-all-start.2) | async-done | bytes 524320 | tf_op jit(solution)/shard_map/all_to_all | solution.py:574
  126.8 0.1 reduce_sum.24
  126.9 13.8 %all_to_all.20 = bf16[8,8,8,256]{3,2,1,0:T(8,128)(2,1)S(1)} all-to-all(bf16[8,8,8,256]{3,2,1,0:T(8,128)(2,1)S(1)} %broadcast_in_dim.2), channel_id=1, replica_groups={{0,32,64,96,128,160,192,224},{16,48,80,112,144,176,208,240},{1,33,65,97..., dimensions={0} | all-to-all | bytes 524288 | tf_op jit(solution)/shard_map/all_to_all | solution.py:574
  140.8 4.3 %collective-permute-start.2 = (bf16[8,8,256]{2,1,0:T(8,128)(2,1)S(1)}, bf16[8,8,256]{2,1,0:T(8,128)(2,1)S(1)}, u32[]{:S(2)}, u32[]{:S(2)}) collective-permute-start(bf16[8,8,256]{2,1,0:T(8,128)(2,1)S(1)} %reduce_sum.25), channel_id=1, source_target_pairs={{0,16},{16,0},{32,48},{48,32},{64,80},{80,64},{96,112},{112,96},{1... | collective-permute-start | bytes 98312 | tf_op jit(solution)/shard_map/ppermute | solution.py:580
  145.1 0.9 collective-permute-done.2
  146.0 0.7 fusion
  (4 shorter events, 0.1 us)
Async XLA Ops:
  0.6 16.9 %copy-start.11 = (s32[16,3]{0,1:T(4,128)S(1)}, s32[16,3]{0,1:T(4,128)}, u32[]{:S(2)}) copy-start(s32[16,3]{0,1:T(4,128)} %param.9) | copy-start | bytes 580
  0.6 17.0 %copy-start.4 = (bf16[1,2048,1,256]{3,1,2,0:T(8,128)(2,1)S(1)}, bf16[1,2048,1,256]{3,1,2,0:T(8,128)(2,1)}, u32[]{:S(2)}) copy-start(bf16[1,2048,1,256]{3,1,2,0:T(8,128)(2,1)} %param.6) | copy-start | bytes 3145732
  0.7 17.0 %copy-start.6 = (bf16[4,256,256]{2,1,0:T(8,128)(2,1)S(1)}, bf16[4,256,256]{2,1,0:T(8,128)(2,1)}, u32[]{:S(2)}) copy-start(bf16[4,256,256]{2,1,0:T(8,128)(2,1)} %w_ref.5) | copy-start | bytes 1572868
  7.4 35.9 %all-to-all-start = ((bf16[16,128,256]{2,1,0:T(8,128)(2,1)}), bf16[16,128,256]{2,1,0:T(8,128)(2,1)S(1)}, u32[]{:S(2)}, u32[]{:S(2)}) async-start(bf16[16,128,256]{2,1,0:T(8,128)(2,1)} %time_forward.1), calls=%async_computation | async-start | bytes 2097152 | tf_op jit(solution)/shard_map/all_to_all | solution.py:574
  18.7 1.0 copy-start.10
  63.4 31.4 %all-to-all-start.1 = ((bf16[16,128,256]{2,1,0:T(8,128)(2,1)}), bf16[16,128,256]{2,1,0:T(8,128)(2,1)S(1)}, u32[]{:S(2)}, u32[]{:S(2)}) async-start(bf16[16,128,256]{2,1,0:T(8,128)(2,1)} %bitcast.17), calls=%async_computation.1 | async-start | bytes 2097152 | tf_op jit(solution)/shard_map/all_to_all | solution.py:574
  70.9 1.2 copy-start.5
  72.2 1.0 copy-start.7
  73.2 1.9 %copy-start.8 = (bf16[2048,768]{1,0:T(8,128)(2,1)S(1)}, bf16[2048,768]{1,0:T(8,128)(2,1)}, u32[]{:S(2)}) copy-start(bf16[2048,768]{1,0:T(8,128)(2,1)} %get-tuple-element.34.back_ref) | copy-start | bytes 9437188
  75.1 1.2 copy-start.9
  76.3 4.1 %copy-start.1 = (bf16[1,128,16,256]{3,2,1,0:T(8,128)(2,1)S(1)}, bf16[1,128,16,256]{3,2,1,0:T(8,128)(2,1)}, u32[]{:S(2)}) copy-start(bf16[1,128,16,256]{3,2,1,0:T(8,128)(2,1)} %param.5) | copy-start | bytes 3145732
  76.3 4.1 %copy-start.2 = (bf16[4,256,256]{2,1,0:T(8,128)(2,1)S(1)}, bf16[4,256,256]{2,1,0:T(8,128)(2,1)}, u32[]{:S(2)}) copy-start(bf16[4,256,256]{2,1,0:T(8,128)(2,1)} %w_ref.7) | copy-start | bytes 1572868
  79.7 7.1 %collective-permute-start = (bf16[16,4,8,256]{3,2,1,0:T(8,128)(2,1)S(1)}, bf16[16,4,8,256]{3,2,1,0:T(8,128)(2,1)S(1)}, u32[]{:S(2)}, u32[]{:S(2)}) collective-permute-start(bf16[16,4,8,256]{3,2,1,0:T(8,128)(2,1)S(1)} %get-tuple-element.40), channel_id=1, source_target_pairs={{0,16},{16,0},{32,48},{48,32},{64,80},{80,64},{96,112},{112,96},{1... | collective-permute-start | bytes 786440 | tf_op jit(solution)/shard_map/ppermute | solution.py:580
  104.3 8.9 %copy-start.3 = (bf16[4,256,256]{2,1,0:T(8,128)(2,1)S(1)}, bf16[4,256,256]{2,1,0:T(8,128)(2,1)}, u32[]{:S(2)}) copy-start(bf16[4,256,256]{2,1,0:T(8,128)(2,1)} %w_ref.7) | copy-start | bytes 1572868
  104.3 3.8 %collective-permute-start.1 = (bf16[16,4,8,256]{3,2,1,0:T(8,128)(2,1)S(1)}, bf16[16,4,8,256]{3,2,1,0:T(8,128)(2,1)S(1)}, u32[]{:S(2)}, u32[]{:S(2)}) collective-permute-start(bf16[16,4,8,256]{3,2,1,0:T(8,128)(2,1)S(1)} %get-tuple-element.59), channel_id=1, source_target_pairs={{0,16},{16,0},{32,48},{48,32},{64,80},{80,64},{96,112},{112,96},{1... | collective-permute-start | bytes 786440 | tf_op jit(solution)/shard_map/ppermute | solution.py:580
  109.1 17.8 %all-to-all-start.2 = ((bf16[16,8,8,256]{3,2,1,0:T(8,128)(2,1)}), bf16[16,8,8,256]{3,2,1,0:T(8,128)(2,1)S(1)}, u32[]{:S(2)}, u32[]{:S(2)}) async-start(bf16[16,8,8,256]{3,2,1,0:T(8,128)(2,1)} %pad_maximum_fusion), calls=%async_computation.2 | async-start | bytes 1048576 | tf_op jit(solution)/shard_map/all_to_all | solution.py:574
  113.2 1.9 %copy-start = (bf16[2048,768]{1,0:T(8,128)(2,1)S(1)}, bf16[2048,768]{1,0:T(8,128)(2,1)}, u32[]{:S(2)}) copy-start(bf16[2048,768]{1,0:T(8,128)(2,1)} %get-tuple-element.61.back_ref) | copy-start | bytes 9437188
  140.8 5.2 %collective-permute-start.2 = (bf16[8,8,256]{2,1,0:T(8,128)(2,1)S(1)}, bf16[8,8,256]{2,1,0:T(8,128)(2,1)S(1)}, u32[]{:S(2)}, u32[]{:S(2)}) collective-permute-start(bf16[8,8,256]{2,1,0:T(8,128)(2,1)S(1)} %reduce_sum.25), channel_id=1, source_target_pairs={{0,16},{16,0},{32,48},{48,32},{64,80},{80,64},{96,112},{112,96},{1... | collective-permute-start | bytes 98312 | tf_op jit(solution)/shard_map/ppermute | solution.py:580

commit v5 on v4

--- a/solution.py
+++ b/solution.py
@@ -349,7 +349,7 @@
 def channel_kernel(
     nb_ref, x_ref, up_hbm, do_hbm, w_hbm, sg_hbm, back_hbm, mixed_hbm,
     up_ref, do_ref, w_ref, up_sem, do_sem, w_sem, sg_s, back_s, mixed_s, qs_s, kn_s, v_s, kt_s, vt_s, rq_s, rk_s, dq_s, dk_s, dv_s,
-    sg_sem, back_sem, mixed_sem,
+    sg_sem, back_sem, value_sem, mixed_sem,
 ):
     w_in = pltpu.make_async_copy(w_hbm.at[pl.ds(0, 3)], w_ref, w_sem)
     w_in.start()
@@ -418,21 +418,28 @@
     mixed_out = pltpu.make_async_copy(mixed_s, mixed_hbm, mixed_sem)
     mixed_out.start()
     sg_out = copies(sg_s, sg_hbm, sg_sem, C_STEP)
-    back_out = copies(back_s, back_hbm, back_sem, C_STEP)
+    cols, value = pl.ds(0, 2 * D), pl.ds(2 * D, D)
+    value_out = copies(back_s.at[:, value], back_hbm.at[:, value], value_sem, C_STEP)
+    back_out = copies(back_s.at[:, cols], back_hbm.at[:, cols], back_sem, C_STEP)
+    for i in range(ROWS // C_STEP):
+        at = slice(i * C_STEP, (i + 1) * C_STEP)
+        back_s[at, 2 * D :] = dv_s[at, :].astype(BF16)
+        value_out[i].start()
     for i in range(ROWS // C_STEP):
         at = slice(i * C_STEP, (i + 1) * C_STEP)
         x = x_ref[at, :].astype(F32)
         r = rms_scale(x)
         qb = query_back(rq_s[at, :].astype(F32) * 0.25, qs_s[at, :], dq_s[at, :], means)
         kb = key_back(rk_s[at, :].astype(F32), kn_s[at, :], dk_s[at, :], means)
-        back = jnp.concatenate([qb, kb, dv_s[at, :].astype(BF16)], axis=1)
-        back_s[at, :] = back
+        pair = jnp.concatenate([qb, kb], axis=1)
+        back_s[at, : 2 * D] = pair
+        back = jnp.concatenate([pair, back_s[at, 2 * D :]], axis=1)
         back_out[i].start()
         dx = rms_back(x, r, dot_rt(back, wqkv))
         sg_s[at, :] = (up_ref[at, :].astype(F32) + dx).astype(BF16)
         sg_out[i].start()
     mixed_out.wait()
-    for c in back_out + sg_out:
+    for c in value_out + back_out + sg_out:
         c.wait()
 
 
@@ -539,7 +546,7 @@
         [SM, VM, HB, HB, HB], [HB] * 3, (nb, x, up, do, w),
         [vm(ROW), vm(ROW), vm((3, D, D)), DMA, DMA, DMA]
         + [vm(ROW), vm((ROWS, 3 * D)), vm(ROW), vm(ROW), vm(ROW), vm(ROW)]
-        + [vm((D, ROWS))] * 2 + [vm(ROW)] * 2 + [vm(ROW, F32)] * 3 + [DMA((2,)), DMA((2,)), DMA],
+        + [vm((D, ROWS))] * 2 + [vm(ROW)] * 2 + [vm(ROW, F32)] * 3 + [DMA((2,)), DMA((2,)), DMA((2,)), DMA],
         flops=8 * 10**9,
     )
 

time: 147 us -> 147 us (level)
  no operation moved by 1% of the time
where the time goes in v5:
time: 147 us; the launch traced here: 146 us
  Pallas kernels  49.9 us (34%)
  waiting for transfers between devices  42.1 us (29%)
  starting transfers between devices  28 us (19%)
  blocking collectives  13.8 us (9%)
  local copies, waits for them, and re-layouts  10.6 us (7%)
    pallas_call x7, Pallas kernels, call(): pl.pallas_call(kernel, out_shape=[pltpu.HBM(o.shape, o.dtype) if spec is...  49.9 us
    all_to_all x3, waiting for transfers between devices, exchange(): lax.all_to_all(x, axis, split_axis=0, concat_axis=0, tiled=True, axis_ind...  40.1 us
    all_to_all x3, starting transfers between devices, exchange(): lax.all_to_all(x, axis, split_axis=0, concat_axis=0, tiled=True, axis_ind...  20.3 us
    all_to_all x1, blocking collectives, exchange(): lax.all_to_all(x, axis, split_axis=0, concat_axis=0, tiled=True, axis_ind...  13.8 us
    unnamed x25, local copies, waits for them, and re-layouts  8.34 us
    ppermute x3, starting transfers between devices, other_core(): return lax.ppermute(x, 'dp', [(i, i ^ 1) for i in range(16)])  7.77 us
  transfers between devices with their start and end apart: 6, of which 5 were waited for; matrix products, arithmetic and copies ran while one was open for 1% of the time, Pallas kernels for 9%

profile of v5, /device:TPU:1, one launch (start us, length us, event | category | flops | bytes accessed | tf_op | source)
XLA Modules:
  0.0 146.4 jit_solution(16241546993208003412)
XLA Ops:
  0.6 0.0 copy-start.11
  0.6 0.0 copy-start.4
  0.7 0.0 copy-start.6
  0.7 6.7 %time_forward.1 = bf16[16,128,256]{2,1,0:T(8,128)(2,1)} custom-call(bf16[2048,256]{1,0:T(8,128)(2,1)} %bitcast.11, bf16[4,256,256]{2,1,0:T(8,128)(2,1)} %w_ref.7), custom_call_target="tpu_custom_call" | custom-call | flops 2000000000 | bytes 8388608 | tf_op jit(solution)/shard_map/time_forward/pallas_call | solution.py:492
  7.4 10.1 %all-to-all-start = ((bf16[16,128,256]{2,1,0:T(8,128)(2,1)}), bf16[16,128,256]{2,1,0:T(8,128)(2,1)S(1)}, u32[]{:S(2)}, u32[]{:S(2)}) async-start(bf16[16,128,256]{2,1,0:T(8,128)(2,1)} %time_forward.1), calls=%async_computation | async-start | bytes 2097152 | tf_op jit(solution)/shard_map/all_to_all | solution.py:581
  17.6 0.0 copy-done.11
  17.6 0.1 copy.10.nb_ref
  17.7 0.0 copy-done.4
  17.7 0.0 copy-done.6
  17.7 1.1 output_back.1.do_hbm
  18.7 0.0 copy-start.10
  18.7 1.0 copy-done.10
  19.7 23.6 %all-to-all-done = bf16[16,128,256]{2,1,0:T(8,128)(2,1)S(1)} async-done(((bf16[16,128,256]{2,1,0:T(8,128)(2,1)}), bf16[16,128,256]{2,1,0:T(8,128)(2,1)S(1)}, u32[]{:S(2)}, u32[]{:S(2)}) %all-to-all-start) | async-done | bytes 1048608 | tf_op jit(solution)/shard_map/all_to_all | solution.py:581
  43.3 19.9 %channel.1 = (bf16[2048,256]{1,0:T(8,128)(2,1)}, bf16[2048,768]{1,0:T(8,128)(2,1)}, bf16[2048,256]{1,0:T(8,128)(2,1)}) custom-call(s32[16,3]{1,0:T(8,128)S(1)} %copy.10.nb_ref, bf16[2048,256]{1,0:T(8,128)(2,1)S(1)} %bitcast.9, bf16[2048,256]{1,0:T(8,128)(2,1)} %bitcast.14, bf16[2048,256]{1,0:T(8,128)(2,1)} %copy-done.10, bf16[4,256,256]{2,1,0:T(8,128)(2,1)} %w_ref.5), custom_call_target="tpu_custom_call" | custom-call | flops 8000000000 | bytes 8388608 | tf_op jit(solution)/shard_map/channel/pallas_call | solution.py:492
  63.2 6.0 %all-to-all-start.1 = ((bf16[16,128,256]{2,1,0:T(8,128)(2,1)}), bf16[16,128,256]{2,1,0:T(8,128)(2,1)S(1)}, u32[]{:S(2)}, u32[]{:S(2)}) async-start(bf16[16,128,256]{2,1,0:T(8,128)(2,1)} %bitcast.17), calls=%async_computation.1 | async-start | bytes 2097152 | tf_op jit(solution)/shard_map/all_to_all | solution.py:581
  69.1 1.6 %slice_bitcast_fusion.w_hbm = bf16[256,256]{1,0:T(8,128)(2,1)} fusion(bf16[4,256,256]{2,1,0:T(8,128)(2,1)} %w_ref.7), kind=kLoop, calls=%fused_computation.4 | loop fusion | bytes 262144 | tf_op jit(solution)/shard_map/squeeze | solution.py:565
  70.7 0.0 copy-start.5
  70.7 1.2 copy-done.5
  71.9 0.0 copy-start.7
  71.9 1.0 copy-done.7
  73.0 0.0 copy-start.8
  73.0 1.9 %copy-done.8 = bf16[2048,768]{1,0:T(8,128)(2,1)S(1)} copy-done((bf16[2048,768]{1,0:T(8,128)(2,1)S(1)}, bf16[2048,768]{1,0:T(8,128)(2,1)}, u32[]{:S(2)}) %copy-start.8) | copy-done | bytes 3145752
  74.9 0.0 copy-start.9
  74.9 1.2 copy-done.9
  76.1 0.0 copy-start.1
  76.1 0.0 copy-start.2
  76.1 3.3 %channel_grads.1 = (bf16[2048,256]{1,0:T(8,128)(2,1)}, bf16[16,4,8,256]{3,2,1,0:T(8,128)(2,1)S(1)}, bf16[16,4,8,256]{3,2,1,0:T(8,128)(2,1)S(1)}) custom-call(s32[1]{0:T(128)} %bitcast.core_ref, bf16[2048,256]{1,0:T(8,128)(2,1)S(1)} %bitcast.10, bf16[2048,256]{1,0:T(8,128)(2,1)S(1)} %bitcast.16, bf16[2048,768]{1,0:T(8,128)(2,1)S(1)} %copy-done.8, ...), custom_call_target="tpu_custom_call" | custom-call | flops 2000000000 | bytes 8388608 | tf_op jit(solution)/shard_map/channel_grads/pallas_call | solution.py:492
  79.4 0.8 collective-permute-start
  80.2 0.0 copy-done.1
  80.2 0.0 copy-done.2
  80.2 6.3 %prepare.1 = (bf16[2048,256]{1,0:T(8,128)(2,1)}, bf16[2048,128]{1,0:T(8,128)(2,1)}, bf16[256,2048]{1,0:T(8,128)(2,1)}, bf16[16,128,512]{2,1,0:T(8,128)(2,1)}, bf...) custom-call(bf16[2048,256]{1,0:T(8,128)(2,1)S(1)} %bitcast.12, ...), custom_call_target="tpu_custom_call" | custom-call | flops 3000000000 | bytes 8388608 | tf_op jit(solution)/shard_map/prepare/pallas_call | solution.py:492
  86.5 0.0 collective-permute-done
  86.5 0.1 add_convert_fusion.1
  86.6 8.0 %all-to-all-done.1.sg_ref = bf16[16,128,256]{2,1,0:T(8,128)(2,1)S(1)} async-done(((bf16[16,128,256]{2,1,0:T(8,128)(2,1)}), bf16[16,128,256]{2,1,0:T(8,128)(2,1)S(1)}, u32[]{:S(2)}, u32[]{:S(2)}) %all-to-all-start.1) | async-done | bytes 1048608 | tf_op jit(solution)/shard_map/all_to_all | solution.py:581
  94.6 9.4 %time_backward.1 = (bf16[2048,768]{1,0:T(8,128)(2,1)}, bf16[16,4,8,256]{3,2,1,0:T(8,128)(2,1)S(1)}, bf16[16,4,8,256]{3,2,1,0:T(8,128)(2,1)S(1)}) custom-call(s32[1]{0:T(128)} %bitcast.core_ref, bf16[16,128,256]{2,1,0:T(8,128)(2,1)S(1)} %all-to-all-done.1.sg_ref, bf16[256,256]{1,0:T(8,128)(2,1)} %slice_bitcast_fusion.w_hbm, ...), custom_call_target="tpu_custom_call" | custom-call | flops 4000000000 | bytes 8388608 | tf_op jit(solution)/shard_map/time_backward/pallas_call | solution.py:492
  104.1 0.0 copy-start.3
  104.1 2.7 %collective-permute-start.1 = (bf16[16,4,8,256]{3,2,1,0:T(8,128)(2,1)S(1)}, bf16[16,4,8,256]{3,2,1,0:T(8,128)(2,1)S(1)}, u32[]{:S(2)}, u32[]{:S(2)}) collective-permute-start(bf16[16,4,8,256]{3,2,1,0:T(8,128)(2,1)S(1)} %get-tuple-element.59), channel_id=1, source_target_pairs={{0,16},{16,0},{32,48},{48,32},{64,80},{80,64},{96,112},{112,96},{1... | collective-permute-start | bytes 786440 | tf_op jit(solution)/shard_map/ppermute | solution.py:587
  106.7 1.2 collective-permute-done.1
  107.9 0.1 add_convert_fusion
  108.0 0.8 pad_maximum_fusion
  108.8 4.2 %all-to-all-start.2 = ((bf16[16,8,8,256]{3,2,1,0:T(8,128)(2,1)}), bf16[16,8,8,256]{3,2,1,0:T(8,128)(2,1)S(1)}, u32[]{:S(2)}, u32[]{:S(2)}) async-start(bf16[16,8,8,256]{3,2,1,0:T(8,128)(2,1)} %pad_maximum_fusion), calls=%async_computation.2 | async-start | bytes 1048576 | tf_op jit(solution)/shard_map/all_to_all | solution.py:581
  113.0 0.0 copy-done.3
  113.0 0.0 copy-start
  113.0 1.9 %copy-done = bf16[2048,768]{1,0:T(8,128)(2,1)S(1)} copy-done((bf16[2048,768]{1,0:T(8,128)(2,1)S(1)}, bf16[2048,768]{1,0:T(8,128)(2,1)}, u32[]{:S(2)}) %copy-start) | copy-done | bytes 3145752
  114.9 3.2 %series_grad.1 = bf16[2048,256]{1,0:T(8,128)(2,1)} custom-call(bf16[2048,256]{1,0:T(8,128)(2,1)S(1)} %bitcast.13, bf16[16,128,256]{2,1,0:T(8,128)(2,1)S(1)} %all-to-all-done.1.sg_ref, bf16[2048,768]{1,0:T(8,128)(2,1)S(1)} %copy-done, bf16[4,256,256]{2,1,0:T(8,128)(2,1)S(1)} %copy-done.3), custom_call_target="tpu_custom_call" | custom-call | flops 1000000000 | bytes 8388608 | tf_op jit(solution)/shard_map/series_grad/pallas_call | solution.py:492
  118.1 8.5 %all-to-all-done.2 = bf16[16,8,8,256]{3,2,1,0:T(8,128)(2,1)S(1)} async-done(((bf16[16,8,8,256]{3,2,1,0:T(8,128)(2,1)}), bf16[16,8,8,256]{3,2,1,0:T(8,128)(2,1)S(1)}, u32[]{:S(2)}, u32[]{:S(2)}) %all-to-all-start.2) | async-done | bytes 524320 | tf_op jit(solution)/shard_map/all_to_all | solution.py:581
  126.6 0.1 reduce_sum.24
  126.7 13.8 %all_to_all.20 = bf16[8,8,8,256]{3,2,1,0:T(8,128)(2,1)S(1)} all-to-all(bf16[8,8,8,256]{3,2,1,0:T(8,128)(2,1)S(1)} %broadcast_in_dim.2), channel_id=1, replica_groups={{0,32,64,96,128,160,192,224},{16,48,80,112,144,176,208,240},{1,33,65,97..., dimensions={0} | all-to-all | bytes 524288 | tf_op jit(solution)/shard_map/all_to_all | solution.py:581
  140.5 4.3 %collective-permute-start.2 = (bf16[8,8,256]{2,1,0:T(8,128)(2,1)S(1)}, bf16[8,8,256]{2,1,0:T(8,128)(2,1)S(1)}, u32[]{:S(2)}, u32[]{:S(2)}) collective-permute-start(bf16[8,8,256]{2,1,0:T(8,128)(2,1)S(1)} %reduce_sum.25), channel_id=1, source_target_pairs={{0,16},{16,0},{32,48},{48,32},{64,80},{80,64},{96,112},{112,96},{1... | collective-permute-start | bytes 98312 | tf_op jit(solution)/shard_map/ppermute | solution.py:587
  144.9 0.9 collective-permute-done.2
  145.8 0.7 fusion
  (4 shorter events, 0.1 us)
Async XLA Ops:
  0.6 16.9 %copy-start.11 = (s32[16,3]{0,1:T(4,128)S(1)}, s32[16,3]{0,1:T(4,128)}, u32[]{:S(2)}) copy-start(s32[16,3]{0,1:T(4,128)} %param.9) | copy-start | bytes 580
  0.6 17.0 %copy-start.4 = (bf16[1,2048,1,256]{3,1,2,0:T(8,128)(2,1)S(1)}, bf16[1,2048,1,256]{3,1,2,0:T(8,128)(2,1)}, u32[]{:S(2)}) copy-start(bf16[1,2048,1,256]{3,1,2,0:T(8,128)(2,1)} %param.6) | copy-start | bytes 3145732
  0.7 17.0 %copy-start.6 = (bf16[4,256,256]{2,1,0:T(8,128)(2,1)S(1)}, bf16[4,256,256]{2,1,0:T(8,128)(2,1)}, u32[]{:S(2)}) copy-start(bf16[4,256,256]{2,1,0:T(8,128)(2,1)} %w_ref.5) | copy-start | bytes 1572868
  7.4 35.9 %all-to-all-start = ((bf16[16,128,256]{2,1,0:T(8,128)(2,1)}), bf16[16,128,256]{2,1,0:T(8,128)(2,1)S(1)}, u32[]{:S(2)}, u32[]{:S(2)}) async-start(bf16[16,128,256]{2,1,0:T(8,128)(2,1)} %time_forward.1), calls=%async_computation | async-start | bytes 2097152 | tf_op jit(solution)/shard_map/all_to_all | solution.py:581
  18.7 1.0 copy-start.10
  63.2 31.4 %all-to-all-start.1 = ((bf16[16,128,256]{2,1,0:T(8,128)(2,1)}), bf16[16,128,256]{2,1,0:T(8,128)(2,1)S(1)}, u32[]{:S(2)}, u32[]{:S(2)}) async-start(bf16[16,128,256]{2,1,0:T(8,128)(2,1)} %bitcast.17), calls=%async_computation.1 | async-start | bytes 2097152 | tf_op jit(solution)/shard_map/all_to_all | solution.py:581
  70.7 1.2 copy-start.5
  71.9 1.0 copy-start.7
  73.0 1.9 %copy-start.8 = (bf16[2048,768]{1,0:T(8,128)(2,1)S(1)}, bf16[2048,768]{1,0:T(8,128)(2,1)}, u32[]{:S(2)}) copy-start(bf16[2048,768]{1,0:T(8,128)(2,1)} %get-tuple-element.34.back_ref) | copy-start | bytes 9437188
  74.9 1.2 copy-start.9
  76.1 4.1 %copy-start.1 = (bf16[1,128,16,256]{3,2,1,0:T(8,128)(2,1)S(1)}, bf16[1,128,16,256]{3,2,1,0:T(8,128)(2,1)}, u32[]{:S(2)}) copy-start(bf16[1,128,16,256]{3,2,1,0:T(8,128)(2,1)} %param.5) | copy-start | bytes 3145732
  76.1 4.1 %copy-start.2 = (bf16[4,256,256]{2,1,0:T(8,128)(2,1)S(1)}, bf16[4,256,256]{2,1,0:T(8,128)(2,1)}, u32[]{:S(2)}) copy-start(bf16[4,256,256]{2,1,0:T(8,128)(2,1)} %w_ref.7) | copy-start | bytes 1572868
  79.4 7.1 %collective-permute-start = (bf16[16,4,8,256]{3,2,1,0:T(8,128)(2,1)S(1)}, bf16[16,4,8,256]{3,2,1,0:T(8,128)(2,1)S(1)}, u32[]{:S(2)}, u32[]{:S(2)}) collective-permute-start(bf16[16,4,8,256]{3,2,1,0:T(8,128)(2,1)S(1)} %get-tuple-element.40), channel_id=1, source_target_pairs={{0,16},{16,0},{32,48},{48,32},{64,80},{80,64},{96,112},{112,96},{1... | collective-permute-start | bytes 786440 | tf_op jit(solution)/shard_map/ppermute | solution.py:587
  104.1 8.9 %copy-start.3 = (bf16[4,256,256]{2,1,0:T(8,128)(2,1)S(1)}, bf16[4,256,256]{2,1,0:T(8,128)(2,1)}, u32[]{:S(2)}) copy-start(bf16[4,256,256]{2,1,0:T(8,128)(2,1)} %w_ref.7) | copy-start | bytes 1572868
  104.1 3.8 %collective-permute-start.1 = (bf16[16,4,8,256]{3,2,1,0:T(8,128)(2,1)S(1)}, bf16[16,4,8,256]{3,2,1,0:T(8,128)(2,1)S(1)}, u32[]{:S(2)}, u32[]{:S(2)}) collective-permute-start(bf16[16,4,8,256]{3,2,1,0:T(8,128)(2,1)S(1)} %get-tuple-element.59), channel_id=1, source_target_pairs={{0,16},{16,0},{32,48},{48,32},{64,80},{80,64},{96,112},{112,96},{1... | collective-permute-start | bytes 786440 | tf_op jit(solution)/shard_map/ppermute | solution.py:587
  108.8 17.8 %all-to-all-start.2 = ((bf16[16,8,8,256]{3,2,1,0:T(8,128)(2,1)}), bf16[16,8,8,256]{3,2,1,0:T(8,128)(2,1)S(1)}, u32[]{:S(2)}, u32[]{:S(2)}) async-start(bf16[16,8,8,256]{3,2,1,0:T(8,128)(2,1)} %pad_maximum_fusion), calls=%async_computation.2 | async-start | bytes 1048576 | tf_op jit(solution)/shard_map/all_to_all | solution.py:581
  113.0 1.9 %copy-start = (bf16[2048,768]{1,0:T(8,128)(2,1)S(1)}, bf16[2048,768]{1,0:T(8,128)(2,1)}, u32[]{:S(2)}) copy-start(bf16[2048,768]{1,0:T(8,128)(2,1)} %get-tuple-element.61.back_ref) | copy-start | bytes 9437188
  140.5 5.2 %collective-permute-start.2 = (bf16[8,8,256]{2,1,0:T(8,128)(2,1)S(1)}, bf16[8,8,256]{2,1,0:T(8,128)(2,1)S(1)}, u32[]{:S(2)}, u32[]{:S(2)}) collective-permute-start(bf16[8,8,256]{2,1,0:T(8,128)(2,1)S(1)} %reduce_sum.25), channel_id=1, source_target_pairs={{0,16},{16,0},{32,48},{48,32},{64,80},{80,64},{96,112},{112,96},{1... | collective-permute-start | bytes 98312 | tf_op jit(solution)/shard_map/ppermute | solution.py:587
